TPU v7x, 256 devices: a whole 4x4x8 slice. The times are simulated.
256 devices in a mesh: frames: 8 (over z), segments: 4 (over y), coils: 8 (over x, core).
Axes of the slice: x: 4, y: 4, z: 8, core: 2. Of those that a mesh axis runs over, the one named last changes fastest.
Arguments:
- x_in: float32 [8, 2, 2, 256, 256], P('frames', None, None, ('segments', 'coils')), may hold values from -6 to 6
- r_in: float32 [8, 2, 2, 256, 256], P('frames', None, None, ('segments', 'coils')), may hold values from -6 to 6
- p_in: float32 [8, 2, 2, 256, 256], P('frames', None, None, ('segments', 'coils')), may hold values from -6 to 6
- sens: bfloat16 [16, 2, 2, 256, 256], P('coils'), may hold values from -1 to 1
- seg_weights: bfloat16 [12, 8, 2, 16, 256], P('segments'), may hold values from 0.19921875 to 1
- seg_freq: float32 [12], replicated, may hold values from -3 to 3
- band_ids: int32 [12, 8], replicated, may hold values from 0 to 15, as said below
- seg_count: int32 [12], replicated, may hold values from 1 to 8, as said below
- k_bands: int32 [8, 16], P('frames'), may hold values from 0 to 31, as said below
Outputs:
- x_out: float32 [8, 2, 2, 256, 256], P('frames', None, None, ('segments', 'coils'))
- r_out: float32 [8, 2, 2, 256, 256], P('frames', None, None, ('segments', 'coils'))
- p_out: float32 [8, 2, 2, 256, 256], P('frames', None, None, ('segments', 'coils'))
Inputs may be any that keep to these rules, and one draw needn't show every extreme that they name: `band_ids`: the 8 entries of one segment name distinct image bands. `seg_count`: some segment uses all 8 blocks. `k_bands`: the 16 entries of one frame name distinct k-space bands.
All inputs are finite; a program needn't handle non-finite values.
Results may differ from a plain program's by a relative error of at most 0.0028.
Values may be sent and summed in bfloat16 or wider, within the bound.
No kernel may reach another device: no remote copies, remote signals or barrier semaphores. Data moves between devices by JAX's collectives and lax.ppermute only.
A program may use at most 64 MiB of HBM per device.

v0:
```python
import math

import jax
import jax.numpy as jnp
from jax import lax
from jax.experimental import pallas as pl
from jax.experimental.pallas import tpu as pltpu
from jax.sharding import PartitionSpec as P

BR = 16
KB = 8
NX = 256
NY = 256
OT = 8
NSEG = 12
KR = 128
SEGS_DEV = 3
YDEV = 4
GROUP = 32
ROWS = 8

reg_weight = 0.5
shift_weight = 0.1
epsilon = 1e-06

F32 = jnp.float32
BF16 = jnp.bfloat16
SPACE = ("segments", "coils")


def sin_cos(angle):
    half = angle * 0.5
    sq = half * half
    s = F32(1.0 / math.factorial(13))
    for n in (11, 9, 7, 5, 3, 1):
        s = s * sq + F32((-1.0) ** (n // 2) / math.factorial(n))
    s = s * half
    c = F32(1.0 / math.factorial(16))
    for n in (14, 12, 10, 8, 6, 4, 2, 0):
        c = c * sq + F32((-1.0) ** (n // 2) / math.factorial(n))
    return 2.0 * s * c, 1.0 - 2.0 * s * s


def unit_parts(products):
    n = ((products + 128) & 255) - 128
    s, c = sin_cos(n.astype(F32) * F32(2.0 * math.pi / 256))
    return c * F32(1.0 / 16.0), s * F32(-1.0 / 16.0)


def segment_of(slot):
    y = lax.axis_index("segments")
    return lax.rem(y - slot // SEGS_DEV + YDEV, YDEV) * SEGS_DEV + slot % SEGS_DEV


def tables_kernel(bands_ref, kb_ref, freq_ref, g_ref, gt_ref, gx_ref, gxt_ref, cs_ref, sn_ref):
    def spread(values, index, width):
        out = jnp.zeros_like(index)
        for j, value in enumerate(values):
            out = jnp.where(index // width == j, value * width + index % width, out)
        return out

    kbs = [kb_ref[0, j] for j in range(KR // KB)]
    ky_col = spread(kbs, lax.broadcasted_iota(jnp.int32, (KR, KR), 0), KB)
    ky_row = spread(kbs, lax.broadcasted_iota(jnp.int32, (KR, KR), 1), KB)
    rows = lax.broadcasted_iota(jnp.int32, (NX, NX), 0)
    cols = lax.broadcasted_iota(jnp.int32, (NX, NX), 1)
    gre, gim = unit_parts(rows * cols)
    gre, gim, ngim = gre.astype(BF16), gim.astype(BF16), (-gim).astype(BF16)
    gx_ref[:NX, :NX] = gre
    gx_ref[:NX, NX:] = gim
    gx_ref[NX:, :NX] = ngim
    gx_ref[NX:, NX:] = gre
    gxt_ref[:NX, :NX] = gre
    gxt_ref[:NX, NX:] = ngim
    gxt_ref[NX:, :NX] = gim
    gxt_ref[NX:, NX:] = gre
    cy = (((ky_col + 128) & 255) - 128).astype(F32) * F32(1.0 / 128.0)
    cy = jnp.concatenate([cy, cy], axis=1)
    cx_index = lax.broadcasted_iota(jnp.int32, (KR, NX), 1)
    cx = (((cx_index + 128) & 255) - 128).astype(F32) * F32(1.0 / 128.0)
    elapsed = jnp.sqrt(cy * cy + cx * cx)

    @pl.loop(0, NSEG)
    def _(slot):
        seg = segment_of(slot)
        s, c = sin_cos(freq_ref[seg] * elapsed)
        cs_ref[slot] = c
        sn_ref[slot] = s
        bands = [bands_ref[seg, j] for j in range(OT)]
        yr_row = spread(bands, lax.broadcasted_iota(jnp.int32, (KR, KR), 1), BR)
        yr_col = spread(bands, lax.broadcasted_iota(jnp.int32, (KR, KR), 0), BR)
        re, im = unit_parts(ky_col * yr_row)
        g_ref[slot, :KR, :KR] = re.astype(BF16)
        g_ref[slot, :KR, KR:] = (-im).astype(BF16)
        g_ref[slot, KR:, :KR] = im.astype(BF16)
        g_ref[slot, KR:, KR:] = re.astype(BF16)
        re, im = unit_parts(yr_col * ky_row)
        gt_ref[slot, :KR, :KR] = re.astype(BF16)
        gt_ref[slot, :KR, KR:] = im.astype(BF16)
        gt_ref[slot, KR:, :KR] = (-im).astype(BF16)
        gt_ref[slot, KR:, KR:] = re.astype(BF16)


def mm(a, b):
    return jnp.dot(a, b, preferred_element_type=F32)


def normal_kernel(
    bands_ref, count_ref, p_ref, sens_ref, w0_ref, w1_ref, w2_ref, w3_ref,
    g_ref, gt_ref, gx_ref, gxt_ref, cs_ref, sn_ref, out_ref,
    coil, blk, first, ks, acc,
):
    w_refs = (w0_ref, w1_ref, w2_ref, w3_ref)
    sre = sens_ref[0].astype(F32)
    sim = sens_ref[1].astype(F32)
    pre = p_ref[:, 0].reshape(NY, NX)
    pim = p_ref[:, 1].reshape(NY, NX)
    coil[0] = sre * pre - sim * pim
    coil[1] = sre * pim + sim * pre
    acc[...] = jnp.zeros_like(acc)
    for slot in range(NSEG):
        seg = segment_of(slot)
        count = count_ref[seg]
        for j in range(OT):
            live = (j < count).astype(F32)
            at = pl.ds(pl.multiple_of(bands_ref[seg, j] * BR, BR), BR)
            w = w_refs[slot // SEGS_DEV][slot % SEGS_DEV, j].astype(F32) * live
            blk[slot % 2, j * BR : (j + 1) * BR] = (coil[0, at] * w).astype(BF16)
            blk[slot % 2, KR + j * BR : KR + (j + 1) * BR] = (coil[1, at] * w).astype(BF16)
        got = mm(g_ref[slot], blk[slot % 2]).astype(BF16)
        first[slot * KR : (slot + 1) * KR, :NX] = got[:KR]
        first[slot * KR : (slot + 1) * KR, NX:] = got[KR:]
    for slot in range(NSEG):
        spec = mm(first[slot * KR : (slot + 1) * KR], gx_ref[...])
        re, im = spec[:, :NX], spec[:, NX:]
        c, s = cs_ref[slot], sn_ref[slot]
        if slot == 0:
            ks[:, :NX] = re * c + im * s
            ks[:, NX:] = im * c - re * s
        else:
            ks[:, :NX] += re * c + im * s
            ks[:, NX:] += im * c - re * s
    for slot in range(NSEG):
        seg = segment_of(slot)
        count = count_ref[seg]
        re, im = ks[:, :NX], ks[:, NX:]
        c, s = cs_ref[slot], sn_ref[slot]
        demod = jnp.concatenate([(re * c - im * s).astype(BF16), (im * c + re * s).astype(BF16)], axis=1)
        back = mm(demod, gxt_ref[...]).astype(BF16)
        band = mm(gt_ref[slot], jnp.concatenate([back[:, :NX], back[:, NX:]], axis=0))
        for j in range(OT):
            live = (j < count).astype(F32)
            at = pl.ds(pl.multiple_of(bands_ref[seg, j] * BR, BR), BR)
            w = w_refs[slot // SEGS_DEV][slot % SEGS_DEV, j].astype(F32) * live
            acc[0, at] += band[j * BR : (j + 1) * BR] * w
            acc[1, at] += band[KR + j * BR : KR + (j + 1) * BR] * w
    sre = sens_ref[0].astype(F32)
    sim = sens_ref[1].astype(F32)
    out_ref[:, 0] = (sre * acc[0] + sim * acc[1]).reshape(GROUP, ROWS, NX)
    out_ref[:, 1] = (sre * acc[1] - sim * acc[0]).reshape(GROUP, ROWS, NX)


def applied_kernel(parts_ref, r_ref, p_ref, low_ref, high_ref, applied_ref, sums_ref):
    totals = [jnp.zeros((ROWS, NX), F32) for _ in range(4)]
    for q in range(2):
        for c in range(2):
            total = jnp.zeros((ROWS, NX), F32)
            for half in range(2):
                for xc in range(8):
                    total = total + parts_ref[(half * 2 + q) * 8 + xc, c]
            p = p_ref[0, q, c]
            r = r_ref[0, q, c]
            smooth = 2.0 * p - low_ref[0, q, c].astype(F32) - high_ref[0, q, c].astype(F32)
            applied = total + reg_weight * smooth + shift_weight * p
            applied_ref[0, q, c] = applied
            for i, term in enumerate((r * r, p * applied, r * applied, applied * applied)):
                totals[i] = totals[i] + term
    sums_ref[...] = jnp.zeros_like(sums_ref)
    for i in range(4):
        line = jnp.sum(totals[i], axis=0, keepdims=True)
        sums_ref[i : i + 1] = line[:, :128] + line[:, 128:]


def update_kernel(sums_ref, x_ref, r_ref, p_ref, applied_ref, x_out, r_out, p_out):
    sums = jnp.sum(sums_ref[...], axis=1, keepdims=True)
    rr, pa, ra, aa = (sums[i : i + 1] for i in range(4))
    alpha = rr / (pa + epsilon)
    rnew = rr - 2.0 * alpha * ra + alpha * alpha * aa
    beta = rnew / (rr + epsilon)
    alpha = jnp.broadcast_to(alpha, (ROWS, NX))
    beta = jnp.broadcast_to(beta, (ROWS, NX))
    for q in range(2):
        for c in range(2):
            p = p_ref[0, q, c]
            r = r_ref[0, q, c] - alpha * applied_ref[0, q, c]
            x_out[0, q, c] = x_ref[0, q, c] + alpha * p
            r_out[0, q, c] = r
            p_out[0, q, c] = r + beta * p


VM = pl.BlockSpec(memory_space=pltpu.VMEM)
SM = pl.BlockSpec(memory_space=pltpu.SMEM)


def sum_all(v):
    def step(v, axes, perms):
        parts = [lax.ppermute(v, axes, perm) for perm in perms]
        return v + parts[0] + parts[1] + parts[2]

    v = step(v, "segments", [[(i, (i + k) % 4) for i in range(4)] for k in (1, 2, 3)])
    v = step(v, "coils", [[(i, (i + k) % 8) for i in range(8)] for k in (2, 4, 6)])
    v = step(v, "frames", [[(i, (i + k) % 8) for i in range(8)] for k in (2, 4, 6)])
    return step(v, ("frames", "coils"), [[(i, i ^ k) for i in range(64)] for k in (1, 8, 9)])


def local(x_in, r_in, p_in, sens, seg_weights, seg_freq, band_ids, seg_count, k_bands):
    y = lax.axis_index("segments")
    plane = lax.rem(y, 2)
    w_own = lax.dynamic_index_in_dim(seg_weights, plane, 2, keepdims=False)
    w_other = lax.dynamic_index_in_dim(seg_weights, 1 - plane, 2, keepdims=False)
    w_parts = [w_own] + [
        lax.ppermute(w_own if k == 2 else w_other, "segments", [(i, (i + k) % 4) for i in range(4)])
        for k in (1, 2, 3)
    ]
    halo = p_in.astype(BF16)
    low = lax.ppermute(halo, "frames", [(i, (i + 1) % 8) for i in range(8)])
    high = lax.ppermute(halo, "frames", [(i, (i + 7) % 8) for i in range(8)])
    send = jnp.broadcast_to(p_in[0][None, :, None], (2, 2, 8, 2, ROWS, NX)).reshape(GROUP, 2, ROWS, NX)
    whole = lax.all_to_all(send, SPACE, 0, 0, tiled=True)
    tables = pl.pallas_call(
        tables_kernel,
        in_specs=[SM, SM, SM],
        out_specs=[VM] * 6,
        out_shape=[
            jax.ShapeDtypeStruct((NSEG, 2 * KR, 2 * KR), BF16),
            jax.ShapeDtypeStruct((NSEG, 2 * KR, 2 * KR), BF16),
            jax.ShapeDtypeStruct((2 * NX, 2 * NX), BF16),
            jax.ShapeDtypeStruct((2 * NX, 2 * NX), BF16),
            jax.ShapeDtypeStruct((NSEG, KR, NX), F32),
            jax.ShapeDtypeStruct((NSEG, KR, NX), F32),
        ],
        compiler_params=pltpu.CompilerParams(vmem_limit_bytes=24 << 20),
        cost_estimate=pl.CostEstimate(flops=30_000_000, bytes_accessed=8 << 20, transcendentals=0),
        name="tables",
    )(band_ids, k_bands, seg_freq)
    sens_mine = lax.dynamic_slice(sens, (y // 2, plane, 0, 0, 0), (1, 1, 2, NY, NX)).reshape(2, NY, NX)
    parts = pl.pallas_call(
        normal_kernel,
        in_specs=[SM, SM] + [VM] * 12,
        out_specs=VM,
        out_shape=jax.ShapeDtypeStruct((GROUP, 2, ROWS, NX), F32),
        scratch_shapes=[
            pltpu.VMEM((2, NY, NX), F32),
            pltpu.VMEM((2, 2 * KR, NX), BF16),
            pltpu.VMEM((NSEG * KR, 2 * NX), BF16),
            pltpu.VMEM((KR, 2 * NX), F32),
            pltpu.VMEM((2, NY, NX), F32),
        ],
        compiler_params=pltpu.CompilerParams(vmem_limit_bytes=40 << 20),
        cost_estimate=pl.CostEstimate(flops=2_400_000_000, bytes_accessed=8 << 20, transcendentals=0),
        name="normal",
    )(band_ids, seg_count, whole, sens_mine, *w_parts, *tables)
    parts = lax.all_to_all(parts, SPACE, 0, 0, tiled=True)
    share = jax.ShapeDtypeStruct(p_in.shape, F32)
    applied, sums = pl.pallas_call(
        applied_kernel,
        in_specs=[VM] * 5,
        out_specs=[VM, VM],
        out_shape=[share, jax.ShapeDtypeStruct((8, 128), F32)],
        name="applied",
    )(parts, r_in, p_in, low, high)
    sums = sum_all(sums)
    return tuple(
        pl.pallas_call(
            update_kernel,
            in_specs=[VM] * 5,
            out_specs=[VM] * 3,
            out_shape=[share] * 3,
            name="update",
        )(sums, x_in, r_in, p_in, applied)
    )


def solution(mesh):
    image = P("frames", None, None, ("segments", "coils"), None)
    in_specs = (
        image,
        image,
        image,
        P("coils", None, None, None, None),
        P("segments", None, None, None, None),
        P(),
        P(),
        P(),
        P("frames", None),
    )
    return jax.shard_map(local, mesh=mesh, in_specs=in_specs, out_specs=(image,) * 3, check_vma=False)
```

profile of v0, /device:TPU:1, one launch (start us, length us, event | category | flops | bytes accessed | tf_op | source)
XLA Modules:
  0.0 97.4 jit_solution(5210787560945240524)
XLA Ops:
  0.7 1.7 %broadcast_in_dim.8 = f32[2,2,8,2,8,256]{5,4,3,2,1,0:T(8,128)} broadcast(f32[2,2,8,256]{3,2,1,0:T(8,128)} %bitcast.8), dimensions={1,3,4,5} | broadcast | bytes 557056 | tf_op jit(solution)/shard_map/broadcast_in_dim | solution.py:228
  2.4 8.6 %all-to-all-start = ((f32[32,2,8,256]{3,2,1,0:T(8,128)}), f32[32,2,8,256]{3,2,1,0:T(8,128)S(1)}, u32[]{:S(2)}, u32[]{:S(2)}) async-start(f32[32,2,8,256]{3,2,1,0:T(8,128)} %bitcast.1), calls=%async_computation | async-start | bytes 1048576 | tf_op jit(solution)/shard_map/all_to_all | solution.py:229
  11.8 1.4 %collective-permute-start = (bf16[3,8,16,256]{3,2,1,0:T(8,128)(2,1)}, bf16[3,8,16,256]{3,2,1,0:T(8,128)(2,1)}, u32[]{:S(2)}, u32[]{:S(2)}) collective-permute-start(bf16[3,8,16,256]{3,2,1,0:T(8,128)(2,1)} %get-tuple-element.19), channel_id=1, source_target_pairs={{0,8},{8,16},{16,24},{24,0},{1,9},{9,17},{17,25},{25,1},{2,10},{10... | collective-permute-start | bytes 589832 | tf_op jit(solution)/shard_map/ppermute | solution.py:222
  13.2 2.4 %collective-permute-start.1 = (bf16[3,8,16,256]{3,2,1,0:T(8,128)(2,1)}, bf16[3,8,16,256]{3,2,1,0:T(8,128)(2,1)}, u32[]{:S(2)}, u32[]{:S(2)}) collective-permute-start(bf16[3,8,16,256]{3,2,1,0:T(8,128)(2,1)} %get-tuple-element.20.w0_ref), channel_id=1, source_target_pairs={{0,16},{8,24},{16,0},{24,8},{1,17},{9,25},{17,1},{25,9},{2,18},{10... | collective-permute-start | bytes 589832 | tf_op jit(solution)/shard_map/ppermute | solution.py:222
  16.9 6.0 %tables.1 = (bf16[12,256,256]{2,1,0:T(8,128)(2,1)S(1)}, bf16[12,256,256]{2,1,0:T(8,128)(2,1)S(1)}, bf16[512,512]{1,0:T(8,128)(2,1)S(1)}, bf16[512,512]{1,0:T(8,1...) custom-call(s32[12,8]{1,0:T(8,128)S(1)} %copy.13.bands_ref, s32[1,16]{1,0:T(1,128)S(1)} %copy-done.12, ...), custom_call_target="tpu_custom_call" | custom-call | flops 30000000 | bytes 8388608 | tf_op jit(solution)/shard_map/tables/pallas_call | solution.py:230
  27.2 2.3 %collective-permute-done.1.w2_ref = bf16[3,8,16,256]{3,2,1,0:T(8,128)(2,1)} collective-permute-done((bf16[3,8,16,256]{3,2,1,0:T(8,128)(2,1)}, bf16[3,8,16,256]{3,2,1,0:T(8,128)(2,1)}, u32[]{:S(2)}, u32[]{:S(2)}) %collective-permute-start.1) | collective-permute-done | bytes 196640 | tf_op jit(solution)/shard_map/ppermute | solution.py:222
  29.6 1.4 %copy-done.2 = bf16[12,256,256]{2,1,0:T(8,128)(2,1)S(1)} copy-done((bf16[12,256,256]{2,1,0:T(8,128)(2,1)S(1)}, bf16[12,256,256]{2,1,0:T(8,128)(2,1)}, u32[]{:S(2)}) %copy-start.2) | copy-done | bytes 1572888
  31.0 1.4 %copy-done.4 = f32[12,128,256]{2,1,0:T(8,128)S(1)} copy-done((f32[12,128,256]{2,1,0:T(8,128)S(1)}, f32[12,128,256]{2,1,0:T(8,128)}, u32[]{:S(2)}) %copy-start.4) | copy-done | bytes 1572888
  32.4 1.4 %copy-done.6 = f32[12,128,256]{2,1,0:T(8,128)S(1)} copy-done((f32[12,128,256]{2,1,0:T(8,128)S(1)}, f32[12,128,256]{2,1,0:T(8,128)}, u32[]{:S(2)}) %copy-start.6) | copy-done | bytes 1572888
  35.9 7.3 %normal.1 = f32[32,2,8,256]{3,2,1,0:T(8,128)} custom-call(s32[12,8]{1,0:T(8,128)S(1)} %copy.13.bands_ref, s32[12]{0:T(128)S(1)} %copy-done.11, f32[32,2,8,256]{3,2,1,0:T(8,128)S(1)} %all-to-all-done.p_ref, bf16[2,256,256]{2,1,0:T(8,128)(2,1)S(1)} %dynamic-slice_bitcast_fusion.sens_ref, bf16[3,8,16,256]{3,2,1,0:T(8,128)(2,1)} %get-tuple-element.20.w0_ref, ...), custom_call_target="tpu_custom_call" | custom-call | flops 2400000000 | bytes 8388608 | tf_op jit(solution)/shard_map/normal/pallas_call | solution.py:247
  43.3 5.3 %all-to-all-start.1 = ((f32[32,2,8,256]{3,2,1,0:T(8,128)}), f32[32,2,8,256]{3,2,1,0:T(8,128)S(1)}, u32[]{:S(2)}, u32[]{:S(2)}) async-start(f32[32,2,8,256]{3,2,1,0:T(8,128)} %normal.1), calls=%async_computation.1 | async-start | bytes 1048576 | tf_op jit(solution)/shard_map/all_to_all | solution.py:263
  48.6 1.7 %collective-permute-start.3 = (bf16[1,2,2,8,256]{4,3,2,1,0:T(8,128)(2,1)S(1)}, bf16[1,2,2,8,256]{4,3,2,1,0:T(8,128)(2,1)S(1)}, u32[]{:S(2)}, u32[]{:S(2)}) collective-permute-start(bf16[1,2,2,8,256]{4,3,2,1,0:T(8,128)(2,1)S(1)} %convert_element_type.3), channel_id=1, source_target_pairs={{0,32},{32,64},{64,96},{96,128},{128,160},{160,192},{192,224},{224... | collective-permute-start | bytes 49160 | tf_op jit(solution)/shard_map/ppermute | solution.py:226
  50.3 4.0 %collective-permute-start.4 = (bf16[1,2,2,8,256]{4,3,2,1,0:T(8,128)(2,1)S(1)}, bf16[1,2,2,8,256]{4,3,2,1,0:T(8,128)(2,1)S(1)}, u32[]{:S(2)}, u32[]{:S(2)}) collective-permute-start(bf16[1,2,2,8,256]{4,3,2,1,0:T(8,128)(2,1)S(1)} %convert_element_type.3), channel_id=1, source_target_pairs={{0,224},{32,0},{64,32},{96,64},{128,96},{160,128},{192,160},{224,1... | collective-permute-start | bytes 49160 | tf_op jit(solution)/shard_map/ppermute | solution.py:227
  55.4 4.7 %all-to-all-done.1.parts_ref = f32[32,2,8,256]{3,2,1,0:T(8,128)S(1)} async-done(((f32[32,2,8,256]{3,2,1,0:T(8,128)}), f32[32,2,8,256]{3,2,1,0:T(8,128)S(1)}, u32[]{:S(2)}, u32[]{:S(2)}) %all-to-all-start.1) | async-done | bytes 524320 | tf_op jit(solution)/shard_map/all_to_all | solution.py:263
  60.9 1.7 %applied.1 = (f32[1,2,2,8,256]{4,3,2,1,0:T(8,128)}, f32[8,128]{1,0:T(8,128)}) custom-call(f32[32,2,8,256]{3,2,1,0:T(8,128)} %copy-done.14, f32[1,2,2,8,256]{4,3,2,1,0:T(8,128)} %r_ref.3, f32[1,2,2,8,256]{4,3,2,1,0:T(8,128)} %p_ref.3, bf16[1,2,2,8,256]{4,3,2,1,0:T(8,128)(2,1)} %copy-done.17, bf16[1,2,2,8,256]{4,3,2,1,0:T(8,128)(2,1)} %copy-done.18), custom_call_target="tpu_custom_call" | custom-call | tf_op jit(solution)/shard_map/applied/pallas_call | solution.py:265
  63.3 1.3 %collective-permute-start.6 = (f32[8,128]{1,0:T(8,128)}, f32[8,128]{1,0:T(8,128)S(1)}, u32[]{:S(2)}, u32[]{:S(2)}) collective-permute-start(f32[8,128]{1,0:T(8,128)} %get-tuple-element.17), channel_id=1, source_target_pairs={{0,16},{8,24},{16,0},{24,8},{1,17},{9,25},{17,1},{25,9},{2,18},{10... | collective-permute-start | bytes 12296 | tf_op jit(solution)/shard_map/ppermute | solution.py:207
  65.3 2.2 %collective-permute-done.6 = f32[8,128]{1,0:T(8,128)S(1)} collective-permute-done((f32[8,128]{1,0:T(8,128)}, f32[8,128]{1,0:T(8,128)S(1)}, u32[]{:S(2)}, u32[]{:S(2)}) %collective-permute-start.6) | collective-permute-done | bytes 4128 | tf_op jit(solution)/shard_map/ppermute | solution.py:207
  71.9 2.7 %collective-permute-done.9 = f32[8,128]{1,0:T(8,128)S(1)} collective-permute-done((f32[8,128]{1,0:T(8,128)S(1)}, f32[8,128]{1,0:T(8,128)S(1)}, u32[]{:S(2)}, u32[]{:S(2)}) %collective-permute-start.9) | collective-permute-done | bytes 4128 | tf_op jit(solution)/shard_map/ppermute | solution.py:207
  75.3 6.0 %collective-permute-start.13 = (f32[8,128]{1,0:T(8,128)S(1)}, f32[8,128]{1,0:T(8,128)S(1)}, u32[]{:S(2)}, u32[]{:S(2)}) collective-permute-start(f32[8,128]{1,0:T(8,128)S(1)} %add_add_fusion.2), channel_id=1, source_target_pairs={{0,192},{32,224},{64,0},{96,32},{128,64},{160,96},{192,128},{224,1... | collective-permute-start | bytes 12296 | tf_op jit(solution)/shard_map/ppermute | solution.py:207
  82.3 2.3 %collective-permute-start.11 = (f32[8,128]{1,0:T(8,128)S(1)}, f32[8,128]{1,0:T(8,128)S(1)}, u32[]{:S(2)}, u32[]{:S(2)}) collective-permute-start(f32[8,128]{1,0:T(8,128)S(1)} %add_add_fusion.2), channel_id=1, source_target_pairs={{0,64},{32,96},{64,128},{96,160},{128,192},{160,224},{192,0},{224,... | collective-permute-start | bytes 12296 | tf_op jit(solution)/shard_map/ppermute | solution.py:207
  84.6 3.1 %collective-permute-done.12 = f32[8,128]{1,0:T(8,128)S(1)} collective-permute-done((f32[8,128]{1,0:T(8,128)S(1)}, f32[8,128]{1,0:T(8,128)S(1)}, u32[]{:S(2)}, u32[]{:S(2)}) %collective-permute-start.12) | collective-permute-done | bytes 4128 | tf_op jit(solution)/shard_map/ppermute | solution.py:207
  87.7 4.8 %collective-permute-start.16 = (f32[8,128]{1,0:T(8,128)S(1)}, f32[8,128]{1,0:T(8,128)S(1)}, u32[]{:S(2)}, u32[]{:S(2)}) collective-permute-start(f32[8,128]{1,0:T(8,128)S(1)} %add_add_fusion.1), channel_id=1, source_target_pairs={{0,33},{1,32},{2,35},{3,34},{4,37},{5,36},{6,39},{7,38},{32,1},{33... | collective-permute-start | bytes 12296 | tf_op jit(solution)/shard_map/ppermute | solution.py:207
  93.8 1.4 %collective-permute-done.15 = f32[8,128]{1,0:T(8,128)S(1)} collective-permute-done((f32[8,128]{1,0:T(8,128)S(1)}, f32[8,128]{1,0:T(8,128)S(1)}, u32[]{:S(2)}, u32[]{:S(2)}) %collective-permute-start.15) | collective-permute-done | bytes 4128 | tf_op jit(solution)/shard_map/ppermute | solution.py:207
  95.8 1.6 %update.1 = (f32[1,2,2,8,256]{4,3,2,1,0:T(8,128)}, f32[1,2,2,8,256]{4,3,2,1,0:T(8,128)}, f32[1,2,2,8,256]{4,3,2,1,0:T(8,128)}) custom-call(f32[8,128]{1,0:T(8,128)} %add_add_fusion.sums_ref, f32[1,2,2,8,256]{4,3,2,1,0:T(8,128)} %x_ref.1, f32[1,2,2,8,256]{4,3,2,1,0:T(8,128)} %r_ref.3, f32[1,2,2,8,256]{4,3,2,1,0:T(8,128)} %p_ref.3, ...), custom_call_target="tpu_custom_call" | custom-call | tf_op jit(solution)/shard_map/update/pallas_call | solution.py:274
  (67 shorter events, 19.6 us)
Async XLA Ops:
  0.6 26.6 %copy-start = (bf16[2,2,2,256,256]{4,3,2,1,0:T(8,128)(2,1)S(1)}, bf16[2,2,2,256,256]{4,3,2,1,0:T(8,128)(2,1)}, u32[]{:S(2)}) copy-start(bf16[2,2,2,256,256]{4,3,2,1,0:T(8,128)(2,1)} %param.12) | copy-start | bytes 3145732
  0.7 16.1 %copy-start.19 = (s32[12,8]{0,1:T(8,128)S(1)}, s32[12,8]{0,1:T(8,128)}, u32[]{:S(2)}) copy-start(s32[12,8]{0,1:T(8,128)} %param.15) | copy-start | bytes 1156
  0.7 16.2 %copy-start.12 = (s32[1,16]{1,0:T(1,128)S(1)}, s32[1,16]{1,0:T(1,128)}, u32[]{:S(2)}) copy-start(s32[1,16]{1,0:T(1,128)} %kb_ref.1) | copy-start | bytes 196
  0.7 16.2 %copy-start.13 = (f32[12]{0:T(128)S(1)}, f32[12]{0:T(128)}, u32[]{:S(2)}) copy-start(f32[12]{0:T(128)} %freq_ref.1) | copy-start | bytes 148
  0.7 28.9 %copy-start.11 = (s32[12]{0:T(128)S(1)}, s32[12]{0:T(128)}, u32[]{:S(2)}) copy-start(s32[12]{0:T(128)} %count_ref.1) | copy-start | bytes 148
  2.4 27.2 %all-to-all-start = ((f32[32,2,8,256]{3,2,1,0:T(8,128)}), f32[32,2,8,256]{3,2,1,0:T(8,128)S(1)}, u32[]{:S(2)}, u32[]{:S(2)}) async-start(f32[32,2,8,256]{3,2,1,0:T(8,128)} %bitcast.1), calls=%async_computation | async-start | bytes 1048576 | tf_op jit(solution)/shard_map/all_to_all | solution.py:229
  11.8 15.4 %collective-permute-start = (bf16[3,8,16,256]{3,2,1,0:T(8,128)(2,1)}, bf16[3,8,16,256]{3,2,1,0:T(8,128)(2,1)}, u32[]{:S(2)}, u32[]{:S(2)}) collective-permute-start(bf16[3,8,16,256]{3,2,1,0:T(8,128)(2,1)} %get-tuple-element.19), channel_id=1, source_target_pairs={{0,8},{8,16},{16,24},{24,0},{1,9},{9,17},{17,25},{25,1},{2,10},{10... | collective-permute-start | bytes 589832 | tf_op jit(solution)/shard_map/ppermute | solution.py:222
  13.2 16.4 %collective-permute-start.1 = (bf16[3,8,16,256]{3,2,1,0:T(8,128)(2,1)}, bf16[3,8,16,256]{3,2,1,0:T(8,128)(2,1)}, u32[]{:S(2)}, u32[]{:S(2)}) collective-permute-start(bf16[3,8,16,256]{3,2,1,0:T(8,128)(2,1)} %get-tuple-element.20.w0_ref), channel_id=1, source_target_pairs={{0,16},{8,24},{16,0},{24,8},{1,17},{9,25},{17,1},{25,9},{2,18},{10... | collective-permute-start | bytes 589832 | tf_op jit(solution)/shard_map/ppermute | solution.py:222
  15.7 13.9 %collective-permute-start.2 = (bf16[3,8,16,256]{3,2,1,0:T(8,128)(2,1)}, bf16[3,8,16,256]{3,2,1,0:T(8,128)(2,1)}, u32[]{:S(2)}, u32[]{:S(2)}) collective-permute-start(bf16[3,8,16,256]{3,2,1,0:T(8,128)(2,1)} %get-tuple-element.19), channel_id=1, source_target_pairs={{0,24},{8,0},{16,8},{24,16},{1,25},{9,1},{17,9},{25,17},{2,26},{10... | collective-permute-start | bytes 589832 | tf_op jit(solution)/shard_map/ppermute | solution.py:222
  43.3 16.8 %all-to-all-start.1 = ((f32[32,2,8,256]{3,2,1,0:T(8,128)}), f32[32,2,8,256]{3,2,1,0:T(8,128)S(1)}, u32[]{:S(2)}, u32[]{:S(2)}) async-start(f32[32,2,8,256]{3,2,1,0:T(8,128)} %normal.1), calls=%async_computation.1 | async-start | bytes 1048576 | tf_op jit(solution)/shard_map/all_to_all | solution.py:263
  48.6 6.8 %collective-permute-start.3 = (bf16[1,2,2,8,256]{4,3,2,1,0:T(8,128)(2,1)S(1)}, bf16[1,2,2,8,256]{4,3,2,1,0:T(8,128)(2,1)S(1)}, u32[]{:S(2)}, u32[]{:S(2)}) collective-permute-start(bf16[1,2,2,8,256]{4,3,2,1,0:T(8,128)(2,1)S(1)} %convert_element_type.3), channel_id=1, source_target_pairs={{0,32},{32,64},{64,96},{96,128},{128,160},{160,192},{192,224},{224... | collective-permute-start | bytes 49160 | tf_op jit(solution)/shard_map/ppermute | solution.py:226
  50.3 5.1 %collective-permute-start.4 = (bf16[1,2,2,8,256]{4,3,2,1,0:T(8,128)(2,1)S(1)}, bf16[1,2,2,8,256]{4,3,2,1,0:T(8,128)(2,1)S(1)}, u32[]{:S(2)}, u32[]{:S(2)}) collective-permute-start(bf16[1,2,2,8,256]{4,3,2,1,0:T(8,128)(2,1)S(1)} %convert_element_type.3), channel_id=1, source_target_pairs={{0,224},{32,0},{64,32},{96,64},{128,96},{160,128},{192,160},{224,1... | collective-permute-start | bytes 49160 | tf_op jit(solution)/shard_map/ppermute | solution.py:227
  62.6 2.7 %collective-permute-start.7 = (f32[8,128]{1,0:T(8,128)}, f32[8,128]{1,0:T(8,128)S(1)}, u32[]{:S(2)}, u32[]{:S(2)}) collective-permute-start(f32[8,128]{1,0:T(8,128)} %get-tuple-element.17), channel_id=1, source_target_pairs={{0,24},{8,0},{16,8},{24,16},{1,25},{9,1},{17,9},{25,17},{2,26},{10... | collective-permute-start | bytes 12296 | tf_op jit(solution)/shard_map/ppermute | solution.py:207
  63.3 4.2 %collective-permute-start.6 = (f32[8,128]{1,0:T(8,128)}, f32[8,128]{1,0:T(8,128)S(1)}, u32[]{:S(2)}, u32[]{:S(2)}) collective-permute-start(f32[8,128]{1,0:T(8,128)} %get-tuple-element.17), channel_id=1, source_target_pairs={{0,16},{8,24},{16,0},{24,8},{1,17},{9,25},{17,1},{25,9},{2,18},{10... | collective-permute-start | bytes 12296 | tf_op jit(solution)/shard_map/ppermute | solution.py:207
  64.6 4.2 %collective-permute-start.5 = (f32[8,128]{1,0:T(8,128)}, f32[8,128]{1,0:T(8,128)S(1)}, u32[]{:S(2)}, u32[]{:S(2)}) collective-permute-start(f32[8,128]{1,0:T(8,128)} %get-tuple-element.17), channel_id=1, source_target_pairs={{0,8},{8,16},{16,24},{24,0},{1,9},{9,17},{17,25},{25,1},{2,10},{10... | collective-permute-start | bytes 12296 | tf_op jit(solution)/shard_map/ppermute | solution.py:207
  69.4 2.5 %collective-permute-start.10 = (f32[8,128]{1,0:T(8,128)S(1)}, f32[8,128]{1,0:T(8,128)S(1)}, u32[]{:S(2)}, u32[]{:S(2)}) collective-permute-start(f32[8,128]{1,0:T(8,128)S(1)} %add_add_fusion.3), channel_id=1, source_target_pairs={{0,6},{1,7},{2,0},{3,1},{4,2},{5,3},{6,4},{7,5},{8,14},{9,15},{10,... | collective-permute-start | bytes 12296 | tf_op jit(solution)/shard_map/ppermute | solution.py:207
  70.7 4.0 %collective-permute-start.9 = (f32[8,128]{1,0:T(8,128)S(1)}, f32[8,128]{1,0:T(8,128)S(1)}, u32[]{:S(2)}, u32[]{:S(2)}) collective-permute-start(f32[8,128]{1,0:T(8,128)S(1)} %add_add_fusion.3), channel_id=1, source_target_pairs={{0,4},{1,5},{2,6},{3,7},{4,0},{5,1},{6,2},{7,3},{8,12},{9,13},{10,... | collective-permute-start | bytes 12296 | tf_op jit(solution)/shard_map/ppermute | solution.py:207
  71.6 3.7 %collective-permute-start.8 = (f32[8,128]{1,0:T(8,128)S(1)}, f32[8,128]{1,0:T(8,128)S(1)}, u32[]{:S(2)}, u32[]{:S(2)}) collective-permute-start(f32[8,128]{1,0:T(8,128)S(1)} %add_add_fusion.3), channel_id=1, source_target_pairs={{0,2},{1,3},{2,4},{3,5},{4,6},{5,7},{6,0},{7,1},{8,10},{9,11},{10,... | collective-permute-start | bytes 12296 | tf_op jit(solution)/shard_map/ppermute | solution.py:207
  75.3 9.3 %collective-permute-start.13 = (f32[8,128]{1,0:T(8,128)S(1)}, f32[8,128]{1,0:T(8,128)S(1)}, u32[]{:S(2)}, u32[]{:S(2)}) collective-permute-start(f32[8,128]{1,0:T(8,128)S(1)} %add_add_fusion.2), channel_id=1, source_target_pairs={{0,192},{32,224},{64,0},{96,32},{128,64},{160,96},{192,128},{224,1... | collective-permute-start | bytes 12296 | tf_op jit(solution)/shard_map/ppermute | solution.py:207
  81.3 6.4 %collective-permute-start.12 = (f32[8,128]{1,0:T(8,128)S(1)}, f32[8,128]{1,0:T(8,128)S(1)}, u32[]{:S(2)}, u32[]{:S(2)}) collective-permute-start(f32[8,128]{1,0:T(8,128)S(1)} %add_add_fusion.2), channel_id=1, source_target_pairs={{0,128},{32,160},{64,192},{96,224},{128,0},{160,32},{192,64},{224,... | collective-permute-start | bytes 12296 | tf_op jit(solution)/shard_map/ppermute | solution.py:207
  82.3 5.4 %collective-permute-start.11 = (f32[8,128]{1,0:T(8,128)S(1)}, f32[8,128]{1,0:T(8,128)S(1)}, u32[]{:S(2)}, u32[]{:S(2)}) collective-permute-start(f32[8,128]{1,0:T(8,128)S(1)} %add_add_fusion.2), channel_id=1, source_target_pairs={{0,64},{32,96},{64,128},{96,160},{128,192},{160,224},{192,0},{224,... | collective-permute-start | bytes 12296 | tf_op jit(solution)/shard_map/ppermute | solution.py:207
  87.7 6.1 %collective-permute-start.16 = (f32[8,128]{1,0:T(8,128)S(1)}, f32[8,128]{1,0:T(8,128)S(1)}, u32[]{:S(2)}, u32[]{:S(2)}) collective-permute-start(f32[8,128]{1,0:T(8,128)S(1)} %add_add_fusion.1), channel_id=1, source_target_pairs={{0,33},{1,32},{2,35},{3,34},{4,37},{5,36},{6,39},{7,38},{32,1},{33... | collective-permute-start | bytes 12296 | tf_op jit(solution)/shard_map/ppermute | solution.py:207
  92.5 2.7 %collective-permute-start.15 = (f32[8,128]{1,0:T(8,128)S(1)}, f32[8,128]{1,0:T(8,128)S(1)}, u32[]{:S(2)}, u32[]{:S(2)}) collective-permute-start(f32[8,128]{1,0:T(8,128)S(1)} %add_add_fusion.1), channel_id=1, source_target_pairs={{0,32},{1,33},{2,34},{3,35},{4,36},{5,37},{6,38},{7,39},{32,0},{33... | collective-permute-start | bytes 12296 | tf_op jit(solution)/shard_map/ppermute | solution.py:207
  93.3 2.0 %collective-permute-start.14 = (f32[8,128]{1,0:T(8,128)S(1)}, f32[8,128]{1,0:T(8,128)S(1)}, u32[]{:S(2)}, u32[]{:S(2)}) collective-permute-start(f32[8,128]{1,0:T(8,128)S(1)} %add_add_fusion.1), channel_id=1, source_target_pairs={{0,1},{1,0},{2,3},{3,2},{4,5},{5,4},{6,7},{7,6},{32,33},{33,32},{3... | collective-permute-start | bytes 12296 | tf_op jit(solution)/shard_map/ppermute | solution.py:207
  (15 other events, 46.2 us)
where the time goes:
time: 98 us; the launch traced here: 97.4 us
  starting transfers between devices  43.7 us (45%)
  waiting for transfers between devices  21 us (21%)
  Pallas kernels  16.7 us (17%)
  local copies, waits for them, and re-layouts  14 us (14%)
  other arithmetic  1.3 us (1%)
    ppermute x12, starting transfers between devices, step(): parts = [lax.ppermute(v, axes, perm) for perm in perms]  19.1 us
    ppermute x12, waiting for transfers between devices, step(): parts = [lax.ppermute(v, axes, perm) for perm in perms]  12.8 us
    unnamed x41, local copies, waits for them, and re-layouts  11.5 us
    all_to_all x1, starting transfers between devices, local(): whole = lax.all_to_all(send, SPACE, 0, 0, tiled=True)  8.59 us
    pallas_call x1, Pallas kernels, local(): pl.pallas_call(normal_kernel, in_specs=[SM, SM] + [VM] * 12, out_specs=VM...  7.33 us
    pallas_call x1, Pallas kernels, local(): pl.pallas_call(tables_kernel, in_specs=[SM, SM, SM], out_specs=[VM] * 6,...  6.05 us
    all_to_all x1, starting transfers between devices, local(): parts = lax.all_to_all(parts, SPACE, 0, 0, tiled=True)  5.28 us
    ppermute x3, starting transfers between devices, local(): lax.ppermute(w_own if k == 2 else w_other, 'segments', [(i, (i + k) % 4)...  4.97 us
  transfers between devices with their start and end apart: 19, of which 12 were waited for; matrix products, arithmetic and copies ran while one was open for 1% of the time, Pallas kernels for 6%

commit v1 on v0

v1 whole, which is shorter than its diff:
```python
import math

import jax
import jax.numpy as jnp
from jax import lax
from jax.experimental import pallas as pl
from jax.experimental.pallas import tpu as pltpu
from jax.sharding import PartitionSpec as P

BR = 16
KB = 8
NX = 256
NY = 256
OT = 8
NSEG = 12
KR = 128
SEGS_DEV = 3
YDEV = 4
GROUP = 32
ROWS = 8
HALF = OT // 2
DEVICES = 256
CODE = 32767.0 / 6.0

reg_weight = 0.5
shift_weight = 0.1
epsilon = 1e-06

F32 = jnp.float32
BF16 = jnp.bfloat16
SPACE = ("segments", "coils")


def sin_cos(angle):
    half = angle * 0.5
    sq = half * half
    s = F32(1.0 / math.factorial(13))
    for n in (11, 9, 7, 5, 3, 1):
        s = s * sq + F32((-1.0) ** (n // 2) / math.factorial(n))
    s = s * half
    c = F32(1.0 / math.factorial(16))
    for n in (14, 12, 10, 8, 6, 4, 2, 0):
        c = c * sq + F32((-1.0) ** (n // 2) / math.factorial(n))
    return 2.0 * s * c, 1.0 - 2.0 * s * s


def unit_parts(products):
    n = ((products + 128) & 255) - 128
    s, c = sin_cos(n.astype(F32) * F32(2.0 * math.pi / 256))
    return c * F32(1.0 / 16.0), s * F32(-1.0 / 16.0)


def segment_of(slot):
    y = lax.axis_index("segments")
    return lax.rem(y - slot // SEGS_DEV + YDEV, YDEV) * SEGS_DEV + slot % SEGS_DEV


def block_of(place):
    core = lax.rem(lax.axis_index("coils"), 2)
    return lax.rem(core * HALF + place, OT)


def prep_kernel(p_ref, w_ref, send_ref, same_ref, other_ref, sem):
    plane = lax.rem(lax.axis_index("segments"), 2)
    first_block = lax.rem(lax.axis_index("coils"), 2) * HALF
    blocks = pl.ds(first_block, HALF)
    copies = [
        pltpu.make_async_copy(w_ref.at[:, blocks, plane], same_ref, sem.at[0]),
        pltpu.make_async_copy(w_ref.at[:, blocks, 1 - plane], other_ref, sem.at[1]),
    ]
    for copy in copies:
        copy.start()
    for q in range(2):
        both = jnp.concatenate([p_ref[0, q, 0], p_ref[0, q, 1]], axis=0)
        code = jnp.floor(both * F32(CODE) + 0.5).astype(jnp.int32).astype(jnp.int16)
        for pair in range(2):
            for xc in range(8):
                send_ref[(pair * 2 + q) * 8 + xc] = code
    for copy in copies:
        copy.wait()


def tables_kernel(
    bands_ref, kb_ref, freq_ref, sens_ref, w_ref,
    g_out, mine_out, own_out, gt_out, gx_out, turn_out,
    g, gt, gx, turn, ft, e, g_sem, gt_sem, turn_sem, sem,
):
    y = lax.axis_index("segments")
    plane = lax.rem(y, 2)
    copies = [
        pltpu.make_async_copy(sens_ref.at[y // 2, plane], mine_out, sem.at[0]),
        pltpu.make_async_copy(w_ref.at[:, :, plane], own_out, sem.at[1]),
        pltpu.make_async_copy(gx, gx_out, sem.at[2]),
    ]
    copies[0].start()
    copies[1].start()

    def spread(values, index, width):
        out = jnp.zeros_like(index)
        for j, value in enumerate(values):
            out = jnp.where(index // width == j, value * width + index % width, out)
        return out

    kbs = [kb_ref[0, j] for j in range(KR // KB)]
    ky_col = spread(kbs, lax.broadcasted_iota(jnp.int32, (KR, KR), 0), KB)
    ky_row = spread(kbs, lax.broadcasted_iota(jnp.int32, (8, KR), 1), KB)[:1]
    rows = lax.broadcasted_iota(jnp.int32, (NX, NX), 0)
    cols = lax.broadcasted_iota(jnp.int32, (NX, NX), 1)
    gre, gim = unit_parts(rows * cols)
    gre, gim, ngim = gre.astype(BF16), gim.astype(BF16), (-gim).astype(BF16)
    gx[0, :NX, :NX] = gre
    gx[0, :NX, NX:] = gim
    gx[0, NX:, :NX] = ngim
    gx[0, NX:, NX:] = gre
    gx[1, :NX, :NX] = gre
    gx[1, :NX, NX:] = ngim
    gx[1, NX:, :NX] = gim
    gx[1, NX:, NX:] = gre
    copies[2].start()
    re, im = unit_parts(lax.broadcasted_iota(jnp.int32, (NY, KR), 0) * ky_row)
    ft[0, :, :KR] = re.astype(BF16)
    ft[0, :, KR:] = im.astype(BF16)
    ft[1, :, :KR] = (-im).astype(BF16)
    ft[1, :, KR:] = re.astype(BF16)
    ky_wide = jnp.concatenate([ky_col, ky_col], axis=1)
    re, im = unit_parts(ky_wide * lax.broadcasted_iota(jnp.int32, (KR, NY), 1))
    e[0, :KR] = re.astype(BF16)
    e[0, KR:] = im.astype(BF16)
    e[1, :KR] = (-im).astype(BF16)
    e[1, KR:] = re.astype(BF16)
    cy = (((ky_wide + 128) & 255) - 128).astype(F32) * F32(1.0 / 128.0)
    cx_index = lax.broadcasted_iota(jnp.int32, (KR, NX), 1)
    cx = (((cx_index + 128) & 255) - 128).astype(F32) * F32(1.0 / 128.0)
    elapsed = jnp.sqrt(cy * cy + cx * cx)
    image_row = lax.broadcasted_iota(jnp.int32, (NY, KR), 0)

    def saves(slot):
        return (
            pltpu.make_async_copy(g.at[slot], g_out.at[slot], g_sem.at[slot]),
            pltpu.make_async_copy(gt.at[slot], gt_out.at[slot], gt_sem.at[slot]),
            pltpu.make_async_copy(turn.at[slot], turn_out.at[slot], turn_sem.at[slot]),
        )

    @pl.loop(0, NSEG)
    def _(slot):
        seg = segment_of(slot)
        s, c = sin_cos(freq_ref[seg] * elapsed)
        turn[slot, 0] = c
        turn[slot, 1] = s
        bands = [bands_ref[seg, block_of(t)] for t in range(OT)]
        yr_row = spread(bands, lax.broadcasted_iota(jnp.int32, (8, KR), 1), BR)[:1]
        pick = jnp.where(image_row == yr_row, F32(1), F32(0)).astype(BF16)
        g[slot, :, :KR] = mm(e[0], pick).astype(BF16)
        g[slot, :, KR:] = mm(e[1], pick).astype(BF16)
        for t in range(OT):
            at = pl.ds(pl.multiple_of(bands[t] * BR, BR), BR)
            gt[slot, t * BR : (t + 1) * BR] = ft[0, at]
            gt[slot, KR + t * BR : KR + (t + 1) * BR] = ft[1, at]
        for copy in saves(slot):
            copy.start()

    @pl.loop(0, NSEG)
    def _(slot):
        for copy in saves(slot):
            copy.wait()

    for copy in copies:
        copy.wait()


def mm(a, b):
    return jnp.dot(a, b, preferred_element_type=F32)


def normal_kernel(
    bands_ref, count_ref, p_ref, mine_in, own_in, g_in, h1_in, o1_in, h2_in, o2_in, h3_in, o3_in,
    gx_in, turn_in, gt_in, out_ref,
    coil, blk, first, ks, acc, mine, own, far, g, gx, turn, gt, sem,
):
    pieces = [(mine_in, mine), (own_in, own), (g_in.at[:SEGS_DEV], g.at[:SEGS_DEV])]
    pieces += [(g_in.at[SEGS_DEV:], g.at[SEGS_DEV:])]
    pieces += [(half, far.at[i]) for i, half in enumerate((h1_in, o1_in, h2_in, o2_in, h3_in, o3_in))]
    pieces += [(gx_in, gx), (turn_in, turn), (gt_in, gt)]
    loads = [pltpu.make_async_copy(source, target, sem.at[i]) for i, (source, target) in enumerate(pieces)]
    for load in loads:
        load.start()
    loads[0].wait()

    def weight(slot, t, seg):
        k, i = slot // SEGS_DEV, slot % SEGS_DEV
        j = block_of(t)
        live = (j < count_ref[seg]).astype(F32)
        if k == 0:
            w = own[i, j]
        else:
            w = far[2 * (k - 1) + t // HALF, i, t % HALF]
        at = pl.ds(pl.multiple_of(bands_ref[seg, j] * BR, BR), BR)
        return w.astype(F32) * live, at

    sre = mine[0].astype(F32)
    sim = mine[1].astype(F32)
    p = p_ref[...].astype(jnp.int32).astype(F32) * F32(1.0 / CODE)
    pre = p[:, :ROWS].reshape(NY, NX)
    pim = p[:, ROWS:].reshape(NY, NX)
    coil[0] = sre * pre - sim * pim
    coil[1] = sre * pim + sim * pre
    acc[...] = jnp.zeros_like(acc)
    for slot in range(NSEG):
        seg = segment_of(slot)
        if slot == 0:
            loads[1].wait()
            loads[2].wait()
        elif slot % SEGS_DEV == 0:
            k = slot // SEGS_DEV
            if k == 1:
                loads[3].wait()
            loads[2 * k + 2].wait()
            loads[2 * k + 3].wait()
        for t in range(OT):
            w, at = weight(slot, t, seg)
            blk[slot % 2, t * BR : (t + 1) * BR] = (coil[0, at] * w).astype(BF16)
            blk[slot % 2, KR + t * BR : KR + (t + 1) * BR] = (coil[1, at] * w).astype(BF16)
        got = mm(g[slot], blk[slot % 2]).astype(BF16)
        first[slot * KR : (slot + 1) * KR, :NX] = got[:KR]
        first[slot * KR : (slot + 1) * KR, NX:] = got[KR:]
    loads[10].wait()
    loads[11].wait()
    for pair in range(NSEG // 2):
        spec = mm(first[pair * 2 * KR : (pair + 1) * 2 * KR], gx[0])
        tre, tim = 0.0, 0.0
        for half in range(2):
            re, im = spec[half * KR : (half + 1) * KR, :NX], spec[half * KR : (half + 1) * KR, NX:]
            c, s = turn[pair * 2 + half, 0], turn[pair * 2 + half, 1]
            tre = tre + (re * c + im * s)
            tim = tim + (im * c - re * s)
        if pair == 0:
            ks[:, :NX] = tre
            ks[:, NX:] = tim
        else:
            ks[:, :NX] += tre
            ks[:, NX:] += tim
    loads[12].wait()
    for pair in range(NSEG // 2):
        for half in range(2):
            re, im = ks[:, :NX], ks[:, NX:]
            c, s = turn[pair * 2 + half, 0], turn[pair * 2 + half, 1]
            here = slice((pair * 2 + half) * KR, (pair * 2 + half + 1) * KR)
            first[here, :NX] = (re * c - im * s).astype(BF16)
            first[here, NX:] = (im * c + re * s).astype(BF16)
        back = mm(first[pair * 2 * KR : (pair + 1) * 2 * KR], gx[1]).astype(BF16)
        for half in range(2):
            slot = pair * 2 + half
            seg = segment_of(slot)
            mid = back[half * KR : (half + 1) * KR]
            band = mm(gt[slot], jnp.concatenate([mid[:, :NX], mid[:, NX:]], axis=0))
            for t in range(OT):
                w, at = weight(slot, t, seg)
                acc[0, at] += band[t * BR : (t + 1) * BR] * w
                acc[1, at] += band[KR + t * BR : KR + (t + 1) * BR] * w
    sre = mine[0].astype(F32)
    sim = mine[1].astype(F32)
    out_re = (sre * acc[0] + sim * acc[1]).reshape(GROUP, ROWS, NX)
    out_im = (sre * acc[1] - sim * acc[0]).reshape(GROUP, ROWS, NX)
    out_ref[...] = jnp.concatenate([out_re, out_im], axis=1).astype(BF16)


def applied_kernel(parts_ref, r_ref, p_ref, low_ref, high_ref, applied_ref, sums_ref):
    totals = [jnp.zeros((ROWS, NX), F32) for _ in range(4)]
    for q in range(2):
        total = jnp.zeros((2 * ROWS, NX), F32)
        for pair in range(2):
            for xc in range(8):
                total = total + parts_ref[(pair * 2 + q) * 8 + xc].astype(F32)
        for c in range(2):
            p = p_ref[0, q, c]
            r = r_ref[0, q, c]
            smooth = 2.0 * p - low_ref[0, q, c].astype(F32) - high_ref[0, q, c].astype(F32)
            applied = total[c * ROWS : (c + 1) * ROWS] + reg_weight * smooth + shift_weight * p
            applied_ref[0, q, c] = applied
            for i, term in enumerate((r * r, p * applied, r * applied, applied * applied)):
                totals[i] = totals[i] + term
    lane = lax.broadcasted_iota(jnp.int32, (8, 128), 1)
    line = jnp.zeros((8, 128), F32)
    for i in range(4):
        whole = jnp.sum(jnp.sum(totals[i], axis=0, keepdims=True), axis=1, keepdims=True)
        line = jnp.where(lane == i, whole, line)
    sums_ref[...] = jnp.broadcast_to(line[:1, :8], (DEVICES, 8))


def update_kernel(sums_ref, x_ref, r_ref, p_ref, applied_ref, x_out, r_out, p_out):
    sums = jnp.sum(sums_ref[...], axis=0, keepdims=True)
    rr, pa, ra, aa = (sums[:, i : i + 1] for i in range(4))
    alpha = rr / (pa + epsilon)
    rnew = rr - 2.0 * alpha * ra + alpha * alpha * aa
    beta = rnew / (rr + epsilon)
    alpha = jnp.broadcast_to(alpha, (ROWS, NX))
    beta = jnp.broadcast_to(beta, (ROWS, NX))
    for q in range(2):
        for c in range(2):
            p = p_ref[0, q, c]
            r = r_ref[0, q, c] - alpha * applied_ref[0, q, c]
            x_out[0, q, c] = x_ref[0, q, c] + alpha * p
            r_out[0, q, c] = r
            p_out[0, q, c] = r + beta * p


VM = pl.BlockSpec(memory_space=pltpu.VMEM)
SM = pl.BlockSpec(memory_space=pltpu.SMEM)
HB = pl.BlockSpec(memory_space=pltpu.HBM)


def hbm(array):
    return pltpu.with_memory_space_constraint(array, pltpu.HBM)


def local(x_in, r_in, p_in, sens, seg_weights, seg_freq, band_ids, seg_count, k_bands):
    send, same, other = pl.pallas_call(
        prep_kernel,
        in_specs=[VM, HB],
        out_specs=[VM, HB, HB],
        out_shape=[jax.ShapeDtypeStruct((GROUP, 2 * ROWS, NX), jnp.int16)] + [pltpu.HBM((SEGS_DEV, HALF, BR, NX), BF16)] * 2,
        scratch_shapes=[pltpu.SemaphoreType.DMA((2,))],
        compiler_params=pltpu.CompilerParams(vmem_limit_bytes=4 << 20),
        name="prep",
    )(p_in, hbm(seg_weights))
    halves = [
        lax.ppermute(same if k == 2 else other, "segments", [(i, (i + k) % 4) for i in range(4)])
        for k in (1, 2, 3)
    ]
    others = [lax.ppermute(half, "coils", [(i, i ^ 1) for i in range(8)]) for half in halves]
    whole = lax.all_to_all(send, SPACE, 0, 0, tiled=True)
    halo = p_in.astype(BF16)
    low = lax.ppermute(halo, "frames", [(i, (i + 1) % 8) for i in range(8)])
    high = lax.ppermute(halo, "frames", [(i, (i + 7) % 8) for i in range(8)])
    g, mine, own, gt, gx, turn = pl.pallas_call(
        tables_kernel,
        in_specs=[SM, SM, SM, HB, HB],
        out_specs=[HB] * 6,
        out_shape=[
            pltpu.HBM((NSEG, 2 * KR, 2 * KR), BF16),
            pltpu.HBM((2, NY, NX), BF16),
            pltpu.HBM((SEGS_DEV, OT, BR, NX), BF16),
            pltpu.HBM((NSEG, 2 * KR, 2 * KR), BF16),
            pltpu.HBM((2, 2 * NX, 2 * NX), BF16),
            pltpu.HBM((NSEG, 2, KR, NX), F32),
        ],
        scratch_shapes=[
            pltpu.VMEM((NSEG, 2 * KR, 2 * KR), BF16),
            pltpu.VMEM((NSEG, 2 * KR, 2 * KR), BF16),
            pltpu.VMEM((2, 2 * NX, 2 * NX), BF16),
            pltpu.VMEM((NSEG, 2, KR, NX), F32),
            pltpu.VMEM((2, NY, 2 * KR), BF16),
            pltpu.VMEM((2, 2 * KR, NY), BF16),
            pltpu.SemaphoreType.DMA((NSEG,)),
            pltpu.SemaphoreType.DMA((NSEG,)),
            pltpu.SemaphoreType.DMA((NSEG,)),
            pltpu.SemaphoreType.DMA((3,)),
        ],
        compiler_params=pltpu.CompilerParams(vmem_limit_bytes=32 << 20),
        cost_estimate=pl.CostEstimate(flops=30_000_000, bytes_accessed=8 << 20, transcendentals=0),
        name="tables",
    )(band_ids, k_bands, seg_freq, hbm(sens), hbm(seg_weights))
    parts = pl.pallas_call(
        normal_kernel,
        in_specs=[SM, SM, VM] + [HB] * 12,
        out_specs=VM,
        out_shape=jax.ShapeDtypeStruct((GROUP, 2 * ROWS, NX), BF16),
        scratch_shapes=[
            pltpu.VMEM((2, NY, NX), F32),
            pltpu.VMEM((2, 2 * KR, NX), BF16),
            pltpu.VMEM((NSEG * KR, 2 * NX), BF16),
            pltpu.VMEM((KR, 2 * NX), F32),
            pltpu.VMEM((2, NY, NX), F32),
            pltpu.VMEM((2, NY, NX), BF16),
            pltpu.VMEM((SEGS_DEV, OT, BR, NX), BF16),
            pltpu.VMEM((6, SEGS_DEV, HALF, BR, NX), BF16),
            pltpu.VMEM((NSEG, 2 * KR, 2 * KR), BF16),
            pltpu.VMEM((2, 2 * NX, 2 * NX), BF16),
            pltpu.VMEM((NSEG, 2, KR, NX), F32),
            pltpu.VMEM((NSEG, 2 * KR, 2 * KR), BF16),
            pltpu.SemaphoreType.DMA((13,)),
        ],
        compiler_params=pltpu.CompilerParams(vmem_limit_bytes=32 << 20),
        cost_estimate=pl.CostEstimate(flops=2_400_000_000, bytes_accessed=8 << 20, transcendentals=0),
        name="normal",
    )(
        band_ids, seg_count, whole, hbm(mine), hbm(own), hbm(g),
        *map(hbm, (halves[0], others[0], halves[1], others[1], halves[2], others[2])), hbm(gx), hbm(turn), hbm(gt),
    )
    parts = lax.all_to_all(parts, SPACE, 0, 0, tiled=True)
    share = jax.ShapeDtypeStruct(p_in.shape, F32)
    applied, sums = pl.pallas_call(
        applied_kernel,
        in_specs=[VM] * 5,
        out_specs=[VM, VM],
        out_shape=[share, jax.ShapeDtypeStruct((DEVICES, 8), F32)],
        compiler_params=pltpu.CompilerParams(vmem_limit_bytes=4 << 20),
        name="applied",
    )(parts, r_in, p_in, low, high)
    sums = lax.all_to_all(sums, ("frames", "segments", "coils"), 0, 0, tiled=True)
    return tuple(
        pl.pallas_call(
            update_kernel,
            in_specs=[VM] * 5,
            out_specs=[VM] * 3,
            out_shape=[share] * 3,
            compiler_params=pltpu.CompilerParams(vmem_limit_bytes=4 << 20),
            name="update",
        )(sums, x_in, r_in, p_in, applied)
    )


def solution(mesh):
    image = P("frames", None, None, ("segments", "coils"), None)
    in_specs = (
        image,
        image,
        image,
        P("coils", None, None, None, None),
        P("segments", None, None, None, None),
        P(),
        P(),
        P(),
        P("frames", None),
    )
    return jax.shard_map(local, mesh=mesh, in_specs=in_specs, out_specs=(image,) * 3, check_vma=False)
```

time: 98 us -> 96 us (0.980)
  blocking collectives: 0 us -> 24 us
  starting transfers between devices: 43.7 us -> 26.6 us
  Pallas kernels: 16.7 us -> 32.8 us
  waiting for transfers between devices: 21 us -> 7.95 us
  local copies, waits for them, and re-layouts: 14 us -> 3.5 us
  other arithmetic: 1.3 us -> 0.01 us
    all_to_all x0 -> x1, blocking collectives: none -> 24 us  [local(): lax.all_to_all(sums, ('frames', 'segments', 'coils'), 0, 0, tiled=True)]
    pallas_call x2 -> x3, Pallas kernels: 13.4 us -> 31.9 us  [the longest x1 16 us: local(): pl.pallas_call(tables_kernel, in_specs=[SM, SM, SM, HB, HB], out_specs=[H...]
    ppermute x15 -> x6, starting transfers between devices: 24.1 us -> 7.32 us  [the longest x3 5.05 us: local(): lax.ppermute(same if k == 2 else other, 'segments', [(i, (i + k) % 4) for...]
    ppermute x15 -> x6, waiting for transfers between devices: 15.2 us -> 4.81 us  [the longest x3 4.81 us: local(): lax.ppermute(same if k == 2 else other, 'segments', [(i, (i + k) % 4) for...]
    unnamed x41 -> x27, local copies, waits for them, and re-layouts: 11.5 us -> 3.5 us
    all_to_all x1, waiting for transfers between devices: 4.72 us -> 1.8 us  [local(): parts = lax.all_to_all(parts, SPACE, 0, 0, tiled=True)]
    broadcast_in_dim x1 -> x0, local copies, waits for them, and re-layouts: 1.75 us -> none  [local(): jnp.broadcast_to(p_in[0][None, :, None], (2, 2, 8, 2, ROWS, NX))]
    pallas_call x1, Pallas kernels: 1.73 us -> 0.15 us  [local(): pl.pallas_call(applied_kernel, in_specs=[VM] * 5, out_specs=[VM, VM], out...]
  transfers between devices with their start and end apart: 19 -> 10, of which waited for: 12 -> 4; matrix products, arithmetic and copies ran while one was open for 1% -> 1% of each run, Pallas kernels for 6% -> 17%
where the time goes in v1:
time: 96 us; the launch traced here: 95.6 us
  Pallas kernels  32.8 us (34%)
  starting transfers between devices  26.6 us (28%)
  blocking collectives  24 us (25%)
  waiting for transfers between devices  7.95 us (8%)
  local copies, waits for them, and re-layouts  3.5 us (4%)
    all_to_all x1, blocking collectives, local(): lax.all_to_all(sums, ('frames', 'segments', 'coils'), 0, 0, tiled=True)  24 us
    pallas_call x1, Pallas kernels, local(): pl.pallas_call(tables_kernel, in_specs=[SM, SM, SM, HB, HB], out_specs=[H...  16 us
    all_to_all x1, starting transfers between devices, local(): whole = lax.all_to_all(send, SPACE, 0, 0, tiled=True)  8.6 us
    pallas_call x1, Pallas kernels, local(): pl.pallas_call(normal_kernel, in_specs=[SM, SM, VM] + [HB] * 12, out_spec...  8.08 us
    pallas_call x1, Pallas kernels, local(): pl.pallas_call(prep_kernel, in_specs=[VM, HB], out_specs=[VM, HB, HB], ou...  7.77 us
    ppermute x3, starting transfers between devices, local(): lax.ppermute(same if k == 2 else other, 'segments', [(i, (i + k) % 4) for...  5.05 us
    all_to_all x1, starting transfers between devices, local(): parts = lax.all_to_all(parts, SPACE, 0, 0, tiled=True)  4.9 us
    ppermute x3, waiting for transfers between devices, local(): lax.ppermute(same if k == 2 else other, 'segments', [(i, (i + k) % 4) for...  4.81 us
  transfers between devices with their start and end apart: 10, of which 4 were waited for; matrix products, arithmetic and copies ran while one was open for 1% of the time, Pallas kernels for 17%

profile of v1, /device:TPU:1, one launch (start us, length us, event | category | flops | bytes accessed | tf_op | source)
XLA Modules:
  0.0 95.6 jit_solution(696998224003231784)
XLA Ops:
  0.6 0.7 copy-done
  1.4 7.8 %prep.1 = (s16[32,16,256]{2,1,0:T(8,128)(2,1)}, bf16[3,4,16,256]{3,2,1,0:T(8,128)(2,1)}, bf16[3,4,16,256]{3,2,1,0:T(8,128)(2,1)}) custom-call(f32[1,2,2,8,256]{4,3,2,1,0:T(8,128)S(1)} %copy-done, bf16[3,8,2,16,256]{4,3,2,1,0:T(8,128)(2,1)} %w_ref.3), custom_call_target="tpu_custom_call" | custom-call | tf_op jit(solution)/shard_map/prep/pallas_call | solution.py:317
  9.2 8.6 %all-to-all-start = ((s16[32,16,256]{2,1,0:T(8,128)(2,1)}), s16[32,16,256]{2,1,0:T(8,128)(2,1)S(1)}, u32[]{:S(2)}, u32[]{:S(2)}) async-start(s16[32,16,256]{2,1,0:T(8,128)(2,1)} %get-tuple-element.14), calls=%async_computation | async-start | bytes 524288 | tf_op jit(solution)/shard_map/all_to_all | solution.py:331
  17.8 1.5 %collective-permute-start = (bf16[3,4,16,256]{3,2,1,0:T(8,128)(2,1)}, bf16[3,4,16,256]{3,2,1,0:T(8,128)(2,1)S(1)}, u32[]{:S(2)}, u32[]{:S(2)}) collective-permute-start(bf16[3,4,16,256]{3,2,1,0:T(8,128)(2,1)} %get-tuple-element.18), channel_id=1, source_target_pairs={{0,8},{8,16},{16,24},{24,0},{1,9},{9,17},{17,25},{25,1},{2,10},{10... | collective-permute-start | bytes 294920 | tf_op jit(solution)/shard_map/ppermute | solution.py:327
  19.2 2.4 %collective-permute-start.2 = (bf16[3,4,16,256]{3,2,1,0:T(8,128)(2,1)}, bf16[3,4,16,256]{3,2,1,0:T(8,128)(2,1)S(1)}, u32[]{:S(2)}, u32[]{:S(2)}) collective-permute-start(bf16[3,4,16,256]{3,2,1,0:T(8,128)(2,1)} %get-tuple-element.19), channel_id=1, source_target_pairs={{0,16},{8,24},{16,0},{24,8},{1,17},{9,25},{17,1},{25,9},{2,18},{10... | collective-permute-start | bytes 294920 | tf_op jit(solution)/shard_map/ppermute | solution.py:327
  21.7 1.1 %collective-permute-start.4 = (bf16[3,4,16,256]{3,2,1,0:T(8,128)(2,1)}, bf16[3,4,16,256]{3,2,1,0:T(8,128)(2,1)S(1)}, u32[]{:S(2)}, u32[]{:S(2)}) collective-permute-start(bf16[3,4,16,256]{3,2,1,0:T(8,128)(2,1)} %get-tuple-element.18), channel_id=1, source_target_pairs={{0,24},{8,0},{16,8},{24,16},{1,25},{9,1},{17,9},{25,17},{2,26},{10... | collective-permute-start | bytes 294920 | tf_op jit(solution)/shard_map/ppermute | solution.py:327
  22.8 3.0 %collective-permute-done.h1_in = bf16[3,4,16,256]{3,2,1,0:T(8,128)(2,1)S(1)} collective-permute-done((bf16[3,4,16,256]{3,2,1,0:T(8,128)(2,1)}, bf16[3,4,16,256]{3,2,1,0:T(8,128)(2,1)S(1)}, u32[]{:S(2)}, u32[]{:S(2)}) %collective-permute-start) | collective-permute-done | bytes 98336 | tf_op jit(solution)/shard_map/ppermute | solution.py:327
  25.8 1.3 %collective-permute-start.1 = (bf16[3,4,16,256]{3,2,1,0:T(8,128)(2,1)S(1)}, bf16[3,4,16,256]{3,2,1,0:T(8,128)(2,1)S(1)}, u32[]{:S(2)}, u32[]{:S(2)}) collective-permute-start(bf16[3,4,16,256]{3,2,1,0:T(8,128)(2,1)S(1)} %collective-permute-done.h1_in), channel_id=1, source_target_pairs={{0,1},{1,0},{2,3},{3,2},{4,5},{5,4},{6,7},{7,6},{8,9},{9,8},{10,11... | collective-permute-start | bytes 294920 | tf_op jit(solution)/shard_map/ppermute | solution.py:330
  27.1 1.9 %collective-permute-done.2.h2_in = bf16[3,4,16,256]{3,2,1,0:T(8,128)(2,1)S(1)} collective-permute-done((bf16[3,4,16,256]{3,2,1,0:T(8,128)(2,1)}, bf16[3,4,16,256]{3,2,1,0:T(8,128)(2,1)S(1)}, u32[]{:S(2)}, u32[]{:S(2)}) %collective-permute-start.2) | collective-permute-done | bytes 98336 | tf_op jit(solution)/shard_map/ppermute | solution.py:327
  28.9 0.9 collective-permute-start.3
  29.9 0.8 copy.15.bands_ref
  30.7 0.7 copy-done.4
  31.3 0.7 copy-done.5
  32.0 16.0 %tables.1 = (bf16[12,256,256]{2,1,0:T(8,128)(2,1)}, bf16[2,256,256]{2,1,0:T(8,128)(2,1)}, bf16[3,8,16,256]{3,2,1,0:T(8,128)(2,1)}, bf16[12,256,256]{2,1,0:T(8,12...) custom-call(s32[12,8]{1,0:T(8,128)S(1)} %copy.15.bands_ref, s32[1,16]{1,0:T(1,128)S(1)} %copy-done.4, ...), custom_call_target="tpu_custom_call" | custom-call | flops 30000000 | bytes 8388608 | tf_op jit(solution)/shard_map/tables/pallas_call | solution.py:335
  48.1 0.5 copy-done.10
  48.8 8.1 %normal.1 = bf16[32,16,256]{2,1,0:T(8,128)(2,1)} custom-call(s32[12,8]{1,0:T(8,128)S(1)} %copy.15.bands_ref, s32[12]{0:T(128)S(1)} %copy-done.6, s16[32,16,256]{2,1,0:T(8,128)(2,1)S(1)} %all-to-all-done.p_ref, bf16[2,256,256]{2,1,0:T(8,128)(2,1)} %get-tuple-element.15.mine_in, bf16[3,8,16,256]{3,2,1,0:T(8,128)(2,1)} %get-tuple-element.16.own_in, ...), custom_call_target="tpu_custom_call" | custom-call | flops 2400000000 | bytes 8388608 | tf_op jit(solution)/shard_map/normal/pallas_call | solution.py:363
  56.9 4.9 %all-to-all-start.1 = ((bf16[32,16,256]{2,1,0:T(8,128)(2,1)}), bf16[32,16,256]{2,1,0:T(8,128)(2,1)S(1)}, u32[]{:S(2)}, u32[]{:S(2)}) async-start(bf16[32,16,256]{2,1,0:T(8,128)(2,1)} %normal.1), calls=%async_computation.1 | async-start | bytes 524288 | tf_op jit(solution)/shard_map/all_to_all | solution.py:390
  61.8 1.7 %collective-permute-start.6 = (bf16[1,2,2,8,256]{4,3,2,1,0:T(8,128)(2,1)S(1)}, bf16[1,2,2,8,256]{4,3,2,1,0:T(8,128)(2,1)S(1)}, u32[]{:S(2)}, u32[]{:S(2)}) collective-permute-start(bf16[1,2,2,8,256]{4,3,2,1,0:T(8,128)(2,1)S(1)} %convert_element_type.3), channel_id=1, source_target_pairs={{0,32},{32,64},{64,96},{96,128},{128,160},{160,192},{192,224},{224... | collective-permute-start | bytes 49160 | tf_op jit(solution)/shard_map/ppermute | solution.py:333
  63.5 4.0 %collective-permute-start.7 = (bf16[1,2,2,8,256]{4,3,2,1,0:T(8,128)(2,1)S(1)}, bf16[1,2,2,8,256]{4,3,2,1,0:T(8,128)(2,1)S(1)}, u32[]{:S(2)}, u32[]{:S(2)}) collective-permute-start(bf16[1,2,2,8,256]{4,3,2,1,0:T(8,128)(2,1)S(1)} %convert_element_type.3), channel_id=1, source_target_pairs={{0,224},{32,0},{64,32},{96,64},{128,96},{160,128},{192,160},{224,1... | collective-permute-start | bytes 49160 | tf_op jit(solution)/shard_map/ppermute | solution.py:334
  67.6 1.3 %collective-permute-done.6.low_ref = bf16[1,2,2,8,256]{4,3,2,1,0:T(8,128)(2,1)S(1)} collective-permute-done((bf16[1,2,2,8,256]{4,3,2,1,0:T(8,128)(2,1)S(1)}, bf16[1,2,2,8,256]{4,3,2,1,0:T(8,128)(2,1)S(1)}, u32[]{:S(2)}, u32[]{:S(2)}) %collective-permute-start.6) | collective-permute-done | bytes 16416 | tf_op jit(solution)/shard_map/ppermute | solution.py:333
  68.9 1.8 %all-to-all-done.1.parts_ref = bf16[32,16,256]{2,1,0:T(8,128)(2,1)S(1)} async-done(((bf16[32,16,256]{2,1,0:T(8,128)(2,1)}), bf16[32,16,256]{2,1,0:T(8,128)(2,1)S(1)}, u32[]{:S(2)}, u32[]{:S(2)}) %all-to-all-start.1) | async-done | bytes 262176 | tf_op jit(solution)/shard_map/all_to_all | solution.py:390
  70.7 0.1 applied.1
  70.8 24.0 %all_to_all.21 = f32[256,1,8]{2,1,0:T(1,128)S(1)} all-to-all(f32[256,1,8]{2,1,0:T(1,128)S(1)} %bitcast.5), channel_id=1, replica_groups=mesh['frames'=8,'segments'=4,'coils'=8] {'frames','segments','coils'}, dimensions={0} | all-to-all | bytes 16384 | tf_op jit(solution)/shard_map/all_to_all | solution.py:400
  94.8 0.8 update.1
  (30 shorter events, 0.3 us)
Async XLA Ops:
  0.6 0.8 copy-start
  1.4 47.4 %copy-start.6 = (s32[12]{0:T(128)S(1)}, s32[12]{0:T(128)}, u32[]{:S(2)}) copy-start(s32[12]{0:T(128)} %count_ref.1) | copy-start | bytes 148
  9.2 38.9 %all-to-all-start = ((s16[32,16,256]{2,1,0:T(8,128)(2,1)}), s16[32,16,256]{2,1,0:T(8,128)(2,1)S(1)}, u32[]{:S(2)}, u32[]{:S(2)}) async-start(s16[32,16,256]{2,1,0:T(8,128)(2,1)} %get-tuple-element.14), calls=%async_computation | async-start | bytes 524288 | tf_op jit(solution)/shard_map/all_to_all | solution.py:331
  17.8 8.0 %collective-permute-start = (bf16[3,4,16,256]{3,2,1,0:T(8,128)(2,1)}, bf16[3,4,16,256]{3,2,1,0:T(8,128)(2,1)S(1)}, u32[]{:S(2)}, u32[]{:S(2)}) collective-permute-start(bf16[3,4,16,256]{3,2,1,0:T(8,128)(2,1)} %get-tuple-element.18), channel_id=1, source_target_pairs={{0,8},{8,16},{16,24},{24,0},{1,9},{9,17},{17,25},{25,1},{2,10},{10... | collective-permute-start | bytes 294920 | tf_op jit(solution)/shard_map/ppermute | solution.py:327
  19.2 9.7 %collective-permute-start.2 = (bf16[3,4,16,256]{3,2,1,0:T(8,128)(2,1)}, bf16[3,4,16,256]{3,2,1,0:T(8,128)(2,1)S(1)}, u32[]{:S(2)}, u32[]{:S(2)}) collective-permute-start(bf16[3,4,16,256]{3,2,1,0:T(8,128)(2,1)} %get-tuple-element.19), channel_id=1, source_target_pairs={{0,16},{8,24},{16,0},{24,8},{1,17},{9,25},{17,1},{25,9},{2,18},{10... | collective-permute-start | bytes 294920 | tf_op jit(solution)/shard_map/ppermute | solution.py:327
  21.7 8.1 %collective-permute-start.4 = (bf16[3,4,16,256]{3,2,1,0:T(8,128)(2,1)}, bf16[3,4,16,256]{3,2,1,0:T(8,128)(2,1)S(1)}, u32[]{:S(2)}, u32[]{:S(2)}) collective-permute-start(bf16[3,4,16,256]{3,2,1,0:T(8,128)(2,1)} %get-tuple-element.18), channel_id=1, source_target_pairs={{0,24},{8,0},{16,8},{24,16},{1,25},{9,1},{17,9},{25,17},{2,26},{10... | collective-permute-start | bytes 294920 | tf_op jit(solution)/shard_map/ppermute | solution.py:327
  25.8 22.3 %copy-start.7 = (bf16[3,4,16,256]{3,2,1,0:T(8,128)(2,1)}, bf16[3,4,16,256]{3,2,1,0:T(8,128)(2,1)S(1)}, u32[]{:S(2)}) copy-start(bf16[3,4,16,256]{3,2,1,0:T(8,128)(2,1)S(1)} %collective-permute-done.h1_in) | copy-start | bytes 294916
  25.8 22.3 %collective-permute-start.1 = (bf16[3,4,16,256]{3,2,1,0:T(8,128)(2,1)S(1)}, bf16[3,4,16,256]{3,2,1,0:T(8,128)(2,1)S(1)}, u32[]{:S(2)}, u32[]{:S(2)}) collective-permute-start(bf16[3,4,16,256]{3,2,1,0:T(8,128)(2,1)S(1)} %collective-permute-done.h1_in), channel_id=1, source_target_pairs={{0,1},{1,0},{2,3},{3,2},{4,5},{5,4},{6,7},{7,6},{8,9},{9,8},{10,11... | collective-permute-start | bytes 294920 | tf_op jit(solution)/shard_map/ppermute | solution.py:330
  28.9 19.2 %copy-start.8 = (bf16[3,4,16,256]{3,2,1,0:T(8,128)(2,1)}, bf16[3,4,16,256]{3,2,1,0:T(8,128)(2,1)S(1)}, u32[]{:S(2)}) copy-start(bf16[3,4,16,256]{3,2,1,0:T(8,128)(2,1)S(1)} %collective-permute-done.2.h2_in) | copy-start | bytes 294916
  28.9 19.1 %collective-permute-start.3 = (bf16[3,4,16,256]{3,2,1,0:T(8,128)(2,1)S(1)}, bf16[3,4,16,256]{3,2,1,0:T(8,128)(2,1)S(1)}, u32[]{:S(2)}, u32[]{:S(2)}) collective-permute-start(bf16[3,4,16,256]{3,2,1,0:T(8,128)(2,1)S(1)} %collective-permute-done.2.h2_in), channel_id=1, source_target_pairs={{0,1},{1,0},{2,3},{3,2},{4,5},{5,4},{6,7},{7,6},{8,9},{9,8},{10,11... | collective-permute-start | bytes 294920 | tf_op jit(solution)/shard_map/ppermute | solution.py:330
  29.8 18.3 %copy-start.9 = (bf16[3,4,16,256]{3,2,1,0:T(8,128)(2,1)}, bf16[3,4,16,256]{3,2,1,0:T(8,128)(2,1)S(1)}, u32[]{:S(2)}) copy-start(bf16[3,4,16,256]{3,2,1,0:T(8,128)(2,1)S(1)} %collective-permute-done.4.h3_in) | copy-start | bytes 294916
  29.8 18.3 %collective-permute-start.5 = (bf16[3,4,16,256]{3,2,1,0:T(8,128)(2,1)S(1)}, bf16[3,4,16,256]{3,2,1,0:T(8,128)(2,1)S(1)}, u32[]{:S(2)}, u32[]{:S(2)}) collective-permute-start(bf16[3,4,16,256]{3,2,1,0:T(8,128)(2,1)S(1)} %collective-permute-done.4.h3_in), channel_id=1, source_target_pairs={{0,1},{1,0},{2,3},{3,2},{4,5},{5,4},{6,7},{7,6},{8,9},{9,8},{10,11... | collective-permute-start | bytes 294920 | tf_op jit(solution)/shard_map/ppermute | solution.py:330
  30.7 0.7 copy-start.4
  31.3 0.7 copy-start.5
  48.1 0.6 copy-start.10
  48.1 0.7 copy-start.11
  48.1 0.7 copy-start.12
  48.8 13.0 %copy-start.1 = (f32[1,2,2,8,256]{4,3,2,1,0:T(8,128)S(1)}, f32[1,2,2,8,256]{4,3,2,1,0:T(8,128)}, u32[]{:S(2)}) copy-start(f32[1,2,2,8,256]{4,3,2,1,0:T(8,128)} %p_ref.5) | copy-start | bytes 98308
  48.8 21.9 %copy-start.2 = (f32[1,2,2,8,256]{4,3,2,1,0:T(8,128)S(1)}, f32[1,2,2,8,256]{4,3,2,1,0:T(8,128)}, u32[]{:S(2)}) copy-start(f32[1,2,2,8,256]{4,3,2,1,0:T(8,128)} %r_ref.3) | copy-start | bytes 98308
  48.8 46.0 %copy-start.3 = (f32[1,2,2,8,256]{4,3,2,1,0:T(8,128)S(1)}, f32[1,2,2,8,256]{4,3,2,1,0:T(8,128)}, u32[]{:S(2)}) copy-start(f32[1,2,2,8,256]{4,3,2,1,0:T(8,128)} %x_ref.1) | copy-start | bytes 98308
  56.9 13.8 %all-to-all-start.1 = ((bf16[32,16,256]{2,1,0:T(8,128)(2,1)}), bf16[32,16,256]{2,1,0:T(8,128)(2,1)S(1)}, u32[]{:S(2)}, u32[]{:S(2)}) async-start(bf16[32,16,256]{2,1,0:T(8,128)(2,1)} %normal.1), calls=%async_computation.1 | async-start | bytes 524288 | tf_op jit(solution)/shard_map/all_to_all | solution.py:390
  61.8 7.1 %collective-permute-start.6 = (bf16[1,2,2,8,256]{4,3,2,1,0:T(8,128)(2,1)S(1)}, bf16[1,2,2,8,256]{4,3,2,1,0:T(8,128)(2,1)S(1)}, u32[]{:S(2)}, u32[]{:S(2)}) collective-permute-start(bf16[1,2,2,8,256]{4,3,2,1,0:T(8,128)(2,1)S(1)} %convert_element_type.3), channel_id=1, source_target_pairs={{0,32},{32,64},{64,96},{96,128},{128,160},{160,192},{192,224},{224... | collective-permute-start | bytes 49160 | tf_op jit(solution)/shard_map/ppermute | solution.py:333
  63.5 5.4 %collective-permute-start.7 = (bf16[1,2,2,8,256]{4,3,2,1,0:T(8,128)(2,1)S(1)}, bf16[1,2,2,8,256]{4,3,2,1,0:T(8,128)(2,1)S(1)}, u32[]{:S(2)}, u32[]{:S(2)}) collective-permute-start(bf16[1,2,2,8,256]{4,3,2,1,0:T(8,128)(2,1)S(1)} %convert_element_type.3), channel_id=1, source_target_pairs={{0,224},{32,0},{64,32},{96,64},{128,96},{160,128},{192,160},{224,1... | collective-permute-start | bytes 49160 | tf_op jit(solution)/shard_map/ppermute | solution.py:334

commit v2 on v1

--- a/solution.py
+++ b/solution.py
@@ -60,40 +60,26 @@
     return lax.rem(core * HALF + place, OT)
 
 
-def prep_kernel(p_ref, w_ref, send_ref, same_ref, other_ref, sem):
+def prep_kernel(p_ref, w_ref, send_ref, same_ref, other_ref):
     plane = lax.rem(lax.axis_index("segments"), 2)
-    first_block = lax.rem(lax.axis_index("coils"), 2) * HALF
-    blocks = pl.ds(first_block, HALF)
-    copies = [
-        pltpu.make_async_copy(w_ref.at[:, blocks, plane], same_ref, sem.at[0]),
-        pltpu.make_async_copy(w_ref.at[:, blocks, 1 - plane], other_ref, sem.at[1]),
-    ]
-    for copy in copies:
-        copy.start()
+    core = lax.rem(lax.axis_index("coils"), 2)
+    for i in range(SEGS_DEV):
+        for t in range(HALF):
+            same_ref[i, t] = w_ref[i, core * HALF + t, plane]
+            other_ref[i, t] = w_ref[i, core * HALF + t, 1 - plane]
     for q in range(2):
         both = jnp.concatenate([p_ref[0, q, 0], p_ref[0, q, 1]], axis=0)
         code = jnp.floor(both * F32(CODE) + 0.5).astype(jnp.int32).astype(jnp.int16)
         for pair in range(2):
             for xc in range(8):
                 send_ref[(pair * 2 + q) * 8 + xc] = code
-    for copy in copies:
-        copy.wait()
 
 
 def tables_kernel(
-    bands_ref, kb_ref, freq_ref, sens_ref, w_ref,
-    g_out, mine_out, own_out, gt_out, gx_out, turn_out,
+    bands_ref, kb_ref, freq_ref, g_out, gt_out, gx_out, turn_out,
     g, gt, gx, turn, ft, e, g_sem, gt_sem, turn_sem, sem,
 ):
-    y = lax.axis_index("segments")
-    plane = lax.rem(y, 2)
-    copies = [
-        pltpu.make_async_copy(sens_ref.at[y // 2, plane], mine_out, sem.at[0]),
-        pltpu.make_async_copy(w_ref.at[:, :, plane], own_out, sem.at[1]),
-        pltpu.make_async_copy(gx, gx_out, sem.at[2]),
-    ]
-    copies[0].start()
-    copies[1].start()
+    save_gx = pltpu.make_async_copy(gx, gx_out, sem.at[0])
 
     def spread(values, index, width):
         out = jnp.zeros_like(index)
@@ -116,7 +102,7 @@
     gx[1, :NX, NX:] = ngim
     gx[1, NX:, :NX] = gim
     gx[1, NX:, NX:] = gre
-    copies[2].start()
+    save_gx.start()
     re, im = unit_parts(lax.broadcasted_iota(jnp.int32, (NY, KR), 0) * ky_row)
     ft[0, :, :KR] = re.astype(BF16)
     ft[0, :, KR:] = im.astype(BF16)
@@ -147,7 +133,7 @@
         s, c = sin_cos(freq_ref[seg] * elapsed)
         turn[slot, 0] = c
         turn[slot, 1] = s
-        bands = [bands_ref[seg, block_of(t)] for t in range(OT)]
+        bands = [bands_ref[block_of(t), seg] for t in range(OT)]
         yr_row = spread(bands, lax.broadcasted_iota(jnp.int32, (8, KR), 1), BR)[:1]
         pick = jnp.where(image_row == yr_row, F32(1), F32(0)).astype(BF16)
         g[slot, :, :KR] = mm(e[0], pick).astype(BF16)
@@ -164,8 +150,7 @@
         for copy in saves(slot):
             copy.wait()
 
-    for copy in copies:
-        copy.wait()
+    save_gx.wait()
 
 
 def mm(a, b):
@@ -173,11 +158,13 @@
 
 
 def normal_kernel(
-    bands_ref, count_ref, p_ref, mine_in, own_in, g_in, h1_in, o1_in, h2_in, o2_in, h3_in, o3_in,
+    bands_ref, count_ref, p_ref, sens_in, w_in, g_in, h1_in, o1_in, h2_in, o2_in, h3_in, o3_in,
     gx_in, turn_in, gt_in, out_ref,
     coil, blk, first, ks, acc, mine, own, far, g, gx, turn, gt, sem,
 ):
-    pieces = [(mine_in, mine), (own_in, own), (g_in.at[:SEGS_DEV], g.at[:SEGS_DEV])]
+    y = lax.axis_index("segments")
+    plane = lax.rem(y, 2)
+    pieces = [(sens_in.at[y // 2, plane], mine), (w_in.at[:, :, plane], own), (g_in.at[:SEGS_DEV], g.at[:SEGS_DEV])]
     pieces += [(g_in.at[SEGS_DEV:], g.at[SEGS_DEV:])]
     pieces += [(half, far.at[i]) for i, half in enumerate((h1_in, o1_in, h2_in, o2_in, h3_in, o3_in))]
     pieces += [(gx_in, gx), (turn_in, turn), (gt_in, gt)]
@@ -194,7 +181,7 @@
             w = own[i, j]
         else:
             w = far[2 * (k - 1) + t // HALF, i, t % HALF]
-        at = pl.ds(pl.multiple_of(bands_ref[seg, j] * BR, BR), BR)
+        at = pl.ds(pl.multiple_of(bands_ref[j, seg] * BR, BR), BR)
         return w.astype(F32) * live, at
 
     sre = mine[0].astype(F32)
@@ -314,32 +301,30 @@
 
 
 def local(x_in, r_in, p_in, sens, seg_weights, seg_freq, band_ids, seg_count, k_bands):
+    half_shape = jax.ShapeDtypeStruct((SEGS_DEV, HALF, BR, NX), BF16)
     send, same, other = pl.pallas_call(
         prep_kernel,
-        in_specs=[VM, HB],
-        out_specs=[VM, HB, HB],
-        out_shape=[jax.ShapeDtypeStruct((GROUP, 2 * ROWS, NX), jnp.int16)] + [pltpu.HBM((SEGS_DEV, HALF, BR, NX), BF16)] * 2,
-        scratch_shapes=[pltpu.SemaphoreType.DMA((2,))],
+        in_specs=[VM, VM],
+        out_specs=[VM, VM, VM],
+        out_shape=[jax.ShapeDtypeStruct((GROUP, 2 * ROWS, NX), jnp.int16), half_shape, half_shape],
         compiler_params=pltpu.CompilerParams(vmem_limit_bytes=4 << 20),
         name="prep",
-    )(p_in, hbm(seg_weights))
+    )(hbm(p_in), hbm(seg_weights))
     halves = [
         lax.ppermute(same if k == 2 else other, "segments", [(i, (i + k) % 4) for i in range(4)])
         for k in (1, 2, 3)
     ]
-    others = [lax.ppermute(half, "coils", [(i, i ^ 1) for i in range(8)]) for half in halves]
     whole = lax.all_to_all(send, SPACE, 0, 0, tiled=True)
     halo = p_in.astype(BF16)
     low = lax.ppermute(halo, "frames", [(i, (i + 1) % 8) for i in range(8)])
     high = lax.ppermute(halo, "frames", [(i, (i + 7) % 8) for i in range(8)])
-    g, mine, own, gt, gx, turn = pl.pallas_call(
+    bands = hbm(band_ids.T)
+    g, gt, gx, turn = pl.pallas_call(
         tables_kernel,
-        in_specs=[SM, SM, SM, HB, HB],
-        out_specs=[HB] * 6,
+        in_specs=[SM, SM, SM],
+        out_specs=[HB] * 4,
         out_shape=[
             pltpu.HBM((NSEG, 2 * KR, 2 * KR), BF16),
-            pltpu.HBM((2, NY, NX), BF16),
-            pltpu.HBM((SEGS_DEV, OT, BR, NX), BF16),
             pltpu.HBM((NSEG, 2 * KR, 2 * KR), BF16),
             pltpu.HBM((2, 2 * NX, 2 * NX), BF16),
             pltpu.HBM((NSEG, 2, KR, NX), F32),
@@ -354,12 +339,14 @@
             pltpu.SemaphoreType.DMA((NSEG,)),
             pltpu.SemaphoreType.DMA((NSEG,)),
             pltpu.SemaphoreType.DMA((NSEG,)),
-            pltpu.SemaphoreType.DMA((3,)),
+            pltpu.SemaphoreType.DMA((1,)),
         ],
         compiler_params=pltpu.CompilerParams(vmem_limit_bytes=32 << 20),
         cost_estimate=pl.CostEstimate(flops=30_000_000, bytes_accessed=8 << 20, transcendentals=0),
         name="tables",
-    )(band_ids, k_bands, seg_freq, hbm(sens), hbm(seg_weights))
+    )(bands, hbm(k_bands), hbm(seg_freq))
+    halves, g = lax.optimization_barrier((halves, g))
+    others = [lax.ppermute(half, "coils", [(i, i ^ 1) for i in range(8)]) for half in halves]
     parts = pl.pallas_call(
         normal_kernel,
         in_specs=[SM, SM, VM] + [HB] * 12,
@@ -384,7 +371,7 @@
         cost_estimate=pl.CostEstimate(flops=2_400_000_000, bytes_accessed=8 << 20, transcendentals=0),
         name="normal",
     )(
-        band_ids, seg_count, whole, hbm(mine), hbm(own), hbm(g),
+        bands, hbm(seg_count), whole, hbm(sens), hbm(seg_weights), hbm(g),
         *map(hbm, (halves[0], others[0], halves[1], others[1], halves[2], others[2])), hbm(gx), hbm(turn), hbm(gt),
     )
     parts = lax.all_to_all(parts, SPACE, 0, 0, tiled=True)

time: 96 us -> 72.8 us (0.76)
  Pallas kernels: 32.8 us -> 17 us
  waiting for transfers between devices: 7.95 us -> 4.08 us
  local copies, waits for them, and re-layouts: 3.5 us -> 0.64 us
    pallas_call x2, Pallas kernels: 23.8 us -> 7.81 us  [the longest x1 6.07 us: local(): pl.pallas_call(tables_kernel, in_specs=[SM, SM, SM], out_specs=[HB] * 4,...]
    ppermute x3, waiting for transfers between devices: 4.81 us -> 0.01 us  [local(): lax.ppermute(same if k == 2 else other, 'segments', [(i, (i + k) % 4) for...]
    unnamed x27 -> x18, local copies, waits for them, and re-layouts: 3.5 us -> 0.64 us
  transfers between devices with their start and end apart: 10 -> 10, of which waited for: 4 -> 5; matrix products, arithmetic and copies ran while one was open for 1% -> 0% of each run, Pallas kernels for 17% -> 8%
where the time goes in v2:
time: 72.8 us; the launch traced here: 72.5 us
  starting transfers between devices  26 us (36%)
  blocking collectives  24 us (33%)
  Pallas kernels  17 us (23%)
  waiting for transfers between devices  4.08 us (6%)
  between operations  0.76 us (1%)
    all_to_all x1, blocking collectives, local(): lax.all_to_all(sums, ('frames', 'segments', 'coils'), 0, 0, tiled=True)  24 us
    all_to_all x1, starting transfers between devices, local(): whole = lax.all_to_all(send, SPACE, 0, 0, tiled=True)  8.59 us
    pallas_call x1, Pallas kernels, local(): pl.pallas_call(normal_kernel, in_specs=[SM, SM, VM] + [HB] * 12, out_spec...  8.25 us
    pallas_call x1, Pallas kernels, local(): pl.pallas_call(tables_kernel, in_specs=[SM, SM, SM], out_specs=[HB] * 4,...  6.07 us
    ppermute x3, starting transfers between devices, local(): lax.ppermute(same if k == 2 else other, 'segments', [(i, (i + k) % 4) for...  5.05 us
    all_to_all x1, starting transfers between devices, local(): parts = lax.all_to_all(parts, SPACE, 0, 0, tiled=True)  4.83 us
    ppermute x1, starting transfers between devices, local(): high = lax.ppermute(halo, 'frames', [(i, (i + 7) % 8) for i in range(8)])  4.03 us
    ppermute x3, starting transfers between devices, local(): lax.ppermute(half, 'coils', [(i, i ^ 1) for i in range(8)])  1.8 us
  transfers between devices with their start and end apart: 10, of which 5 were waited for; matrix products, arithmetic and copies ran while one was open for 0% of the time, Pallas kernels for 8%

profile of v2, /device:TPU:1, one launch (start us, length us, event | category | flops | bytes accessed | tf_op | source)
XLA Modules:
  0.0 72.5 jit_solution(3111188892906373671)
XLA Ops:
  0.6 1.7 %prep.1 = (s16[32,16,256]{2,1,0:T(8,128)(2,1)}, bf16[3,4,16,256]{3,2,1,0:T(8,128)(2,1)S(1)}, bf16[3,4,16,256]{3,2,1,0:T(8,128)(2,1)S(1)}) custom-call(f32[1,2,2,8,256]{4,3,2,1,0:T(8,128)} %p_ref.5, bf16[3,8,2,16,256]{4,3,2,1,0:T(8,128)(2,1)} %w_in.1), custom_call_target="tpu_custom_call" | custom-call | tf_op jit(solution)/shard_map/prep/pallas_call | solution.py:305
  2.4 8.6 %all-to-all-start = ((s16[32,16,256]{2,1,0:T(8,128)(2,1)}), s16[32,16,256]{2,1,0:T(8,128)(2,1)S(1)}, u32[]{:S(2)}, u32[]{:S(2)}) async-start(s16[32,16,256]{2,1,0:T(8,128)(2,1)} %get-tuple-element.16), calls=%async_computation | async-start | bytes 524288 | tf_op jit(solution)/shard_map/all_to_all | solution.py:317
  11.0 1.5 %collective-permute-start = (bf16[3,4,16,256]{3,2,1,0:T(8,128)(2,1)S(1)}, bf16[3,4,16,256]{3,2,1,0:T(8,128)(2,1)S(1)}, u32[]{:S(2)}, u32[]{:S(2)}) collective-permute-start(bf16[3,4,16,256]{3,2,1,0:T(8,128)(2,1)S(1)} %get-tuple-element.17), channel_id=1, source_target_pairs={{0,8},{8,16},{16,24},{24,0},{1,9},{9,17},{17,25},{25,1},{2,10},{10... | collective-permute-start | bytes 294920 | tf_op jit(solution)/shard_map/ppermute | solution.py:314
  12.4 2.4 %collective-permute-start.1 = (bf16[3,4,16,256]{3,2,1,0:T(8,128)(2,1)S(1)}, bf16[3,4,16,256]{3,2,1,0:T(8,128)(2,1)S(1)}, u32[]{:S(2)}, u32[]{:S(2)}) collective-permute-start(bf16[3,4,16,256]{3,2,1,0:T(8,128)(2,1)S(1)} %get-tuple-element.18), channel_id=1, source_target_pairs={{0,16},{8,24},{16,0},{24,8},{1,17},{9,25},{17,1},{25,9},{2,18},{10... | collective-permute-start | bytes 294920 | tf_op jit(solution)/shard_map/ppermute | solution.py:314
  14.9 1.1 %collective-permute-start.2 = (bf16[3,4,16,256]{3,2,1,0:T(8,128)(2,1)S(1)}, bf16[3,4,16,256]{3,2,1,0:T(8,128)(2,1)S(1)}, u32[]{:S(2)}, u32[]{:S(2)}) collective-permute-start(bf16[3,4,16,256]{3,2,1,0:T(8,128)(2,1)S(1)} %get-tuple-element.17), channel_id=1, source_target_pairs={{0,24},{8,0},{16,8},{24,16},{1,25},{9,1},{17,9},{25,17},{2,26},{10... | collective-permute-start | bytes 294920 | tf_op jit(solution)/shard_map/ppermute | solution.py:314
  16.0 6.1 %tables.1 = (bf16[12,256,256]{2,1,0:T(8,128)(2,1)}, bf16[12,256,256]{2,1,0:T(8,128)(2,1)}, bf16[2,512,512]{2,1,0:T(8,128)(2,1)}, f32[12,2,128,256]{3,2,1,0:T(8,128)}) custom-call(s32[8,12]{1,0:T(8,128)} %bitcast.7, s32[1,16]{1,0:T(1,128)} %kb_ref.1, f32[12]{0:T(128)} %freq_ref.1), custom_call_target="tpu_custom_call" | custom-call | flops 30000000 | bytes 8388608 | tf_op jit(solution)/shard_map/tables/pallas_call | solution.py:322
  22.2 1.3 %collective-permute-start.3 = (bf16[3,4,16,256]{3,2,1,0:T(8,128)(2,1)S(1)}, bf16[3,4,16,256]{3,2,1,0:T(8,128)(2,1)S(1)}, u32[]{:S(2)}, u32[]{:S(2)}) collective-permute-start(bf16[3,4,16,256]{3,2,1,0:T(8,128)(2,1)S(1)} %collective-permute-done.h1_in), channel_id=1, source_target_pairs={{0,1},{1,0},{2,3},{3,2},{4,5},{5,4},{6,7},{7,6},{8,9},{9,8},{10,11... | collective-permute-start | bytes 294920 | tf_op jit(solution)/shard_map/ppermute | solution.py:349
  23.4 0.1 collective-permute-start.4
  23.5 0.4 collective-permute-start.5
  24.0 0.4 collective-permute-done.3.o1_in
  24.4 0.4 collective-permute-done.4.o2_in
  24.7 0.2 collective-permute-done.5.o3_in
  24.9 0.1 copy-done.6
  25.0 0.4 copy-done.7
  25.4 0.1 copy-done.8
  25.5 8.3 %normal.1 = bf16[32,16,256]{2,1,0:T(8,128)(2,1)} custom-call(s32[8,12]{1,0:T(8,128)} %bitcast.8, s32[12]{0:T(128)} %count_ref.1, s16[32,16,256]{2,1,0:T(8,128)(2,1)S(1)} %all-to-all-done.p_ref, bf16[2,2,2,256,256]{4,3,2,1,0:T(8,128)(2,1)} %sens_in.1, bf16[3,8,2,16,256]{4,3,2,1,0:T(8,128)(2,1)} %w_in.1, bf16[12,256,256]{2,1,0:T(8,128)(2,1)} %get-tuple-element.20.g_in, ...), custom_call_target="tpu_custom_call" | custom-call | flops 2400000000 | bytes 8388608 | tf_op jit(solution)/shard_map/normal/pallas_call | solution.py:350
  33.8 4.8 %all-to-all-start.1 = ((bf16[32,16,256]{2,1,0:T(8,128)(2,1)}), bf16[32,16,256]{2,1,0:T(8,128)(2,1)S(1)}, u32[]{:S(2)}, u32[]{:S(2)}) async-start(bf16[32,16,256]{2,1,0:T(8,128)(2,1)} %normal.1), calls=%async_computation.1 | async-start | bytes 524288 | tf_op jit(solution)/shard_map/all_to_all | solution.py:377
  38.7 1.7 %collective-permute-start.6 = (bf16[1,2,2,8,256]{4,3,2,1,0:T(8,128)(2,1)S(1)}, bf16[1,2,2,8,256]{4,3,2,1,0:T(8,128)(2,1)S(1)}, u32[]{:S(2)}, u32[]{:S(2)}) collective-permute-start(bf16[1,2,2,8,256]{4,3,2,1,0:T(8,128)(2,1)S(1)} %convert_element_type.3), channel_id=1, source_target_pairs={{0,32},{32,64},{64,96},{96,128},{128,160},{160,192},{192,224},{224... | collective-permute-start | bytes 49160 | tf_op jit(solution)/shard_map/ppermute | solution.py:319
  40.4 4.0 %collective-permute-start.7 = (bf16[1,2,2,8,256]{4,3,2,1,0:T(8,128)(2,1)S(1)}, bf16[1,2,2,8,256]{4,3,2,1,0:T(8,128)(2,1)S(1)}, u32[]{:S(2)}, u32[]{:S(2)}) collective-permute-start(bf16[1,2,2,8,256]{4,3,2,1,0:T(8,128)(2,1)S(1)} %convert_element_type.3), channel_id=1, source_target_pairs={{0,224},{32,0},{64,32},{96,64},{128,96},{160,128},{192,160},{224,1... | collective-permute-start | bytes 49160 | tf_op jit(solution)/shard_map/ppermute | solution.py:320
  44.4 1.3 %collective-permute-done.6.low_ref = bf16[1,2,2,8,256]{4,3,2,1,0:T(8,128)(2,1)S(1)} collective-permute-done((bf16[1,2,2,8,256]{4,3,2,1,0:T(8,128)(2,1)S(1)}, bf16[1,2,2,8,256]{4,3,2,1,0:T(8,128)(2,1)S(1)}, u32[]{:S(2)}, u32[]{:S(2)}) %collective-permute-start.6) | collective-permute-done | bytes 16416 | tf_op jit(solution)/shard_map/ppermute | solution.py:319
  45.7 1.8 %all-to-all-done.1.parts_ref = bf16[32,16,256]{2,1,0:T(8,128)(2,1)S(1)} async-done(((bf16[32,16,256]{2,1,0:T(8,128)(2,1)}), bf16[32,16,256]{2,1,0:T(8,128)(2,1)S(1)}, u32[]{:S(2)}, u32[]{:S(2)}) %all-to-all-start.1) | async-done | bytes 262176 | tf_op jit(solution)/shard_map/all_to_all | solution.py:377
  47.5 0.1 applied.1
  47.7 24.0 %all_to_all.21 = f32[256,1,8]{2,1,0:T(1,128)S(1)} all-to-all(f32[256,1,8]{2,1,0:T(1,128)S(1)} %bitcast.6), channel_id=1, replica_groups=mesh['frames'=8,'segments'=4,'coils'=8] {'frames','segments','coils'}, dimensions={0} | all-to-all | bytes 16384 | tf_op jit(solution)/shard_map/all_to_all | solution.py:387
  71.7 0.8 %update.1 = (f32[1,2,2,8,256]{4,3,2,1,0:T(8,128)}, f32[1,2,2,8,256]{4,3,2,1,0:T(8,128)}, f32[1,2,2,8,256]{4,3,2,1,0:T(8,128)}) custom-call(f32[256,8]{1,0:T(8,128)S(1)} %bitcast.5, f32[1,2,2,8,256]{4,3,2,1,0:T(8,128)S(1)} %copy-done.2, f32[1,2,2,8,256]{4,3,2,1,0:T(8,128)S(1)} %copy-done.1, f32[1,2,2,8,256]{4,3,2,1,0:T(8,128)S(1)} %copy-done, ...), custom_call_target="tpu_custom_call" | custom-call | tf_op jit(solution)/shard_map/update/pallas_call | solution.py:389
  (21 shorter events, 0.0 us)
Async XLA Ops:
  2.4 22.5 %all-to-all-start = ((s16[32,16,256]{2,1,0:T(8,128)(2,1)}), s16[32,16,256]{2,1,0:T(8,128)(2,1)S(1)}, u32[]{:S(2)}, u32[]{:S(2)}) async-start(s16[32,16,256]{2,1,0:T(8,128)(2,1)} %get-tuple-element.16), calls=%async_computation | async-start | bytes 524288 | tf_op jit(solution)/shard_map/all_to_all | solution.py:317
  11.0 11.1 %collective-permute-start = (bf16[3,4,16,256]{3,2,1,0:T(8,128)(2,1)S(1)}, bf16[3,4,16,256]{3,2,1,0:T(8,128)(2,1)S(1)}, u32[]{:S(2)}, u32[]{:S(2)}) collective-permute-start(bf16[3,4,16,256]{3,2,1,0:T(8,128)(2,1)S(1)} %get-tuple-element.17), channel_id=1, source_target_pairs={{0,8},{8,16},{16,24},{24,0},{1,9},{9,17},{17,25},{25,1},{2,10},{10... | collective-permute-start | bytes 294920 | tf_op jit(solution)/shard_map/ppermute | solution.py:314
  12.4 9.7 %collective-permute-start.1 = (bf16[3,4,16,256]{3,2,1,0:T(8,128)(2,1)S(1)}, bf16[3,4,16,256]{3,2,1,0:T(8,128)(2,1)S(1)}, u32[]{:S(2)}, u32[]{:S(2)}) collective-permute-start(bf16[3,4,16,256]{3,2,1,0:T(8,128)(2,1)S(1)} %get-tuple-element.18), channel_id=1, source_target_pairs={{0,16},{8,24},{16,0},{24,8},{1,17},{9,25},{17,1},{25,9},{2,18},{10... | collective-permute-start | bytes 294920 | tf_op jit(solution)/shard_map/ppermute | solution.py:314
  14.9 7.3 %collective-permute-start.2 = (bf16[3,4,16,256]{3,2,1,0:T(8,128)(2,1)S(1)}, bf16[3,4,16,256]{3,2,1,0:T(8,128)(2,1)S(1)}, u32[]{:S(2)}, u32[]{:S(2)}) collective-permute-start(bf16[3,4,16,256]{3,2,1,0:T(8,128)(2,1)S(1)} %get-tuple-element.17), channel_id=1, source_target_pairs={{0,24},{8,0},{16,8},{24,16},{1,25},{9,1},{17,9},{25,17},{2,26},{10... | collective-permute-start | bytes 294920 | tf_op jit(solution)/shard_map/ppermute | solution.py:314
  22.1 2.8 %copy-start.3 = (bf16[3,4,16,256]{3,2,1,0:T(8,128)(2,1)}, bf16[3,4,16,256]{3,2,1,0:T(8,128)(2,1)S(1)}, u32[]{:S(2)}) copy-start(bf16[3,4,16,256]{3,2,1,0:T(8,128)(2,1)S(1)} %collective-permute-done.h1_in) | copy-start | bytes 294916
  22.1 2.8 %copy-start.4 = (bf16[3,4,16,256]{3,2,1,0:T(8,128)(2,1)}, bf16[3,4,16,256]{3,2,1,0:T(8,128)(2,1)S(1)}, u32[]{:S(2)}) copy-start(bf16[3,4,16,256]{3,2,1,0:T(8,128)(2,1)S(1)} %collective-permute-done.1.h2_in) | copy-start | bytes 294916
  22.1 2.8 %copy-start.5 = (bf16[3,4,16,256]{3,2,1,0:T(8,128)(2,1)}, bf16[3,4,16,256]{3,2,1,0:T(8,128)(2,1)S(1)}, u32[]{:S(2)}) copy-start(bf16[3,4,16,256]{3,2,1,0:T(8,128)(2,1)S(1)} %collective-permute-done.2.h3_in) | copy-start | bytes 294916
  22.2 2.2 %collective-permute-start.3 = (bf16[3,4,16,256]{3,2,1,0:T(8,128)(2,1)S(1)}, bf16[3,4,16,256]{3,2,1,0:T(8,128)(2,1)S(1)}, u32[]{:S(2)}, u32[]{:S(2)}) collective-permute-start(bf16[3,4,16,256]{3,2,1,0:T(8,128)(2,1)S(1)} %collective-permute-done.h1_in), channel_id=1, source_target_pairs={{0,1},{1,0},{2,3},{3,2},{4,5},{5,4},{6,7},{7,6},{8,9},{9,8},{10,11... | collective-permute-start | bytes 294920 | tf_op jit(solution)/shard_map/ppermute | solution.py:349
  23.4 1.3 %collective-permute-start.4 = (bf16[3,4,16,256]{3,2,1,0:T(8,128)(2,1)S(1)}, bf16[3,4,16,256]{3,2,1,0:T(8,128)(2,1)S(1)}, u32[]{:S(2)}, u32[]{:S(2)}) collective-permute-start(bf16[3,4,16,256]{3,2,1,0:T(8,128)(2,1)S(1)} %collective-permute-done.1.h2_in), channel_id=1, source_target_pairs={{0,1},{1,0},{2,3},{3,2},{4,5},{5,4},{6,7},{7,6},{8,9},{9,8},{10,11... | collective-permute-start | bytes 294920 | tf_op jit(solution)/shard_map/ppermute | solution.py:349
  23.5 1.4 %collective-permute-start.5 = (bf16[3,4,16,256]{3,2,1,0:T(8,128)(2,1)S(1)}, bf16[3,4,16,256]{3,2,1,0:T(8,128)(2,1)S(1)}, u32[]{:S(2)}, u32[]{:S(2)}) collective-permute-start(bf16[3,4,16,256]{3,2,1,0:T(8,128)(2,1)S(1)} %collective-permute-done.2.h3_in), channel_id=1, source_target_pairs={{0,1},{1,0},{2,3},{3,2},{4,5},{5,4},{6,7},{7,6},{8,9},{9,8},{10,11... | collective-permute-start | bytes 294920 | tf_op jit(solution)/shard_map/ppermute | solution.py:349
  24.4 0.6 copy-start.6
  24.7 0.7 copy-start.7
  24.9 0.6 copy-start.8
  25.5 13.1 %copy-start = (f32[1,2,2,8,256]{4,3,2,1,0:T(8,128)S(1)}, f32[1,2,2,8,256]{4,3,2,1,0:T(8,128)}, u32[]{:S(2)}) copy-start(f32[1,2,2,8,256]{4,3,2,1,0:T(8,128)} %p_ref.5) | copy-start | bytes 98308
  25.5 22.0 %copy-start.1 = (f32[1,2,2,8,256]{4,3,2,1,0:T(8,128)S(1)}, f32[1,2,2,8,256]{4,3,2,1,0:T(8,128)}, u32[]{:S(2)}) copy-start(f32[1,2,2,8,256]{4,3,2,1,0:T(8,128)} %r_ref.3) | copy-start | bytes 98308
  25.5 46.1 %copy-start.2 = (f32[1,2,2,8,256]{4,3,2,1,0:T(8,128)S(1)}, f32[1,2,2,8,256]{4,3,2,1,0:T(8,128)}, u32[]{:S(2)}) copy-start(f32[1,2,2,8,256]{4,3,2,1,0:T(8,128)} %x_ref.1) | copy-start | bytes 98308
  33.8 13.7 %all-to-all-start.1 = ((bf16[32,16,256]{2,1,0:T(8,128)(2,1)}), bf16[32,16,256]{2,1,0:T(8,128)(2,1)S(1)}, u32[]{:S(2)}, u32[]{:S(2)}) async-start(bf16[32,16,256]{2,1,0:T(8,128)(2,1)} %normal.1), calls=%async_computation.1 | async-start | bytes 524288 | tf_op jit(solution)/shard_map/all_to_all | solution.py:377
  38.7 7.1 %collective-permute-start.6 = (bf16[1,2,2,8,256]{4,3,2,1,0:T(8,128)(2,1)S(1)}, bf16[1,2,2,8,256]{4,3,2,1,0:T(8,128)(2,1)S(1)}, u32[]{:S(2)}, u32[]{:S(2)}) collective-permute-start(bf16[1,2,2,8,256]{4,3,2,1,0:T(8,128)(2,1)S(1)} %convert_element_type.3), channel_id=1, source_target_pairs={{0,32},{32,64},{64,96},{96,128},{128,160},{160,192},{192,224},{224... | collective-permute-start | bytes 49160 | tf_op jit(solution)/shard_map/ppermute | solution.py:319
  40.4 5.4 %collective-permute-start.7 = (bf16[1,2,2,8,256]{4,3,2,1,0:T(8,128)(2,1)S(1)}, bf16[1,2,2,8,256]{4,3,2,1,0:T(8,128)(2,1)S(1)}, u32[]{:S(2)}, u32[]{:S(2)}) collective-permute-start(bf16[1,2,2,8,256]{4,3,2,1,0:T(8,128)(2,1)S(1)} %convert_element_type.3), channel_id=1, source_target_pairs={{0,224},{32,0},{64,32},{96,64},{128,96},{160,128},{192,160},{224,1... | collective-permute-start | bytes 49160 | tf_op jit(solution)/shard_map/ppermute | solution.py:320

commit v3 on v2

v3 whole, which is shorter than its diff:
```python
import math

import jax
import jax.numpy as jnp
from jax import lax
from jax.experimental import pallas as pl
from jax.experimental.pallas import tpu as pltpu
from jax.sharding import PartitionSpec as P

BR = 16
KB = 8
NX = 256
NY = 256
OT = 8
NSEG = 12
KR = 128
SEGS_DEV = 3
YDEV = 4
GROUP = 32
ROWS = 8
HALF = OT // 2
DEVICES = 256
CODE = 32767.0 / 6.0

reg_weight = 0.5
shift_weight = 0.1
epsilon = 1e-06

F32 = jnp.float32
BF16 = jnp.bfloat16
SPACE = ("segments", "coils")


def sin_cos(angle):
    half = angle * 0.5
    sq = half * half
    s = F32(1.0 / math.factorial(13))
    for n in (11, 9, 7, 5, 3, 1):
        s = s * sq + F32((-1.0) ** (n // 2) / math.factorial(n))
    s = s * half
    c = F32(1.0 / math.factorial(16))
    for n in (14, 12, 10, 8, 6, 4, 2, 0):
        c = c * sq + F32((-1.0) ** (n // 2) / math.factorial(n))
    return 2.0 * s * c, 1.0 - 2.0 * s * s


def unit_parts(products):
    n = ((products + 128) & 255) - 128
    s, c = sin_cos(n.astype(F32) * F32(2.0 * math.pi / 256))
    return c * F32(1.0 / 16.0), s * F32(-1.0 / 16.0)


def segment_of(slot):
    y = lax.axis_index("segments")
    return lax.rem(y - slot // SEGS_DEV + YDEV, YDEV) * SEGS_DEV + slot % SEGS_DEV


def block_of(place):
    core = lax.rem(lax.axis_index("coils"), 2)
    return lax.rem(core * HALF + place, OT)


def spread(values, index, width):
    out = jnp.zeros_like(index)
    for j, value in enumerate(values):
        out = jnp.where(index // width == j, value * width + index % width, out)
    return out


def prep_kernel(p_ref, w_ref, send_ref, same_ref, other_ref):
    plane = lax.rem(lax.axis_index("segments"), 2)
    core = lax.rem(lax.axis_index("coils"), 2)
    for i in range(SEGS_DEV):
        for t in range(HALF):
            same_ref[i, t] = w_ref[i, core * HALF + t, plane]
            other_ref[i, t] = w_ref[i, core * HALF + t, 1 - plane]
    for q in range(2):
        both = jnp.concatenate([p_ref[0, q, 0], p_ref[0, q, 1]], axis=0)
        code = jnp.floor(both * F32(CODE) + 0.5).astype(jnp.int32).astype(jnp.int16)
        for pair in range(2):
            for xc in range(8):
                send_ref[(pair * 2 + q) * 8 + xc] = code


def turns_kernel(kb_ref, freq_ref, h1, h2, h3, turn_out, turn, turn_sem):
    kbs = [kb_ref[0, j] for j in range(KR // KB)]
    ky = spread(kbs, lax.broadcasted_iota(jnp.int32, (KR, KR), 0), KB)
    cy = (((ky + 128) & 255) - 128).astype(F32) * F32(1.0 / 128.0)
    cy = jnp.concatenate([cy, cy], axis=1)
    cx_index = lax.broadcasted_iota(jnp.int32, (KR, NX), 1)
    cx = (((cx_index + 128) & 255) - 128).astype(F32) * F32(1.0 / 128.0)
    elapsed = jnp.sqrt(cy * cy + cx * cx)
    saves = [pltpu.make_async_copy(turn.at[slot], turn_out.at[slot], turn_sem.at[slot]) for slot in range(NSEG)]
    for slot in range(NSEG):
        turn[slot, 1], turn[slot, 0] = sin_cos(freq_ref[segment_of(slot)] * elapsed)
        saves[slot].start()
    for save in saves:
        save.wait()


def tables_kernel(bands_ref, kb_ref, g_ref, ft, gx_ref, e):
    kbs = [kb_ref[0, j] for j in range(KR // KB)]
    ky_col = spread(kbs, lax.broadcasted_iota(jnp.int32, (KR, KR), 0), KB)
    ky_row = spread(kbs, lax.broadcasted_iota(jnp.int32, (8, KR), 1), KB)[:1]
    ky_wide = jnp.concatenate([ky_col, ky_col], axis=1)
    rows = lax.broadcasted_iota(jnp.int32, (NX, NX), 0)
    cols = lax.broadcasted_iota(jnp.int32, (NX, NX), 1)
    re, im = unit_parts(rows * cols)
    gx_ref[0] = re.astype(BF16)
    gx_ref[1] = im.astype(BF16)
    re, im = unit_parts(lax.broadcasted_iota(jnp.int32, (NY, KR), 0) * ky_row)
    ft[0, :, :KR] = re.astype(BF16)
    ft[0, :, KR:] = im.astype(BF16)
    ft[1, :, :KR] = (-im).astype(BF16)
    ft[1, :, KR:] = re.astype(BF16)
    re, im = unit_parts(ky_wide * lax.broadcasted_iota(jnp.int32, (KR, NY), 1))
    e[0, :KR] = re.astype(BF16)
    e[0, KR:] = im.astype(BF16)
    e[1, :KR] = (-im).astype(BF16)
    e[1, KR:] = re.astype(BF16)
    image_row = lax.broadcasted_iota(jnp.int32, (NY, KR), 0)
    for slot in range(NSEG):
        seg = segment_of(slot)
        bands = [bands_ref[block_of(t), seg] for t in range(OT)]
        yr_row = spread(bands, lax.broadcasted_iota(jnp.int32, (8, KR), 1), BR)[:1]
        pick = jnp.where(image_row == yr_row, F32(1), F32(0)).astype(BF16)
        g_ref[slot, :, :KR] = mm(e[0], pick).astype(BF16)
        g_ref[slot, :, KR:] = mm(e[1], pick).astype(BF16)


def mm(a, b):
    return jnp.dot(a, b, preferred_element_type=F32)


def normal_kernel(
    bands_ref, count_ref, p_ref, g, ft, gx_ref, h1, o1, h2, o2, h3, o3, sens_in, w_in, turn_in, out_ref,
    coil, blk, first, ks, acc, mine, near, gx, turn, sem,
):
    y = lax.axis_index("segments")
    plane = lax.rem(y, 2)
    core = lax.rem(lax.axis_index("coils"), 2)
    loads = [
        pltpu.make_async_copy(source, target, sem.at[i])
        for i, (source, target) in enumerate(
            [
                (sens_in.at[y // 2, plane], mine),
                (w_in.at[:, pl.ds(core * HALF, HALF), plane], near.at[0]),
                (w_in.at[:, pl.ds((1 - core) * HALF, HALF), plane], near.at[1]),
                (turn_in, turn),
            ]
        )
    ]
    for load in loads:
        load.start()
    halves = ((near.at[0], near.at[1]), (h1, o1), (h2, o2), (h3, o3))
    gre, gim = gx_ref[0], gx_ref[1]
    for i, sign in enumerate((1, -1)):
        gx[i, :NX, :NX] = gre
        gx[i, :NX, NX:] = sign * gim
        gx[i, NX:, :NX] = -sign * gim
        gx[i, NX:, NX:] = gre

    def weight(slot, t):
        seg = segment_of(slot)
        j = block_of(t)
        live = (j < count_ref[seg]).astype(F32)
        w = halves[slot // SEGS_DEV][t // HALF][slot % SEGS_DEV, t % HALF]
        at = pl.ds(pl.multiple_of(bands_ref[j, seg] * BR, BR), BR)
        return w.astype(F32) * live, at

    loads[0].wait()
    for chunk in range(4):
        rows = slice(chunk * 64, chunk * 64 + 64)
        p = p_ref[chunk * 8 : chunk * 8 + 8].astype(jnp.int32).astype(F32) * F32(1.0 / CODE)
        pre = p[:, :ROWS].reshape(64, NX)
        pim = p[:, ROWS:].reshape(64, NX)
        sre = mine[0, rows].astype(F32)
        sim = mine[1, rows].astype(F32)
        coil[0, rows] = sre * pre - sim * pim
        coil[1, rows] = sre * pim + sim * pre
    acc[...] = jnp.zeros_like(acc)
    loads[1].wait()
    loads[2].wait()
    for slot in range(NSEG):
        for t in range(OT):
            w, at = weight(slot, t)
            blk[slot, t * BR : (t + 1) * BR] = (coil[0, at] * w).astype(BF16)
            blk[slot, KR + t * BR : KR + (t + 1) * BR] = (coil[1, at] * w).astype(BF16)
        got = mm(g[slot], blk[slot]).astype(BF16)
        first[slot * KR : (slot + 1) * KR, :NX] = got[:KR]
        first[slot * KR : (slot + 1) * KR, NX:] = got[KR:]
    loads[3].wait()
    for pair in range(NSEG // 2):
        spec = mm(first[pair * 2 * KR : (pair + 1) * 2 * KR], gx[0])
        tre, tim = 0.0, 0.0
        for half in range(2):
            re, im = spec[half * KR : (half + 1) * KR, :NX], spec[half * KR : (half + 1) * KR, NX:]
            c, s = turn[pair * 2 + half, 0], turn[pair * 2 + half, 1]
            tre = tre + (re * c + im * s)
            tim = tim + (im * c - re * s)
        ks[0] = tre if pair == 0 else ks[0] + tre
        ks[1] = tim if pair == 0 else ks[1] + tim
    for pair in range(NSEG // 2):
        for half in range(2):
            re, im = ks[0], ks[1]
            c, s = turn[pair * 2 + half, 0], turn[pair * 2 + half, 1]
            here = slice((pair * 2 + half) * KR, (pair * 2 + half + 1) * KR)
            first[here, :NX] = (re * c - im * s).astype(BF16)
            first[here, NX:] = (im * c + re * s).astype(BF16)
        back = mm(first[pair * 2 * KR : (pair + 1) * 2 * KR], gx[1]).astype(BF16)
        for half in range(2):
            slot = pair * 2 + half
            places = [weight(slot, t) for t in range(OT)]
            rows = jnp.concatenate([ft[c, at] for c in range(2) for _, at in places], axis=0)
            mid = back[half * KR : (half + 1) * KR]
            band = mm(rows, jnp.concatenate([mid[:, :NX], mid[:, NX:]], axis=0))
            for t, (w, at) in enumerate(places):
                acc[0, at] += band[t * BR : (t + 1) * BR] * w
                acc[1, at] += band[KR + t * BR : KR + (t + 1) * BR] * w
    for chunk in range(4):
        rows = slice(chunk * 64, chunk * 64 + 64)
        sre = mine[0, rows].astype(F32)
        sim = mine[1, rows].astype(F32)
        are, aim = acc[0, rows], acc[1, rows]
        out_re = (sre * are + sim * aim).reshape(8, ROWS, NX)
        out_im = (sre * aim - sim * are).reshape(8, ROWS, NX)
        out_ref[chunk * 8 : chunk * 8 + 8] = jnp.concatenate([out_re, out_im], axis=1).astype(BF16)


def applied_kernel(parts_ref, r_ref, p_ref, low_ref, high_ref, applied_ref, sums_ref):
    totals = [jnp.zeros((ROWS, NX), F32) for _ in range(4)]
    for q in range(2):
        total = jnp.zeros((2 * ROWS, NX), F32)
        for pair in range(2):
            for xc in range(8):
                total = total + parts_ref[(pair * 2 + q) * 8 + xc].astype(F32)
        for c in range(2):
            p = p_ref[0, q, c]
            r = r_ref[0, q, c]
            smooth = 2.0 * p - low_ref[0, q, c].astype(F32) - high_ref[0, q, c].astype(F32)
            applied = total[c * ROWS : (c + 1) * ROWS] + reg_weight * smooth + shift_weight * p
            applied_ref[0, q, c] = applied
            for i, term in enumerate((r * r, p * applied, r * applied, applied * applied)):
                totals[i] = totals[i] + term
    lane = lax.broadcasted_iota(jnp.int32, (8, 128), 1)
    line = jnp.zeros((8, 128), F32)
    for i in range(4):
        whole = jnp.sum(jnp.sum(totals[i], axis=0, keepdims=True), axis=1, keepdims=True)
        line = jnp.where(lane == i, whole, line)
    sums_ref[...] = jnp.broadcast_to(line[:1, :8], (DEVICES, 8))


def update_kernel(sums_ref, x_ref, r_ref, p_ref, applied_ref, x_out, r_out, p_out):
    sums = jnp.sum(sums_ref[...], axis=0, keepdims=True)
    rr, pa, ra, aa = (sums[:, i : i + 1] for i in range(4))
    alpha = rr / (pa + epsilon)
    rnew = rr - 2.0 * alpha * ra + alpha * alpha * aa
    beta = rnew / (rr + epsilon)
    alpha = jnp.broadcast_to(alpha, (ROWS, NX))
    beta = jnp.broadcast_to(beta, (ROWS, NX))
    for q in range(2):
        for c in range(2):
            p = p_ref[0, q, c]
            r = r_ref[0, q, c] - alpha * applied_ref[0, q, c]
            x_out[0, q, c] = x_ref[0, q, c] + alpha * p
            r_out[0, q, c] = r
            p_out[0, q, c] = r + beta * p


VM = pl.BlockSpec(memory_space=pltpu.VMEM)
SM = pl.BlockSpec(memory_space=pltpu.SMEM)
HB = pl.BlockSpec(memory_space=pltpu.HBM)


def hbm(array):
    return pltpu.with_memory_space_constraint(array, pltpu.HBM)


def local(x_in, r_in, p_in, sens, seg_weights, seg_freq, band_ids, seg_count, k_bands):
    half_shape = jax.ShapeDtypeStruct((SEGS_DEV, HALF, BR, NX), BF16)
    send, same, other = pl.pallas_call(
        prep_kernel,
        in_specs=[VM, VM],
        out_specs=[VM, VM, VM],
        out_shape=[jax.ShapeDtypeStruct((GROUP, 2 * ROWS, NX), jnp.int16), half_shape, half_shape],
        compiler_params=pltpu.CompilerParams(vmem_limit_bytes=4 << 20),
        name="prep",
    )(hbm(p_in), hbm(seg_weights))
    halves = [
        lax.ppermute(same if k == 2 else other, "segments", [(i, (i + k) % 4) for i in range(4)])
        for k in (1, 2, 3)
    ]
    whole = lax.all_to_all(send, SPACE, 0, 0, tiled=True)
    halo = p_in.astype(BF16)
    low = lax.ppermute(halo, "frames", [(i, (i + 1) % 8) for i in range(8)])
    high = lax.ppermute(halo, "frames", [(i, (i + 7) % 8) for i in range(8)])
    bands = hbm(band_ids.T)
    g, ft, gx = pl.pallas_call(
        tables_kernel,
        in_specs=[SM, SM],
        out_specs=[VM, VM, VM],
        out_shape=[
            jax.ShapeDtypeStruct((NSEG, 2 * KR, 2 * KR), BF16),
            jax.ShapeDtypeStruct((2, NY, 2 * KR), BF16),
            jax.ShapeDtypeStruct((2, NX, NX), BF16),
        ],
        scratch_shapes=[pltpu.VMEM((2, 2 * KR, NY), BF16)],
        compiler_params=pltpu.CompilerParams(vmem_limit_bytes=32 << 20),
        cost_estimate=pl.CostEstimate(flops=1_000_000_000, bytes_accessed=2 << 20, transcendentals=0),
        name="tables",
    )(bands, hbm(k_bands))
    turn = pl.pallas_call(
        turns_kernel,
        in_specs=[SM, SM] + [pl.BlockSpec(memory_space=pl.ANY)] * 3,
        out_specs=HB,
        out_shape=pltpu.HBM((NSEG, 2, KR, NX), F32),
        scratch_shapes=[pltpu.VMEM((NSEG, 2, KR, NX), F32), pltpu.SemaphoreType.DMA((NSEG,))],
        compiler_params=pltpu.CompilerParams(vmem_limit_bytes=32 << 20),
        cost_estimate=pl.CostEstimate(flops=40_000_000_000, bytes_accessed=3 << 20, transcendentals=0),
        name="turns",
    )(hbm(k_bands), hbm(seg_freq), *halves)
    others = [lax.ppermute(half, "coils", [(i, i ^ 1) for i in range(8)]) for half in halves]
    parts = pl.pallas_call(
        normal_kernel,
        in_specs=[SM] * 2 + [VM] * 10 + [HB] * 3,
        out_specs=VM,
        out_shape=jax.ShapeDtypeStruct((GROUP, 2 * ROWS, NX), BF16),
        scratch_shapes=[
            pltpu.VMEM((2, NY, NX), F32),
            pltpu.VMEM((NSEG, 2 * KR, NX), BF16),
            pltpu.VMEM((NSEG * KR, 2 * NX), BF16),
            pltpu.VMEM((2, KR, NX), F32),
            pltpu.VMEM((2, NY, NX), F32),
            pltpu.VMEM((2, NY, NX), BF16),
            pltpu.VMEM((2, SEGS_DEV, HALF, BR, NX), BF16),
            pltpu.VMEM((2, 2 * NX, 2 * NX), BF16),
            pltpu.VMEM((NSEG, 2, KR, NX), F32),
            pltpu.SemaphoreType.DMA((4,)),
        ],
        compiler_params=pltpu.CompilerParams(vmem_limit_bytes=32 << 20),
        cost_estimate=pl.CostEstimate(flops=2_400_000_000, bytes_accessed=8 << 20, transcendentals=0),
        name="normal",
    )(
        bands, hbm(seg_count), whole, g, ft, gx,
        halves[0], others[0], halves[1], others[1], halves[2], others[2], hbm(sens), hbm(seg_weights), hbm(turn),
    )
    parts = lax.all_to_all(parts, SPACE, 0, 0, tiled=True)
    share = jax.ShapeDtypeStruct(p_in.shape, F32)
    applied, sums = pl.pallas_call(
        applied_kernel,
        in_specs=[VM] * 5,
        out_specs=[VM, VM],
        out_shape=[share, jax.ShapeDtypeStruct((DEVICES, 8), F32)],
        compiler_params=pltpu.CompilerParams(vmem_limit_bytes=4 << 20),
        name="applied",
    )(parts, r_in, p_in, low, high)
    sums = lax.all_to_all(sums, ("frames", "segments", "coils"), 0, 0, tiled=True)
    return tuple(
        pl.pallas_call(
            update_kernel,
            in_specs=[VM] * 5,
            out_specs=[VM] * 3,
            out_shape=[share] * 3,
            compiler_params=pltpu.CompilerParams(vmem_limit_bytes=4 << 20),
            name="update",
        )(sums, x_in, r_in, p_in, applied)
    )


def solution(mesh):
    image = P("frames", None, None, ("segments", "coils"), None)
    in_specs = (
        image,
        image,
        image,
        P("coils", None, None, None, None),
        P("segments", None, None, None, None),
        P(),
        P(),
        P(),
        P("frames", None),
    )
    return jax.shard_map(local, mesh=mesh, in_specs=in_specs, out_specs=(image,) * 3, check_vma=False)
```

time: 72.8 us -> 70 us (0.962)
  starting transfers between devices: 26 us -> 24 us
  Pallas kernels: 17 us -> 15.8 us
  waiting for transfers between devices: 4.08 us -> 5.13 us
    all_to_all x1, starting transfers between devices: 8.59 us -> 6.08 us  [local(): whole = lax.all_to_all(send, SPACE, 0, 0, tiled=True)]
    all_to_all x1, waiting for transfers between devices: 0.01 us -> 2 us  [local(): whole = lax.all_to_all(send, SPACE, 0, 0, tiled=True)]
    pallas_call x2 -> x3, Pallas kernels: 14.3 us -> 13.1 us  [the longest x1 7.1 us: local(): pl.pallas_call(normal_kernel, in_specs=[SM] * 2 + [VM] * 10 + [HB] * 3, o...]
    ppermute x3, waiting for transfers between devices: 0.94 us -> 0.01 us  [local(): lax.ppermute(half, 'coils', [(i, i ^ 1) for i in range(8)])]
    ppermute x3, starting transfers between devices: 1.8 us -> 0.87 us  [local(): lax.ppermute(half, 'coils', [(i, i ^ 1) for i in range(8)])]
    ppermute x3, starting transfers between devices: 5.05 us -> 5.81 us  [local(): lax.ppermute(same if k == 2 else other, 'segments', [(i, (i + k) % 4) for...]
  transfers between devices with their start and end apart: 10 -> 10, of which waited for: 5 -> 3; matrix products, arithmetic and copies ran while one was open for 0% -> 0% of each run, Pallas kernels for 8% -> 9%
where the time goes in v3:
time: 70 us; the launch traced here: 69.6 us
  starting transfers between devices  24 us (34%)
  blocking collectives  24 us (34%)
  Pallas kernels  15.8 us (23%)
  waiting for transfers between devices  5.13 us (7%)
  between operations  0.73 us (1%)
    all_to_all x1, blocking collectives, local(): lax.all_to_all(sums, ('frames', 'segments', 'coils'), 0, 0, tiled=True)  24 us
    pallas_call x1, Pallas kernels, local(): pl.pallas_call(normal_kernel, in_specs=[SM] * 2 + [VM] * 10 + [HB] * 3, o...  7.1 us
    all_to_all x1, starting transfers between devices, local(): whole = lax.all_to_all(send, SPACE, 0, 0, tiled=True)  6.08 us
    ppermute x3, starting transfers between devices, local(): lax.ppermute(same if k == 2 else other, 'segments', [(i, (i + k) % 4) for...  5.81 us
    all_to_all x1, starting transfers between devices, local(): parts = lax.all_to_all(parts, SPACE, 0, 0, tiled=True)  5.42 us
    ppermute x1, starting transfers between devices, local(): high = lax.ppermute(halo, 'frames', [(i, (i + 7) % 8) for i in range(8)])  4.01 us
    pallas_call x1, Pallas kernels, local(): pl.pallas_call(turns_kernel, in_specs=[SM, SM] + [pl.BlockSpec(memory_spa...  3.45 us
    pallas_call x1, Pallas kernels, local(): pl.pallas_call(tables_kernel, in_specs=[SM, SM], out_specs=[VM, VM, VM],...  2.51 us
  transfers between devices with their start and end apart: 10, of which 3 were waited for; matrix products, arithmetic and copies ran while one was open for 0% of the time, Pallas kernels for 9%

profile of v3, /device:TPU:1, one launch (start us, length us, event | category | flops | bytes accessed | tf_op | source)
XLA Modules:
  0.0 69.6 jit_solution(30078989377662686)
XLA Ops:
  0.6 1.8 %prep.1 = (s16[32,16,256]{2,1,0:T(8,128)(2,1)}, bf16[3,4,16,256]{3,2,1,0:T(8,128)(2,1)S(1)}, bf16[3,4,16,256]{3,2,1,0:T(8,128)(2,1)S(1)}) custom-call(f32[1,2,2,8,256]{4,3,2,1,0:T(8,128)} %p_ref.5, bf16[3,8,2,16,256]{4,3,2,1,0:T(8,128)(2,1)} %w_in.1), custom_call_target="tpu_custom_call" | custom-call | tf_op jit(solution)/shard_map/prep/pallas_call | solution.py:281
  2.4 2.1 %collective-permute-start = (bf16[3,4,16,256]{3,2,1,0:T(8,128)(2,1)S(1)}, bf16[3,4,16,256]{3,2,1,0:T(8,128)(2,1)S(1)}, u32[]{:S(2)}, u32[]{:S(2)}) collective-permute-start(bf16[3,4,16,256]{3,2,1,0:T(8,128)(2,1)S(1)} %get-tuple-element.15), channel_id=1, source_target_pairs={{0,8},{8,16},{16,24},{24,0},{1,9},{9,17},{17,25},{25,1},{2,10},{10... | collective-permute-start | bytes 294920 | tf_op jit(solution)/shard_map/ppermute | solution.py:290
  4.5 2.6 %collective-permute-start.2 = (bf16[3,4,16,256]{3,2,1,0:T(8,128)(2,1)S(1)}, bf16[3,4,16,256]{3,2,1,0:T(8,128)(2,1)S(1)}, u32[]{:S(2)}, u32[]{:S(2)}) collective-permute-start(bf16[3,4,16,256]{3,2,1,0:T(8,128)(2,1)S(1)} %get-tuple-element.16), channel_id=1, source_target_pairs={{0,16},{8,24},{16,0},{24,8},{1,17},{9,25},{17,1},{25,9},{2,18},{10... | collective-permute-start | bytes 294920 | tf_op jit(solution)/shard_map/ppermute | solution.py:290
  7.1 1.1 %collective-permute-start.4 = (bf16[3,4,16,256]{3,2,1,0:T(8,128)(2,1)S(1)}, bf16[3,4,16,256]{3,2,1,0:T(8,128)(2,1)S(1)}, u32[]{:S(2)}, u32[]{:S(2)}) collective-permute-start(bf16[3,4,16,256]{3,2,1,0:T(8,128)(2,1)S(1)} %get-tuple-element.15), channel_id=1, source_target_pairs={{0,24},{8,0},{16,8},{24,16},{1,25},{9,1},{17,9},{25,17},{2,26},{10... | collective-permute-start | bytes 294920 | tf_op jit(solution)/shard_map/ppermute | solution.py:290
  8.2 6.1 %all-to-all-start = ((s16[32,16,256]{2,1,0:T(8,128)(2,1)}), s16[32,16,256]{2,1,0:T(8,128)(2,1)S(1)}, u32[]{:S(2)}, u32[]{:S(2)}) async-start(s16[32,16,256]{2,1,0:T(8,128)(2,1)} %get-tuple-element.11), calls=%async_computation | async-start | bytes 524288 | tf_op jit(solution)/shard_map/all_to_all | solution.py:293
  14.3 2.5 %tables.1 = (bf16[12,256,256]{2,1,0:T(8,128)(2,1)S(1)}, bf16[2,256,256]{2,1,0:T(8,128)(2,1)S(1)}, bf16[2,256,256]{2,1,0:T(8,128)(2,1)S(1)}) custom-call(s32[8,12]{1,0:T(8,128)} %bitcast.7, s32[1,16]{1,0:T(1,128)} %kb_ref.3), custom_call_target="tpu_custom_call" | custom-call | flops 1000000000 | bytes 2097152 | tf_op jit(solution)/shard_map/tables/pallas_call | solution.py:298
  16.8 0.0 collective-permute-done.h1
  16.8 0.3 collective-permute-start.1
  17.1 0.0 collective-permute-done.2.h2
  17.1 0.3 collective-permute-start.3
  17.4 0.3 collective-permute-start.5
  17.7 3.5 %turns.1.turn_in = f32[12,2,128,256]{3,2,1,0:T(8,128)} custom-call(s32[1,16]{1,0:T(1,128)} %kb_ref.3, f32[12]{0:T(128)} %freq_ref.1, bf16[3,4,16,256]{3,2,1,0:T(8,128)(2,1)S(1)} %collective-permute-done.h1, bf16[3,4,16,256]{3,2,1,0:T(8,128)(2,1)S(1)} %collective-permute-done.2.h2, bf16[3,4,16,256]{3,2,1,0:T(8,128)(2,1)S(1)} %collective-permute-done.4.h3), custom_call_target="tpu_custom_call" | custom-call | flops 40000000000 | bytes 3145728 | tf_op jit(solution)/shard_map/turns/pallas_call | solution.py:312
  21.2 0.0 collective-permute-done.1.o1
  21.2 0.0 collective-permute-done.3.o2
  21.2 2.0 %all-to-all-done.p_ref = s16[32,16,256]{2,1,0:T(8,128)(2,1)S(1)} async-done(((s16[32,16,256]{2,1,0:T(8,128)(2,1)}), s16[32,16,256]{2,1,0:T(8,128)(2,1)S(1)}, u32[]{:S(2)}, u32[]{:S(2)}) %all-to-all-start) | async-done | bytes 262176 | tf_op jit(solution)/shard_map/all_to_all | solution.py:293
  23.2 7.1 %normal.1 = bf16[32,16,256]{2,1,0:T(8,128)(2,1)} custom-call(s32[8,12]{1,0:T(8,128)} %bitcast.8, s32[12]{0:T(128)} %count_ref.1, s16[32,16,256]{2,1,0:T(8,128)(2,1)S(1)} %all-to-all-done.p_ref, bf16[12,256,256]{2,1,0:T(8,128)(2,1)S(1)} %get-tuple-element.12.g, bf16[2,256,256]{2,1,0:T(8,128)(2,1)S(1)} %get-tuple-element.13.ft, ...), custom_call_target="tpu_custom_call" | custom-call | flops 2400000000 | bytes 8388608 | tf_op jit(solution)/shard_map/normal/pallas_call | solution.py:323
  30.3 5.4 %all-to-all-start.1 = ((bf16[32,16,256]{2,1,0:T(8,128)(2,1)}), bf16[32,16,256]{2,1,0:T(8,128)(2,1)S(1)}, u32[]{:S(2)}, u32[]{:S(2)}) async-start(bf16[32,16,256]{2,1,0:T(8,128)(2,1)} %normal.1), calls=%async_computation.1 | async-start | bytes 524288 | tf_op jit(solution)/shard_map/all_to_all | solution.py:347
  35.8 1.8 %collective-permute-start.6 = (bf16[1,2,2,8,256]{4,3,2,1,0:T(8,128)(2,1)S(1)}, bf16[1,2,2,8,256]{4,3,2,1,0:T(8,128)(2,1)S(1)}, u32[]{:S(2)}, u32[]{:S(2)}) collective-permute-start(bf16[1,2,2,8,256]{4,3,2,1,0:T(8,128)(2,1)S(1)} %convert_element_type.3), channel_id=1, source_target_pairs={{0,32},{32,64},{64,96},{96,128},{128,160},{160,192},{192,224},{224... | collective-permute-start | bytes 49160 | tf_op jit(solution)/shard_map/ppermute | solution.py:295
  37.5 4.0 %collective-permute-start.7 = (bf16[1,2,2,8,256]{4,3,2,1,0:T(8,128)(2,1)S(1)}, bf16[1,2,2,8,256]{4,3,2,1,0:T(8,128)(2,1)S(1)}, u32[]{:S(2)}, u32[]{:S(2)}) collective-permute-start(bf16[1,2,2,8,256]{4,3,2,1,0:T(8,128)(2,1)S(1)} %convert_element_type.3), channel_id=1, source_target_pairs={{0,224},{32,0},{64,32},{96,64},{128,96},{160,128},{192,160},{224,1... | collective-permute-start | bytes 49160 | tf_op jit(solution)/shard_map/ppermute | solution.py:296
  41.5 1.3 %collective-permute-done.6.low_ref = bf16[1,2,2,8,256]{4,3,2,1,0:T(8,128)(2,1)S(1)} collective-permute-done((bf16[1,2,2,8,256]{4,3,2,1,0:T(8,128)(2,1)S(1)}, bf16[1,2,2,8,256]{4,3,2,1,0:T(8,128)(2,1)S(1)}, u32[]{:S(2)}, u32[]{:S(2)}) %collective-permute-start.6) | collective-permute-done | bytes 16416 | tf_op jit(solution)/shard_map/ppermute | solution.py:295
  42.9 1.8 %all-to-all-done.1.parts_ref = bf16[32,16,256]{2,1,0:T(8,128)(2,1)S(1)} async-done(((bf16[32,16,256]{2,1,0:T(8,128)(2,1)}), bf16[32,16,256]{2,1,0:T(8,128)(2,1)S(1)}, u32[]{:S(2)}, u32[]{:S(2)}) %all-to-all-start.1) | async-done | bytes 262176 | tf_op jit(solution)/shard_map/all_to_all | solution.py:347
  44.6 0.1 applied.1
  44.8 24.0 %all_to_all.21 = f32[256,1,8]{2,1,0:T(1,128)S(1)} all-to-all(f32[256,1,8]{2,1,0:T(1,128)S(1)} %bitcast.6), channel_id=1, replica_groups=mesh['frames'=8,'segments'=4,'coils'=8] {'frames','segments','coils'}, dimensions={0} | all-to-all | bytes 16384 | tf_op jit(solution)/shard_map/all_to_all | solution.py:357
  68.8 0.8 %update.1 = (f32[1,2,2,8,256]{4,3,2,1,0:T(8,128)}, f32[1,2,2,8,256]{4,3,2,1,0:T(8,128)}, f32[1,2,2,8,256]{4,3,2,1,0:T(8,128)}) custom-call(f32[256,8]{1,0:T(8,128)S(1)} %bitcast.5, f32[1,2,2,8,256]{4,3,2,1,0:T(8,128)S(1)} %copy-done.2, f32[1,2,2,8,256]{4,3,2,1,0:T(8,128)S(1)} %copy-done.1, f32[1,2,2,8,256]{4,3,2,1,0:T(8,128)S(1)} %copy-done, ...), custom_call_target="tpu_custom_call" | custom-call | tf_op jit(solution)/shard_map/update/pallas_call | solution.py:359
  (10 shorter events, 0.0 us)
Async XLA Ops:
  2.4 14.4 %collective-permute-start = (bf16[3,4,16,256]{3,2,1,0:T(8,128)(2,1)S(1)}, bf16[3,4,16,256]{3,2,1,0:T(8,128)(2,1)S(1)}, u32[]{:S(2)}, u32[]{:S(2)}) collective-permute-start(bf16[3,4,16,256]{3,2,1,0:T(8,128)(2,1)S(1)} %get-tuple-element.15), channel_id=1, source_target_pairs={{0,8},{8,16},{16,24},{24,0},{1,9},{9,17},{17,25},{25,1},{2,10},{10... | collective-permute-start | bytes 294920 | tf_op jit(solution)/shard_map/ppermute | solution.py:290
  4.5 12.6 %collective-permute-start.2 = (bf16[3,4,16,256]{3,2,1,0:T(8,128)(2,1)S(1)}, bf16[3,4,16,256]{3,2,1,0:T(8,128)(2,1)S(1)}, u32[]{:S(2)}, u32[]{:S(2)}) collective-permute-start(bf16[3,4,16,256]{3,2,1,0:T(8,128)(2,1)S(1)} %get-tuple-element.16), channel_id=1, source_target_pairs={{0,16},{8,24},{16,0},{24,8},{1,17},{9,25},{17,1},{25,9},{2,18},{10... | collective-permute-start | bytes 294920 | tf_op jit(solution)/shard_map/ppermute | solution.py:290
  7.1 10.3 %collective-permute-start.4 = (bf16[3,4,16,256]{3,2,1,0:T(8,128)(2,1)S(1)}, bf16[3,4,16,256]{3,2,1,0:T(8,128)(2,1)S(1)}, u32[]{:S(2)}, u32[]{:S(2)}) collective-permute-start(bf16[3,4,16,256]{3,2,1,0:T(8,128)(2,1)S(1)} %get-tuple-element.15), channel_id=1, source_target_pairs={{0,24},{8,0},{16,8},{24,16},{1,25},{9,1},{17,9},{25,17},{2,26},{10... | collective-permute-start | bytes 294920 | tf_op jit(solution)/shard_map/ppermute | solution.py:290
  8.2 15.0 %all-to-all-start = ((s16[32,16,256]{2,1,0:T(8,128)(2,1)}), s16[32,16,256]{2,1,0:T(8,128)(2,1)S(1)}, u32[]{:S(2)}, u32[]{:S(2)}) async-start(s16[32,16,256]{2,1,0:T(8,128)(2,1)} %get-tuple-element.11), calls=%async_computation | async-start | bytes 524288 | tf_op jit(solution)/shard_map/all_to_all | solution.py:293
  16.8 4.3 %collective-permute-start.1 = (bf16[3,4,16,256]{3,2,1,0:T(8,128)(2,1)S(1)}, bf16[3,4,16,256]{3,2,1,0:T(8,128)(2,1)S(1)}, u32[]{:S(2)}, u32[]{:S(2)}) collective-permute-start(bf16[3,4,16,256]{3,2,1,0:T(8,128)(2,1)S(1)} %collective-permute-done.h1), channel_id=1, source_target_pairs={{0,1},{1,0},{2,3},{3,2},{4,5},{5,4},{6,7},{7,6},{8,9},{9,8},{10,11... | collective-permute-start | bytes 294920 | tf_op jit(solution)/shard_map/ppermute | solution.py:322
  17.1 4.0 %collective-permute-start.3 = (bf16[3,4,16,256]{3,2,1,0:T(8,128)(2,1)S(1)}, bf16[3,4,16,256]{3,2,1,0:T(8,128)(2,1)S(1)}, u32[]{:S(2)}, u32[]{:S(2)}) collective-permute-start(bf16[3,4,16,256]{3,2,1,0:T(8,128)(2,1)S(1)} %collective-permute-done.2.h2), channel_id=1, source_target_pairs={{0,1},{1,0},{2,3},{3,2},{4,5},{5,4},{6,7},{7,6},{8,9},{9,8},{10,11... | collective-permute-start | bytes 294920 | tf_op jit(solution)/shard_map/ppermute | solution.py:322
  17.4 3.8 %collective-permute-start.5 = (bf16[3,4,16,256]{3,2,1,0:T(8,128)(2,1)S(1)}, bf16[3,4,16,256]{3,2,1,0:T(8,128)(2,1)S(1)}, u32[]{:S(2)}, u32[]{:S(2)}) collective-permute-start(bf16[3,4,16,256]{3,2,1,0:T(8,128)(2,1)S(1)} %collective-permute-done.4.h3), channel_id=1, source_target_pairs={{0,1},{1,0},{2,3},{3,2},{4,5},{5,4},{6,7},{7,6},{8,9},{9,8},{10,11... | collective-permute-start | bytes 294920 | tf_op jit(solution)/shard_map/ppermute | solution.py:322
  23.2 12.5 %copy-start = (f32[1,2,2,8,256]{4,3,2,1,0:T(8,128)S(1)}, f32[1,2,2,8,256]{4,3,2,1,0:T(8,128)}, u32[]{:S(2)}) copy-start(f32[1,2,2,8,256]{4,3,2,1,0:T(8,128)} %p_ref.5) | copy-start | bytes 98308
  23.2 21.4 %copy-start.1 = (f32[1,2,2,8,256]{4,3,2,1,0:T(8,128)S(1)}, f32[1,2,2,8,256]{4,3,2,1,0:T(8,128)}, u32[]{:S(2)}) copy-start(f32[1,2,2,8,256]{4,3,2,1,0:T(8,128)} %r_ref.3) | copy-start | bytes 98308
  23.2 45.6 %copy-start.2 = (f32[1,2,2,8,256]{4,3,2,1,0:T(8,128)S(1)}, f32[1,2,2,8,256]{4,3,2,1,0:T(8,128)}, u32[]{:S(2)}) copy-start(f32[1,2,2,8,256]{4,3,2,1,0:T(8,128)} %x_ref.1) | copy-start | bytes 98308
  30.3 14.3 %all-to-all-start.1 = ((bf16[32,16,256]{2,1,0:T(8,128)(2,1)}), bf16[32,16,256]{2,1,0:T(8,128)(2,1)S(1)}, u32[]{:S(2)}, u32[]{:S(2)}) async-start(bf16[32,16,256]{2,1,0:T(8,128)(2,1)} %normal.1), calls=%async_computation.1 | async-start | bytes 524288 | tf_op jit(solution)/shard_map/all_to_all | solution.py:347
  35.8 7.1 %collective-permute-start.6 = (bf16[1,2,2,8,256]{4,3,2,1,0:T(8,128)(2,1)S(1)}, bf16[1,2,2,8,256]{4,3,2,1,0:T(8,128)(2,1)S(1)}, u32[]{:S(2)}, u32[]{:S(2)}) collective-permute-start(bf16[1,2,2,8,256]{4,3,2,1,0:T(8,128)(2,1)S(1)} %convert_element_type.3), channel_id=1, source_target_pairs={{0,32},{32,64},{64,96},{96,128},{128,160},{160,192},{192,224},{224... | collective-permute-start | bytes 49160 | tf_op jit(solution)/shard_map/ppermute | solution.py:295
  37.5 5.3 %collective-permute-start.7 = (bf16[1,2,2,8,256]{4,3,2,1,0:T(8,128)(2,1)S(1)}, bf16[1,2,2,8,256]{4,3,2,1,0:T(8,128)(2,1)S(1)}, u32[]{:S(2)}, u32[]{:S(2)}) collective-permute-start(bf16[1,2,2,8,256]{4,3,2,1,0:T(8,128)(2,1)S(1)} %convert_element_type.3), channel_id=1, source_target_pairs={{0,224},{32,0},{64,32},{96,64},{128,96},{160,128},{192,160},{224,1... | collective-permute-start | bytes 49160 | tf_op jit(solution)/shard_map/ppermute | solution.py:296

commit v4 on v3

--- a/solution.py
+++ b/solution.py
@@ -31,22 +31,24 @@
 SPACE = ("segments", "coils")
 
 
-def sin_cos(angle):
-    half = angle * 0.5
-    sq = half * half
-    s = F32(1.0 / math.factorial(13))
-    for n in (11, 9, 7, 5, 3, 1):
+def sin_cos(quarter):
+    sq = quarter * quarter
+    s = F32(1.0 / math.factorial(9))
+    for n in (7, 5, 3, 1):
         s = s * sq + F32((-1.0) ** (n // 2) / math.factorial(n))
-    s = s * half
-    c = F32(1.0 / math.factorial(16))
-    for n in (14, 12, 10, 8, 6, 4, 2, 0):
+    s = s * quarter
+    c = F32(-1.0 / math.factorial(10))
+    for n in (8, 6, 4, 2, 0):
         c = c * sq + F32((-1.0) ** (n // 2) / math.factorial(n))
-    return 2.0 * s * c, 1.0 - 2.0 * s * s
+    twice = s + s
+    s, c = twice * c, 1.0 - twice * s
+    twice = s + s
+    return twice * c, 1.0 - twice * s
 
 
 def unit_parts(products):
     n = ((products + 128) & 255) - 128
-    s, c = sin_cos(n.astype(F32) * F32(2.0 * math.pi / 256))
+    s, c = sin_cos(n.astype(F32) * F32(0.5 * math.pi / 256))
     return c * F32(1.0 / 16.0), s * F32(-1.0 / 16.0)
 
 
@@ -82,32 +84,41 @@
                 send_ref[(pair * 2 + q) * 8 + xc] = code
 
 
-def turns_kernel(kb_ref, freq_ref, h1, h2, h3, turn_out, turn, turn_sem):
-    kbs = [kb_ref[0, j] for j in range(KR // KB)]
-    ky = spread(kbs, lax.broadcasted_iota(jnp.int32, (KR, KR), 0), KB)
-    cy = (((ky + 128) & 255) - 128).astype(F32) * F32(1.0 / 128.0)
-    cy = jnp.concatenate([cy, cy], axis=1)
-    cx_index = lax.broadcasted_iota(jnp.int32, (KR, NX), 1)
-    cx = (((cx_index + 128) & 255) - 128).astype(F32) * F32(1.0 / 128.0)
-    elapsed = jnp.sqrt(cy * cy + cx * cx)
+def turns_kernel(elapsed_ref, freq_ref, h1, h2, h3, turn_out, turn, turn_sem):
     saves = [pltpu.make_async_copy(turn.at[slot], turn_out.at[slot], turn_sem.at[slot]) for slot in range(NSEG)]
     for slot in range(NSEG):
-        turn[slot, 1], turn[slot, 0] = sin_cos(freq_ref[segment_of(slot)] * elapsed)
+        turn[slot, 1], turn[slot, 0] = sin_cos(freq_ref[slot] * elapsed_ref[...])
         saves[slot].start()
     for save in saves:
         save.wait()
 
 
-def tables_kernel(bands_ref, kb_ref, g_ref, ft, gx_ref, e):
-    kbs = [kb_ref[0, j] for j in range(KR // KB)]
-    ky_col = spread(kbs, lax.broadcasted_iota(jnp.int32, (KR, KR), 0), KB)
-    ky_row = spread(kbs, lax.broadcasted_iota(jnp.int32, (8, KR), 1), KB)[:1]
-    ky_wide = jnp.concatenate([ky_col, ky_col], axis=1)
+def tables_kernel(
+    bands_in, kb_in, freq_in, g_ref, ft, gx_ref, elapsed_ref, quarter_ref, e, bands_ref, kb_ref, freq_ref, sem
+):
+    loads = [
+        pltpu.make_async_copy(source, target, sem.at[i])
+        for i, (source, target) in enumerate([(bands_in, bands_ref), (kb_in, kb_ref), (freq_in, freq_ref)])
+    ]
+    for load in loads:
+        load.start()
     rows = lax.broadcasted_iota(jnp.int32, (NX, NX), 0)
     cols = lax.broadcasted_iota(jnp.int32, (NX, NX), 1)
     re, im = unit_parts(rows * cols)
     gx_ref[0] = re.astype(BF16)
     gx_ref[1] = im.astype(BF16)
+    for load in loads:
+        load.wait()
+    for slot in range(NSEG):
+        quarter_ref[slot] = jnp.broadcast_to(freq_ref[segment_of(slot)] * F32(0.25), (1, NX))
+    kbs = [kb_ref[0, j] for j in range(KR // KB)]
+    ky_col = spread(kbs, lax.broadcasted_iota(jnp.int32, (KR, KR), 0), KB)
+    ky_wide = jnp.concatenate([ky_col, ky_col], axis=1)
+    cy = (((ky_wide + 128) & 255) - 128).astype(F32) * F32(1.0 / 128.0)
+    cx_index = lax.broadcasted_iota(jnp.int32, (KR, NX), 1)
+    cx = (((cx_index + 128) & 255) - 128).astype(F32) * F32(1.0 / 128.0)
+    elapsed_ref[...] = jnp.sqrt(cy * cy + cx * cx)
+    ky_row = spread(kbs, lax.broadcasted_iota(jnp.int32, (8, KR), 1), KB)[:1]
     re, im = unit_parts(lax.broadcasted_iota(jnp.int32, (NY, KR), 0) * ky_row)
     ft[0, :, :KR] = re.astype(BF16)
     ft[0, :, KR:] = im.astype(BF16)
@@ -133,8 +144,8 @@
 
 
 def normal_kernel(
-    bands_ref, count_ref, p_ref, g, ft, gx_ref, h1, o1, h2, o2, h3, o3, sens_in, w_in, turn_in, out_ref,
-    coil, blk, first, ks, acc, mine, near, gx, turn, sem,
+    bands_in, count_in, p_ref, g, ft, gx_ref, h1, o1, h2, o2, h3, o3, sens_in, w_in, turn_in, out,
+    coil, blk, first, ks, acc, mine, near, gx, turn, out_ref, bands_ref, count_ref, sem, out_sem,
 ):
     y = lax.axis_index("segments")
     plane = lax.rem(y, 2)
@@ -146,6 +157,8 @@
                 (sens_in.at[y // 2, plane], mine),
                 (w_in.at[:, pl.ds(core * HALF, HALF), plane], near.at[0]),
                 (w_in.at[:, pl.ds((1 - core) * HALF, HALF), plane], near.at[1]),
+                (bands_in, bands_ref),
+                (count_in, count_ref),
                 (turn_in, turn),
             ]
         )
@@ -168,6 +181,7 @@
         at = pl.ds(pl.multiple_of(bands_ref[j, seg] * BR, BR), BR)
         return w.astype(F32) * live, at
 
+    acc[...] = jnp.zeros_like(acc)
     loads[0].wait()
     for chunk in range(4):
         rows = slice(chunk * 64, chunk * 64 + 64)
@@ -178,9 +192,8 @@
         sim = mine[1, rows].astype(F32)
         coil[0, rows] = sre * pre - sim * pim
         coil[1, rows] = sre * pim + sim * pre
-    acc[...] = jnp.zeros_like(acc)
-    loads[1].wait()
-    loads[2].wait()
+    for load in loads[1:5]:
+        load.wait()
     for slot in range(NSEG):
         for t in range(OT):
             w, at = weight(slot, t)
@@ -189,7 +202,7 @@
         got = mm(g[slot], blk[slot]).astype(BF16)
         first[slot * KR : (slot + 1) * KR, :NX] = got[:KR]
         first[slot * KR : (slot + 1) * KR, NX:] = got[KR:]
-    loads[3].wait()
+    loads[5].wait()
     for pair in range(NSEG // 2):
         spec = mm(first[pair * 2 * KR : (pair + 1) * 2 * KR], gx[0])
         tre, tim = 0.0, 0.0
@@ -217,6 +230,7 @@
             for t, (w, at) in enumerate(places):
                 acc[0, at] += band[t * BR : (t + 1) * BR] * w
                 acc[1, at] += band[KR + t * BR : KR + (t + 1) * BR] * w
+    saves = []
     for chunk in range(4):
         rows = slice(chunk * 64, chunk * 64 + 64)
         sre = mine[0, rows].astype(F32)
@@ -224,7 +238,12 @@
         are, aim = acc[0, rows], acc[1, rows]
         out_re = (sre * are + sim * aim).reshape(8, ROWS, NX)
         out_im = (sre * aim - sim * are).reshape(8, ROWS, NX)
-        out_ref[chunk * 8 : chunk * 8 + 8] = jnp.concatenate([out_re, out_im], axis=1).astype(BF16)
+        here = slice(chunk * 8, chunk * 8 + 8)
+        out_ref[here] = jnp.concatenate([out_re, out_im], axis=1).astype(BF16)
+        saves.append(pltpu.make_async_copy(out_ref.at[here], out.at[here], out_sem.at[chunk]))
+        saves[-1].start()
+    for save in saves:
+        save.wait()
 
 
 def applied_kernel(parts_ref, r_ref, p_ref, low_ref, high_ref, applied_ref, sums_ref):
@@ -268,7 +287,6 @@
 
 
 VM = pl.BlockSpec(memory_space=pltpu.VMEM)
-SM = pl.BlockSpec(memory_space=pltpu.SMEM)
 HB = pl.BlockSpec(memory_space=pltpu.HBM)
 
 
@@ -295,36 +313,44 @@
     low = lax.ppermute(halo, "frames", [(i, (i + 1) % 8) for i in range(8)])
     high = lax.ppermute(halo, "frames", [(i, (i + 7) % 8) for i in range(8)])
     bands = hbm(band_ids.T)
-    g, ft, gx = pl.pallas_call(
+    g, ft, gx, elapsed, quarter = pl.pallas_call(
         tables_kernel,
-        in_specs=[SM, SM],
-        out_specs=[VM, VM, VM],
+        in_specs=[HB] * 3,
+        out_specs=[VM] * 5,
         out_shape=[
             jax.ShapeDtypeStruct((NSEG, 2 * KR, 2 * KR), BF16),
             jax.ShapeDtypeStruct((2, NY, 2 * KR), BF16),
             jax.ShapeDtypeStruct((2, NX, NX), BF16),
+            jax.ShapeDtypeStruct((KR, NX), F32),
+            jax.ShapeDtypeStruct((NSEG, 1, NX), F32),
         ],
-        scratch_shapes=[pltpu.VMEM((2, 2 * KR, NY), BF16)],
+        scratch_shapes=[
+            pltpu.VMEM((2, 2 * KR, NY), BF16),
+            pltpu.SMEM((OT, NSEG), jnp.int32),
+            pltpu.SMEM((1, KR // KB), jnp.int32),
+            pltpu.SMEM((NSEG,), F32),
+            pltpu.SemaphoreType.DMA((3,)),
+        ],
         compiler_params=pltpu.CompilerParams(vmem_limit_bytes=32 << 20),
         cost_estimate=pl.CostEstimate(flops=1_000_000_000, bytes_accessed=2 << 20, transcendentals=0),
         name="tables",
-    )(bands, hbm(k_bands))
+    )(bands, hbm(k_bands), hbm(seg_freq))
     turn = pl.pallas_call(
         turns_kernel,
-        in_specs=[SM, SM] + [pl.BlockSpec(memory_space=pl.ANY)] * 3,
+        in_specs=[VM, VM] + [pl.BlockSpec(memory_space=pl.ANY)] * 3,
         out_specs=HB,
         out_shape=pltpu.HBM((NSEG, 2, KR, NX), F32),
         scratch_shapes=[pltpu.VMEM((NSEG, 2, KR, NX), F32), pltpu.SemaphoreType.DMA((NSEG,))],
         compiler_params=pltpu.CompilerParams(vmem_limit_bytes=32 << 20),
         cost_estimate=pl.CostEstimate(flops=40_000_000_000, bytes_accessed=3 << 20, transcendentals=0),
         name="turns",
-    )(hbm(k_bands), hbm(seg_freq), *halves)
+    )(elapsed, quarter, *halves)
     others = [lax.ppermute(half, "coils", [(i, i ^ 1) for i in range(8)]) for half in halves]
     parts = pl.pallas_call(
         normal_kernel,
-        in_specs=[SM] * 2 + [VM] * 10 + [HB] * 3,
-        out_specs=VM,
-        out_shape=jax.ShapeDtypeStruct((GROUP, 2 * ROWS, NX), BF16),
+        in_specs=[HB] * 2 + [VM] * 10 + [HB] * 3,
+        out_specs=HB,
+        out_shape=pltpu.HBM((GROUP, 2 * ROWS, NX), BF16),
         scratch_shapes=[
             pltpu.VMEM((2, NY, NX), F32),
             pltpu.VMEM((NSEG, 2 * KR, NX), BF16),
@@ -335,6 +361,10 @@
             pltpu.VMEM((2, SEGS_DEV, HALF, BR, NX), BF16),
             pltpu.VMEM((2, 2 * NX, 2 * NX), BF16),
             pltpu.VMEM((NSEG, 2, KR, NX), F32),
+            pltpu.VMEM((GROUP, 2 * ROWS, NX), BF16),
+            pltpu.SMEM((OT, NSEG), jnp.int32),
+            pltpu.SMEM((NSEG,), jnp.int32),
+            pltpu.SemaphoreType.DMA((6,)),
             pltpu.SemaphoreType.DMA((4,)),
         ],
         compiler_params=pltpu.CompilerParams(vmem_limit_bytes=32 << 20),

time: 70 us -> 67.7 us (0.967)
  Pallas kernels: 15.8 us -> 13.4 us
  waiting for transfers between devices: 5.13 us -> 6.75 us
  starting transfers between devices: 24 us -> 22.4 us
    pallas_call x3, Pallas kernels: 13.1 us -> 10.7 us  [the longest x1 6.22 us: local(): pl.pallas_call(normal_kernel, in_specs=[HB] * 2 + [VM] * 10 + [HB] * 3, o...]
    all_to_all x1, waiting for transfers between devices: 2 us -> 3.52 us  [local(): whole = lax.all_to_all(send, SPACE, 0, 0, tiled=True)]
    all_to_all x1, starting transfers between devices: 5.42 us -> 3.94 us  [local(): parts = lax.all_to_all(parts, SPACE, 0, 0, tiled=True)]
  transfers between devices with their start and end apart: 10 -> 10, of which waited for: 3 -> 3; matrix products, arithmetic and copies ran while one was open for 0% -> 0% of each run, Pallas kernels for 9% -> 7%
where the time goes in v4:
time: 67.7 us; the launch traced here: 67.3 us
  blocking collectives  24 us (35%)
  starting transfers between devices  22.4 us (33%)
  Pallas kernels  13.4 us (20%)
  waiting for transfers between devices  6.75 us (10%)
  between operations  0.73 us (1%)
    all_to_all x1, blocking collectives, local(): lax.all_to_all(sums, ('frames', 'segments', 'coils'), 0, 0, tiled=True)  24 us
    pallas_call x1, Pallas kernels, local(): pl.pallas_call(normal_kernel, in_specs=[HB] * 2 + [VM] * 10 + [HB] * 3, o...  6.22 us
    all_to_all x1, starting transfers between devices, local(): whole = lax.all_to_all(send, SPACE, 0, 0, tiled=True)  6.08 us
    ppermute x3, starting transfers between devices, local(): lax.ppermute(same if k == 2 else other, 'segments', [(i, (i + k) % 4) for...  5.81 us
    ppermute x1, starting transfers between devices, local(): high = lax.ppermute(halo, 'frames', [(i, (i + 7) % 8) for i in range(8)])  4.05 us
    all_to_all x1, starting transfers between devices, local(): parts = lax.all_to_all(parts, SPACE, 0, 0, tiled=True)  3.94 us
    all_to_all x1, waiting for transfers between devices, local(): whole = lax.all_to_all(send, SPACE, 0, 0, tiled=True)  3.52 us
    pallas_call x1, Pallas kernels, local(): pl.pallas_call(turns_kernel, in_specs=[VM, VM] + [pl.BlockSpec(memory_spa...  2.29 us
  transfers between devices with their start and end apart: 10, of which 3 were waited for; matrix products, arithmetic and copies ran while one was open for 0% of the time, Pallas kernels for 7%

profile of v4, /device:TPU:1, one launch (start us, length us, event | category | flops | bytes accessed | tf_op | source)
XLA Modules:
  0.0 67.3 jit_solution(8312876082341491956)
XLA Ops:
  0.6 1.8 %prep.1 = (s16[32,16,256]{2,1,0:T(8,128)(2,1)}, bf16[3,4,16,256]{3,2,1,0:T(8,128)(2,1)S(1)}, bf16[3,4,16,256]{3,2,1,0:T(8,128)(2,1)S(1)}) custom-call(f32[1,2,2,8,256]{4,3,2,1,0:T(8,128)} %p_ref.5, bf16[3,8,2,16,256]{4,3,2,1,0:T(8,128)(2,1)} %w_in.1), custom_call_target="tpu_custom_call" | custom-call | tf_op jit(solution)/shard_map/prep/pallas_call | solution.py:299
  2.4 2.1 %collective-permute-start = (bf16[3,4,16,256]{3,2,1,0:T(8,128)(2,1)S(1)}, bf16[3,4,16,256]{3,2,1,0:T(8,128)(2,1)S(1)}, u32[]{:S(2)}, u32[]{:S(2)}) collective-permute-start(bf16[3,4,16,256]{3,2,1,0:T(8,128)(2,1)S(1)} %get-tuple-element.17), channel_id=1, source_target_pairs={{0,8},{8,16},{16,24},{24,0},{1,9},{9,17},{17,25},{25,1},{2,10},{10... | collective-permute-start | bytes 294920 | tf_op jit(solution)/shard_map/ppermute | solution.py:308
  4.5 2.6 %collective-permute-start.2 = (bf16[3,4,16,256]{3,2,1,0:T(8,128)(2,1)S(1)}, bf16[3,4,16,256]{3,2,1,0:T(8,128)(2,1)S(1)}, u32[]{:S(2)}, u32[]{:S(2)}) collective-permute-start(bf16[3,4,16,256]{3,2,1,0:T(8,128)(2,1)S(1)} %get-tuple-element.18), channel_id=1, source_target_pairs={{0,16},{8,24},{16,0},{24,8},{1,17},{9,25},{17,1},{25,9},{2,18},{10... | collective-permute-start | bytes 294920 | tf_op jit(solution)/shard_map/ppermute | solution.py:308
  7.1 1.1 %collective-permute-start.4 = (bf16[3,4,16,256]{3,2,1,0:T(8,128)(2,1)S(1)}, bf16[3,4,16,256]{3,2,1,0:T(8,128)(2,1)S(1)}, u32[]{:S(2)}, u32[]{:S(2)}) collective-permute-start(bf16[3,4,16,256]{3,2,1,0:T(8,128)(2,1)S(1)} %get-tuple-element.17), channel_id=1, source_target_pairs={{0,24},{8,0},{16,8},{24,16},{1,25},{9,1},{17,9},{25,17},{2,26},{10... | collective-permute-start | bytes 294920 | tf_op jit(solution)/shard_map/ppermute | solution.py:308
  8.2 6.1 %all-to-all-start = ((s16[32,16,256]{2,1,0:T(8,128)(2,1)}), s16[32,16,256]{2,1,0:T(8,128)(2,1)S(1)}, u32[]{:S(2)}, u32[]{:S(2)}) async-start(s16[32,16,256]{2,1,0:T(8,128)(2,1)} %get-tuple-element.13), calls=%async_computation | async-start | bytes 524288 | tf_op jit(solution)/shard_map/all_to_all | solution.py:311
  14.3 2.2 %tables.1 = (bf16[12,256,256]{2,1,0:T(8,128)(2,1)S(1)}, bf16[2,256,256]{2,1,0:T(8,128)(2,1)S(1)}, bf16[2,256,256]{2,1,0:T(8,128)(2,1)S(1)}, f32[128,256]{1,0:T(8,128)S(1)}, f32[12,1,256]{2,1,0:T(1,128)S(1)}) custom-call(s32[8,12]{1,0:T(8,128)} %bitcast.7, s32[1,16]{1,0:T(1,128)} %kb_in.1, f32[12]{0:T(128)} %freq_in.1), custom_call_target="tpu_custom_call" | custom-call | flops 1000000000 | bytes 2097152 | tf_op jit(solution)/shard_map/tables/pallas_call | solution.py:316
  16.5 0.3 collective-permute-start.1
  16.8 0.3 collective-permute-start.3
  17.1 0.0 collective-permute-done.4.h3
  17.1 0.2 collective-permute-start.5
  17.3 2.3 %turns.1.turn_in = f32[12,2,128,256]{3,2,1,0:T(8,128)} custom-call(f32[128,256]{1,0:T(8,128)S(1)} %get-tuple-element.19.elapsed_ref, f32[12,1,256]{2,1,0:T(1,128)S(1)} %get-tuple-element.20.freq_ref, bf16[3,4,16,256]{3,2,1,0:T(8,128)(2,1)S(1)} %collective-permute-done.h1, bf16[3,4,16,256]{3,2,1,0:T(8,128)(2,1)S(1)} %collective-permute-done.2.h2, ...), custom_call_target="tpu_custom_call" | custom-call | flops 40000000000 | bytes 3145728 | tf_op jit(solution)/shard_map/turns/pallas_call | solution.py:338
  19.6 0.0 collective-permute-done.1.o1
  19.7 0.0 collective-permute-done.5.o3
  19.7 3.5 %all-to-all-done.p_ref = s16[32,16,256]{2,1,0:T(8,128)(2,1)S(1)} async-done(((s16[32,16,256]{2,1,0:T(8,128)(2,1)}), s16[32,16,256]{2,1,0:T(8,128)(2,1)S(1)}, u32[]{:S(2)}, u32[]{:S(2)}) %all-to-all-start) | async-done | bytes 262176 | tf_op jit(solution)/shard_map/all_to_all | solution.py:311
  23.2 6.2 %normal.1 = bf16[32,16,256]{2,1,0:T(8,128)(2,1)} custom-call(s32[8,12]{1,0:T(8,128)} %bitcast.8, s32[12]{0:T(128)} %count_in.1, s16[32,16,256]{2,1,0:T(8,128)(2,1)S(1)} %all-to-all-done.p_ref, bf16[12,256,256]{2,1,0:T(8,128)(2,1)S(1)} %get-tuple-element.14.g, bf16[2,256,256]{2,1,0:T(8,128)(2,1)S(1)} %get-tuple-element.15.ft, ...), custom_call_target="tpu_custom_call" | custom-call | flops 2400000000 | bytes 8388608 | tf_op jit(solution)/shard_map/normal/pallas_call | solution.py:349
  29.4 3.9 %all-to-all-start.1 = ((bf16[32,16,256]{2,1,0:T(8,128)(2,1)}), bf16[32,16,256]{2,1,0:T(8,128)(2,1)S(1)}, u32[]{:S(2)}, u32[]{:S(2)}) async-start(bf16[32,16,256]{2,1,0:T(8,128)(2,1)} %normal.1), calls=%async_computation.1 | async-start | bytes 524288 | tf_op jit(solution)/shard_map/all_to_all | solution.py:377
  33.4 1.7 %collective-permute-start.6 = (bf16[1,2,2,8,256]{4,3,2,1,0:T(8,128)(2,1)S(1)}, bf16[1,2,2,8,256]{4,3,2,1,0:T(8,128)(2,1)S(1)}, u32[]{:S(2)}, u32[]{:S(2)}) collective-permute-start(bf16[1,2,2,8,256]{4,3,2,1,0:T(8,128)(2,1)S(1)} %convert_element_type.3), channel_id=1, source_target_pairs={{0,32},{32,64},{64,96},{96,128},{128,160},{160,192},{192,224},{224... | collective-permute-start | bytes 49160 | tf_op jit(solution)/shard_map/ppermute | solution.py:313
  35.1 4.1 %collective-permute-start.7 = (bf16[1,2,2,8,256]{4,3,2,1,0:T(8,128)(2,1)S(1)}, bf16[1,2,2,8,256]{4,3,2,1,0:T(8,128)(2,1)S(1)}, u32[]{:S(2)}, u32[]{:S(2)}) collective-permute-start(bf16[1,2,2,8,256]{4,3,2,1,0:T(8,128)(2,1)S(1)} %convert_element_type.3), channel_id=1, source_target_pairs={{0,224},{32,0},{64,32},{96,64},{128,96},{160,128},{192,160},{224,1... | collective-permute-start | bytes 49160 | tf_op jit(solution)/shard_map/ppermute | solution.py:314
  39.2 1.3 %collective-permute-done.6.low_ref = bf16[1,2,2,8,256]{4,3,2,1,0:T(8,128)(2,1)S(1)} collective-permute-done((bf16[1,2,2,8,256]{4,3,2,1,0:T(8,128)(2,1)S(1)}, bf16[1,2,2,8,256]{4,3,2,1,0:T(8,128)(2,1)S(1)}, u32[]{:S(2)}, u32[]{:S(2)}) %collective-permute-start.6) | collective-permute-done | bytes 16416 | tf_op jit(solution)/shard_map/ppermute | solution.py:313
  40.5 0.0 collective-permute-done.7.high_ref
  40.5 1.9 %all-to-all-done.1.parts_ref = bf16[32,16,256]{2,1,0:T(8,128)(2,1)S(1)} async-done(((bf16[32,16,256]{2,1,0:T(8,128)(2,1)}), bf16[32,16,256]{2,1,0:T(8,128)(2,1)S(1)}, u32[]{:S(2)}, u32[]{:S(2)}) %all-to-all-start.1) | async-done | bytes 262176 | tf_op jit(solution)/shard_map/all_to_all | solution.py:377
  42.4 0.1 applied.1
  42.5 24.0 %all_to_all.21 = f32[256,1,8]{2,1,0:T(1,128)S(1)} all-to-all(f32[256,1,8]{2,1,0:T(1,128)S(1)} %bitcast.6), channel_id=1, replica_groups=mesh['frames'=8,'segments'=4,'coils'=8] {'frames','segments','coils'}, dimensions={0} | all-to-all | bytes 16384 | tf_op jit(solution)/shard_map/all_to_all | solution.py:387
  66.5 0.8 %update.1 = (f32[1,2,2,8,256]{4,3,2,1,0:T(8,128)}, f32[1,2,2,8,256]{4,3,2,1,0:T(8,128)}, f32[1,2,2,8,256]{4,3,2,1,0:T(8,128)}) custom-call(f32[256,8]{1,0:T(8,128)S(1)} %bitcast.5, f32[1,2,2,8,256]{4,3,2,1,0:T(8,128)S(1)} %copy-done.2, f32[1,2,2,8,256]{4,3,2,1,0:T(8,128)S(1)} %copy-done.1, f32[1,2,2,8,256]{4,3,2,1,0:T(8,128)S(1)} %copy-done, ...), custom_call_target="tpu_custom_call" | custom-call | tf_op jit(solution)/shard_map/update/pallas_call | solution.py:389
  (10 shorter events, 0.0 us)
Async XLA Ops:
  2.4 14.1 %collective-permute-start = (bf16[3,4,16,256]{3,2,1,0:T(8,128)(2,1)S(1)}, bf16[3,4,16,256]{3,2,1,0:T(8,128)(2,1)S(1)}, u32[]{:S(2)}, u32[]{:S(2)}) collective-permute-start(bf16[3,4,16,256]{3,2,1,0:T(8,128)(2,1)S(1)} %get-tuple-element.17), channel_id=1, source_target_pairs={{0,8},{8,16},{16,24},{24,0},{1,9},{9,17},{17,25},{25,1},{2,10},{10... | collective-permute-start | bytes 294920 | tf_op jit(solution)/shard_map/ppermute | solution.py:308
  4.5 12.3 %collective-permute-start.2 = (bf16[3,4,16,256]{3,2,1,0:T(8,128)(2,1)S(1)}, bf16[3,4,16,256]{3,2,1,0:T(8,128)(2,1)S(1)}, u32[]{:S(2)}, u32[]{:S(2)}) collective-permute-start(bf16[3,4,16,256]{3,2,1,0:T(8,128)(2,1)S(1)} %get-tuple-element.18), channel_id=1, source_target_pairs={{0,16},{8,24},{16,0},{24,8},{1,17},{9,25},{17,1},{25,9},{2,18},{10... | collective-permute-start | bytes 294920 | tf_op jit(solution)/shard_map/ppermute | solution.py:308
  7.1 10.0 %collective-permute-start.4 = (bf16[3,4,16,256]{3,2,1,0:T(8,128)(2,1)S(1)}, bf16[3,4,16,256]{3,2,1,0:T(8,128)(2,1)S(1)}, u32[]{:S(2)}, u32[]{:S(2)}) collective-permute-start(bf16[3,4,16,256]{3,2,1,0:T(8,128)(2,1)S(1)} %get-tuple-element.17), channel_id=1, source_target_pairs={{0,24},{8,0},{16,8},{24,16},{1,25},{9,1},{17,9},{25,17},{2,26},{10... | collective-permute-start | bytes 294920 | tf_op jit(solution)/shard_map/ppermute | solution.py:308
  8.2 15.0 %all-to-all-start = ((s16[32,16,256]{2,1,0:T(8,128)(2,1)}), s16[32,16,256]{2,1,0:T(8,128)(2,1)S(1)}, u32[]{:S(2)}, u32[]{:S(2)}) async-start(s16[32,16,256]{2,1,0:T(8,128)(2,1)} %get-tuple-element.13), calls=%async_computation | async-start | bytes 524288 | tf_op jit(solution)/shard_map/all_to_all | solution.py:311
  16.5 3.1 %collective-permute-start.1 = (bf16[3,4,16,256]{3,2,1,0:T(8,128)(2,1)S(1)}, bf16[3,4,16,256]{3,2,1,0:T(8,128)(2,1)S(1)}, u32[]{:S(2)}, u32[]{:S(2)}) collective-permute-start(bf16[3,4,16,256]{3,2,1,0:T(8,128)(2,1)S(1)} %collective-permute-done.h1), channel_id=1, source_target_pairs={{0,1},{1,0},{2,3},{3,2},{4,5},{5,4},{6,7},{7,6},{8,9},{9,8},{10,11... | collective-permute-start | bytes 294920 | tf_op jit(solution)/shard_map/ppermute | solution.py:348
  16.8 2.8 %collective-permute-start.3 = (bf16[3,4,16,256]{3,2,1,0:T(8,128)(2,1)S(1)}, bf16[3,4,16,256]{3,2,1,0:T(8,128)(2,1)S(1)}, u32[]{:S(2)}, u32[]{:S(2)}) collective-permute-start(bf16[3,4,16,256]{3,2,1,0:T(8,128)(2,1)S(1)} %collective-permute-done.2.h2), channel_id=1, source_target_pairs={{0,1},{1,0},{2,3},{3,2},{4,5},{5,4},{6,7},{7,6},{8,9},{9,8},{10,11... | collective-permute-start | bytes 294920 | tf_op jit(solution)/shard_map/ppermute | solution.py:348
  17.1 2.6 %collective-permute-start.5 = (bf16[3,4,16,256]{3,2,1,0:T(8,128)(2,1)S(1)}, bf16[3,4,16,256]{3,2,1,0:T(8,128)(2,1)S(1)}, u32[]{:S(2)}, u32[]{:S(2)}) collective-permute-start(bf16[3,4,16,256]{3,2,1,0:T(8,128)(2,1)S(1)} %collective-permute-done.4.h3), channel_id=1, source_target_pairs={{0,1},{1,0},{2,3},{3,2},{4,5},{5,4},{6,7},{7,6},{8,9},{9,8},{10,11... | collective-permute-start | bytes 294920 | tf_op jit(solution)/shard_map/ppermute | solution.py:348
  23.2 10.2 %copy-start = (f32[1,2,2,8,256]{4,3,2,1,0:T(8,128)S(1)}, f32[1,2,2,8,256]{4,3,2,1,0:T(8,128)}, u32[]{:S(2)}) copy-start(f32[1,2,2,8,256]{4,3,2,1,0:T(8,128)} %p_ref.5) | copy-start | bytes 98308
  23.2 19.2 %copy-start.1 = (f32[1,2,2,8,256]{4,3,2,1,0:T(8,128)S(1)}, f32[1,2,2,8,256]{4,3,2,1,0:T(8,128)}, u32[]{:S(2)}) copy-start(f32[1,2,2,8,256]{4,3,2,1,0:T(8,128)} %r_ref.3) | copy-start | bytes 98308
  23.2 43.3 %copy-start.2 = (f32[1,2,2,8,256]{4,3,2,1,0:T(8,128)S(1)}, f32[1,2,2,8,256]{4,3,2,1,0:T(8,128)}, u32[]{:S(2)}) copy-start(f32[1,2,2,8,256]{4,3,2,1,0:T(8,128)} %x_ref.1) | copy-start | bytes 98308
  29.4 13.0 %all-to-all-start.1 = ((bf16[32,16,256]{2,1,0:T(8,128)(2,1)}), bf16[32,16,256]{2,1,0:T(8,128)(2,1)S(1)}, u32[]{:S(2)}, u32[]{:S(2)}) async-start(bf16[32,16,256]{2,1,0:T(8,128)(2,1)} %normal.1), calls=%async_computation.1 | async-start | bytes 524288 | tf_op jit(solution)/shard_map/all_to_all | solution.py:377
  33.4 7.1 %collective-permute-start.6 = (bf16[1,2,2,8,256]{4,3,2,1,0:T(8,128)(2,1)S(1)}, bf16[1,2,2,8,256]{4,3,2,1,0:T(8,128)(2,1)S(1)}, u32[]{:S(2)}, u32[]{:S(2)}) collective-permute-start(bf16[1,2,2,8,256]{4,3,2,1,0:T(8,128)(2,1)S(1)} %convert_element_type.3), channel_id=1, source_target_pairs={{0,32},{32,64},{64,96},{96,128},{128,160},{160,192},{192,224},{224... | collective-permute-start | bytes 49160 | tf_op jit(solution)/shard_map/ppermute | solution.py:313
  35.1 5.4 %collective-permute-start.7 = (bf16[1,2,2,8,256]{4,3,2,1,0:T(8,128)(2,1)S(1)}, bf16[1,2,2,8,256]{4,3,2,1,0:T(8,128)(2,1)S(1)}, u32[]{:S(2)}, u32[]{:S(2)}) collective-permute-start(bf16[1,2,2,8,256]{4,3,2,1,0:T(8,128)(2,1)S(1)} %convert_element_type.3), channel_id=1, source_target_pairs={{0,224},{32,0},{64,32},{96,64},{128,96},{160,128},{192,160},{224,1... | collective-permute-start | bytes 49160 | tf_op jit(solution)/shard_map/ppermute | solution.py:314

commit v5 on v4

--- a/solution.py
+++ b/solution.py
@@ -94,14 +94,17 @@
 
 
 def tables_kernel(
-    bands_in, kb_in, freq_in, g_ref, ft, gx_ref, elapsed_ref, quarter_ref, e, bands_ref, kb_ref, freq_ref, sem
+    bands_in, kb_in, freq_in, sens_in, g_ref, ft, gx_ref, elapsed_ref, quarter_ref, mine_ref, e, bands_ref, kb_ref, freq_ref, sem
 ):
     loads = [
         pltpu.make_async_copy(source, target, sem.at[i])
         for i, (source, target) in enumerate([(bands_in, bands_ref), (kb_in, kb_ref), (freq_in, freq_ref)])
     ]
+    y = lax.axis_index("segments")
+    fetch = pltpu.make_async_copy(sens_in.at[y // 2, lax.rem(y, 2)], mine_ref, sem.at[3])
     for load in loads:
         load.start()
+    fetch.start()
     rows = lax.broadcasted_iota(jnp.int32, (NX, NX), 0)
     cols = lax.broadcasted_iota(jnp.int32, (NX, NX), 1)
     re, im = unit_parts(rows * cols)
@@ -137,6 +140,7 @@
         pick = jnp.where(image_row == yr_row, F32(1), F32(0)).astype(BF16)
         g_ref[slot, :, :KR] = mm(e[0], pick).astype(BF16)
         g_ref[slot, :, KR:] = mm(e[1], pick).astype(BF16)
+    fetch.wait()
 
 
 def mm(a, b):
@@ -144,8 +148,8 @@
 
 
 def normal_kernel(
-    bands_in, count_in, p_ref, g, ft, gx_ref, h1, o1, h2, o2, h3, o3, sens_in, w_in, turn_in, out,
-    coil, blk, first, ks, acc, mine, near, gx, turn, out_ref, bands_ref, count_ref, sem, out_sem,
+    bands_in, count_in, p_ref, g, ft, gx_ref, h1, o1, h2, o2, h3, o3, mine, w_in, turn_in, out,
+    coil, blk, first, ks, acc, near, gx, turn, out_ref, bands_ref, count_ref, sem, out_sem,
 ):
     y = lax.axis_index("segments")
     plane = lax.rem(y, 2)
@@ -154,12 +158,11 @@
         pltpu.make_async_copy(source, target, sem.at[i])
         for i, (source, target) in enumerate(
             [
-                (sens_in.at[y // 2, plane], mine),
                 (w_in.at[:, pl.ds(core * HALF, HALF), plane], near.at[0]),
                 (w_in.at[:, pl.ds((1 - core) * HALF, HALF), plane], near.at[1]),
                 (bands_in, bands_ref),
                 (count_in, count_ref),
-                (turn_in, turn),
+                *((turn_in.at[i : i + 2], turn.at[i : i + 2]) for i in range(0, NSEG, 2)),
             ]
         )
     ]
@@ -182,7 +185,6 @@
         return w.astype(F32) * live, at
 
     acc[...] = jnp.zeros_like(acc)
-    loads[0].wait()
     for chunk in range(4):
         rows = slice(chunk * 64, chunk * 64 + 64)
         p = p_ref[chunk * 8 : chunk * 8 + 8].astype(jnp.int32).astype(F32) * F32(1.0 / CODE)
@@ -192,7 +194,7 @@
         sim = mine[1, rows].astype(F32)
         coil[0, rows] = sre * pre - sim * pim
         coil[1, rows] = sre * pim + sim * pre
-    for load in loads[1:5]:
+    for load in loads[:4]:
         load.wait()
     for slot in range(NSEG):
         for t in range(OT):
@@ -202,7 +204,8 @@
         got = mm(g[slot], blk[slot]).astype(BF16)
         first[slot * KR : (slot + 1) * KR, :NX] = got[:KR]
         first[slot * KR : (slot + 1) * KR, NX:] = got[KR:]
-    loads[5].wait()
+    for load in loads[4:]:
+        load.wait()
     for pair in range(NSEG // 2):
         spec = mm(first[pair * 2 * KR : (pair + 1) * 2 * KR], gx[0])
         tre, tim = 0.0, 0.0
@@ -213,23 +216,39 @@
             tim = tim + (im * c - re * s)
         ks[0] = tre if pair == 0 else ks[0] + tre
         ks[1] = tim if pair == 0 else ks[1] + tim
-    for pair in range(NSEG // 2):
+    def demod(pair):
+        re, im = ks[0], ks[1]
         for half in range(2):
-            re, im = ks[0], ks[1]
             c, s = turn[pair * 2 + half, 0], turn[pair * 2 + half, 1]
             here = slice((pair * 2 + half) * KR, (pair * 2 + half + 1) * KR)
             first[here, :NX] = (re * c - im * s).astype(BF16)
             first[here, NX:] = (im * c + re * s).astype(BF16)
+
+    def back_mm(pair):
         back = mm(first[pair * 2 * KR : (pair + 1) * 2 * KR], gx[1]).astype(BF16)
+        for half in range(2):
+            blk[pair * 2 + half, :KR] = back[half * KR : (half + 1) * KR, :NX]
+            blk[pair * 2 + half, KR:] = back[half * KR : (half + 1) * KR, NX:]
+
+    def gather(pair):
         for half in range(2):
             slot = pair * 2 + half
             places = [weight(slot, t) for t in range(OT)]
             rows = jnp.concatenate([ft[c, at] for c in range(2) for _, at in places], axis=0)
-            mid = back[half * KR : (half + 1) * KR]
-            band = mm(rows, jnp.concatenate([mid[:, :NX], mid[:, NX:]], axis=0))
+            band = mm(rows, blk[slot])
             for t, (w, at) in enumerate(places):
                 acc[0, at] += band[t * BR : (t + 1) * BR] * w
                 acc[1, at] += band[KR + t * BR : KR + (t + 1) * BR] * w
+
+    pairs = NSEG // 2
+    demod(0)
+    for pair in range(pairs + 1):
+        if pair < pairs:
+            back_mm(pair)
+        if pair + 1 < pairs:
+            demod(pair + 1)
+        if pair:
+            gather(pair - 1)
     saves = []
     for chunk in range(4):
         rows = slice(chunk * 64, chunk * 64 + 64)
@@ -313,28 +332,29 @@
     low = lax.ppermute(halo, "frames", [(i, (i + 1) % 8) for i in range(8)])
     high = lax.ppermute(halo, "frames", [(i, (i + 7) % 8) for i in range(8)])
     bands = hbm(band_ids.T)
-    g, ft, gx, elapsed, quarter = pl.pallas_call(
+    g, ft, gx, elapsed, quarter, mine = pl.pallas_call(
         tables_kernel,
-        in_specs=[HB] * 3,
-        out_specs=[VM] * 5,
+        in_specs=[HB] * 4,
+        out_specs=[VM] * 6,
         out_shape=[
             jax.ShapeDtypeStruct((NSEG, 2 * KR, 2 * KR), BF16),
             jax.ShapeDtypeStruct((2, NY, 2 * KR), BF16),
             jax.ShapeDtypeStruct((2, NX, NX), BF16),
             jax.ShapeDtypeStruct((KR, NX), F32),
             jax.ShapeDtypeStruct((NSEG, 1, NX), F32),
+            jax.ShapeDtypeStruct((2, NY, NX), BF16),
         ],
         scratch_shapes=[
             pltpu.VMEM((2, 2 * KR, NY), BF16),
             pltpu.SMEM((OT, NSEG), jnp.int32),
             pltpu.SMEM((1, KR // KB), jnp.int32),
             pltpu.SMEM((NSEG,), F32),
-            pltpu.SemaphoreType.DMA((3,)),
+            pltpu.SemaphoreType.DMA((4,)),
         ],
         compiler_params=pltpu.CompilerParams(vmem_limit_bytes=32 << 20),
         cost_estimate=pl.CostEstimate(flops=1_000_000_000, bytes_accessed=2 << 20, transcendentals=0),
         name="tables",
-    )(bands, hbm(k_bands), hbm(seg_freq))
+    )(bands, hbm(k_bands), hbm(seg_freq), hbm(sens))
     turn = pl.pallas_call(
         turns_kernel,
         in_specs=[VM, VM] + [pl.BlockSpec(memory_space=pl.ANY)] * 3,
@@ -348,7 +368,7 @@
     others = [lax.ppermute(half, "coils", [(i, i ^ 1) for i in range(8)]) for half in halves]
     parts = pl.pallas_call(
         normal_kernel,
-        in_specs=[HB] * 2 + [VM] * 10 + [HB] * 3,
+        in_specs=[HB] * 2 + [VM] * 11 + [HB] * 2,
         out_specs=HB,
         out_shape=pltpu.HBM((GROUP, 2 * ROWS, NX), BF16),
         scratch_shapes=[
@@ -357,14 +377,13 @@
             pltpu.VMEM((NSEG * KR, 2 * NX), BF16),
             pltpu.VMEM((2, KR, NX), F32),
             pltpu.VMEM((2, NY, NX), F32),
-            pltpu.VMEM((2, NY, NX), BF16),
             pltpu.VMEM((2, SEGS_DEV, HALF, BR, NX), BF16),
             pltpu.VMEM((2, 2 * NX, 2 * NX), BF16),
             pltpu.VMEM((NSEG, 2, KR, NX), F32),
             pltpu.VMEM((GROUP, 2 * ROWS, NX), BF16),
             pltpu.SMEM((OT, NSEG), jnp.int32),
             pltpu.SMEM((NSEG,), jnp.int32),
-            pltpu.SemaphoreType.DMA((6,)),
+            pltpu.SemaphoreType.DMA((10,)),
             pltpu.SemaphoreType.DMA((4,)),
         ],
         compiler_params=pltpu.CompilerParams(vmem_limit_bytes=32 << 20),
@@ -372,7 +391,7 @@
         name="normal",
     )(
         bands, hbm(seg_count), whole, g, ft, gx,
-        halves[0], others[0], halves[1], others[1], halves[2], others[2], hbm(sens), hbm(seg_weights), hbm(turn),
+        halves[0], others[0], halves[1], others[1], halves[2], others[2], mine, hbm(seg_weights), hbm(turn),
     )
     parts = lax.all_to_all(parts, SPACE, 0, 0, tiled=True)
     share = jax.ShapeDtypeStruct(p_in.shape, F32)

time: 67.7 us -> 66.9 us (0.988)
  Pallas kernels: 13.4 us -> 12.7 us
    pallas_call x2, Pallas kernels: 8.41 us -> 7.67 us  [the longest x1 5.47 us: local(): pl.pallas_call(normal_kernel, in_specs=[HB] * 2 + [VM] * 11 + [HB] * 2, o...]
where the time goes in v5:
time: 66.9 us; the launch traced here: 66.6 us
  blocking collectives  24.2 us (36%)
  starting transfers between devices  22.5 us (34%)
  Pallas kernels  12.7 us (19%)
  waiting for transfers between devices  6.48 us (10%)
  between operations  0.73 us (1%)
    all_to_all x1, blocking collectives, local(): lax.all_to_all(sums, ('frames', 'segments', 'coils'), 0, 0, tiled=True)  24.2 us
    all_to_all x1, starting transfers between devices, local(): whole = lax.all_to_all(send, SPACE, 0, 0, tiled=True)  6.08 us
    ppermute x3, starting transfers between devices, local(): lax.ppermute(same if k == 2 else other, 'segments', [(i, (i + k) % 4) for...  5.81 us
    pallas_call x1, Pallas kernels, local(): pl.pallas_call(normal_kernel, in_specs=[HB] * 2 + [VM] * 11 + [HB] * 2, o...  5.47 us
    ppermute x1, starting transfers between devices, local(): high = lax.ppermute(halo, 'frames', [(i, (i + 7) % 8) for i in range(8)])  4.03 us
    all_to_all x1, starting transfers between devices, local(): parts = lax.all_to_all(parts, SPACE, 0, 0, tiled=True)  3.87 us
    all_to_all x1, waiting for transfers between devices, local(): whole = lax.all_to_all(send, SPACE, 0, 0, tiled=True)  3.51 us
    pallas_call x1, Pallas kernels, local(): pl.pallas_call(turns_kernel, in_specs=[VM, VM] + [pl.BlockSpec(memory_spa...  2.29 us
  transfers between devices with their start and end apart: 10, of which 3 were waited for; matrix products, arithmetic and copies ran while one was open for 0% of the time, Pallas kernels for 7%

profile of v5, /device:TPU:1, one launch (start us, length us, event | category | flops | bytes accessed | tf_op | source)
XLA Modules:
  0.0 66.6 jit_solution(14426711396112231131)
XLA Ops:
  0.6 1.8 %prep.1 = (s16[32,16,256]{2,1,0:T(8,128)(2,1)}, bf16[3,4,16,256]{3,2,1,0:T(8,128)(2,1)S(1)}, bf16[3,4,16,256]{3,2,1,0:T(8,128)(2,1)S(1)}) custom-call(f32[1,2,2,8,256]{4,3,2,1,0:T(8,128)} %p_ref.5, bf16[3,8,2,16,256]{4,3,2,1,0:T(8,128)(2,1)} %w_in.1), custom_call_target="tpu_custom_call" | custom-call | tf_op jit(solution)/shard_map/prep/pallas_call | solution.py:318
  2.4 2.1 %collective-permute-start = (bf16[3,4,16,256]{3,2,1,0:T(8,128)(2,1)S(1)}, bf16[3,4,16,256]{3,2,1,0:T(8,128)(2,1)S(1)}, u32[]{:S(2)}, u32[]{:S(2)}) collective-permute-start(bf16[3,4,16,256]{3,2,1,0:T(8,128)(2,1)S(1)} %get-tuple-element.18), channel_id=1, source_target_pairs={{0,8},{8,16},{16,24},{24,0},{1,9},{9,17},{17,25},{25,1},{2,10},{10... | collective-permute-start | bytes 294920 | tf_op jit(solution)/shard_map/ppermute | solution.py:327
  4.5 2.6 %collective-permute-start.2 = (bf16[3,4,16,256]{3,2,1,0:T(8,128)(2,1)S(1)}, bf16[3,4,16,256]{3,2,1,0:T(8,128)(2,1)S(1)}, u32[]{:S(2)}, u32[]{:S(2)}) collective-permute-start(bf16[3,4,16,256]{3,2,1,0:T(8,128)(2,1)S(1)} %get-tuple-element.19), channel_id=1, source_target_pairs={{0,16},{8,24},{16,0},{24,8},{1,17},{9,25},{17,1},{25,9},{2,18},{10... | collective-permute-start | bytes 294920 | tf_op jit(solution)/shard_map/ppermute | solution.py:327
  7.1 1.1 %collective-permute-start.4 = (bf16[3,4,16,256]{3,2,1,0:T(8,128)(2,1)S(1)}, bf16[3,4,16,256]{3,2,1,0:T(8,128)(2,1)S(1)}, u32[]{:S(2)}, u32[]{:S(2)}) collective-permute-start(bf16[3,4,16,256]{3,2,1,0:T(8,128)(2,1)S(1)} %get-tuple-element.18), channel_id=1, source_target_pairs={{0,24},{8,0},{16,8},{24,16},{1,25},{9,1},{17,9},{25,17},{2,26},{10... | collective-permute-start | bytes 294920 | tf_op jit(solution)/shard_map/ppermute | solution.py:327
  8.2 6.1 %all-to-all-start = ((s16[32,16,256]{2,1,0:T(8,128)(2,1)}), s16[32,16,256]{2,1,0:T(8,128)(2,1)S(1)}, u32[]{:S(2)}, u32[]{:S(2)}) async-start(s16[32,16,256]{2,1,0:T(8,128)(2,1)} %get-tuple-element.14), calls=%async_computation | async-start | bytes 524288 | tf_op jit(solution)/shard_map/all_to_all | solution.py:330
  14.3 2.2 %tables.1 = (bf16[12,256,256]{2,1,0:T(8,128)(2,1)S(1)}, bf16[2,256,256]{2,1,0:T(8,128)(2,1)S(1)}, bf16[2,256,256]{2,1,0:T(8,128)(2,1)S(1)}, f32[128,256]{1,0:T(8...) custom-call(s32[8,12]{1,0:T(8,128)} %bitcast.7, s32[1,16]{1,0:T(1,128)} %kb_in.1, f32[12]{0:T(128)} %freq_in.1, ...), custom_call_target="tpu_custom_call" | custom-call | flops 1000000000 | bytes 2097152 | tf_op jit(solution)/shard_map/tables/pallas_call | solution.py:335
  16.5 0.0 collective-permute-done.h1
  16.5 0.3 collective-permute-start.1
  16.8 0.0 collective-permute-done.2.h2
  16.8 0.3 collective-permute-start.3
  17.1 0.2 collective-permute-start.5
  17.4 2.3 %turns.1.turn_in = f32[12,2,128,256]{3,2,1,0:T(8,128)} custom-call(f32[128,256]{1,0:T(8,128)S(1)} %get-tuple-element.21.elapsed_ref, f32[12,1,256]{2,1,0:T(1,128)S(1)} %get-tuple-element.22.freq_ref, bf16[3,4,16,256]{3,2,1,0:T(8,128)(2,1)S(1)} %collective-permute-done.h1, bf16[3,4,16,256]{3,2,1,0:T(8,128)(2,1)S(1)} %collective-permute-done.2.h2, ...), custom_call_target="tpu_custom_call" | custom-call | flops 40000000000 | bytes 3145728 | tf_op jit(solution)/shard_map/turns/pallas_call | solution.py:358
  19.7 0.0 collective-permute-done.3.o2
  19.7 3.5 %all-to-all-done.p_ref = s16[32,16,256]{2,1,0:T(8,128)(2,1)S(1)} async-done(((s16[32,16,256]{2,1,0:T(8,128)(2,1)}), s16[32,16,256]{2,1,0:T(8,128)(2,1)S(1)}, u32[]{:S(2)}, u32[]{:S(2)}) %all-to-all-start) | async-done | bytes 262176 | tf_op jit(solution)/shard_map/all_to_all | solution.py:330
  23.2 5.5 %normal.1 = bf16[32,16,256]{2,1,0:T(8,128)(2,1)} custom-call(s32[8,12]{1,0:T(8,128)} %bitcast.8, s32[12]{0:T(128)} %count_in.1, s16[32,16,256]{2,1,0:T(8,128)(2,1)S(1)} %all-to-all-done.p_ref, bf16[12,256,256]{2,1,0:T(8,128)(2,1)S(1)} %get-tuple-element.15.g, bf16[2,256,256]{2,1,0:T(8,128)(2,1)S(1)} %get-tuple-element.16.ft, ...), custom_call_target="tpu_custom_call" | custom-call | flops 2400000000 | bytes 8388608 | tf_op jit(solution)/shard_map/normal/pallas_call | solution.py:369
  28.7 3.9 %all-to-all-start.1 = ((bf16[32,16,256]{2,1,0:T(8,128)(2,1)}), bf16[32,16,256]{2,1,0:T(8,128)(2,1)S(1)}, u32[]{:S(2)}, u32[]{:S(2)}) async-start(bf16[32,16,256]{2,1,0:T(8,128)(2,1)} %normal.1), calls=%async_computation.1 | async-start | bytes 524288 | tf_op jit(solution)/shard_map/all_to_all | solution.py:396
  32.6 1.9 %collective-permute-start.6 = (bf16[1,2,2,8,256]{4,3,2,1,0:T(8,128)(2,1)S(1)}, bf16[1,2,2,8,256]{4,3,2,1,0:T(8,128)(2,1)S(1)}, u32[]{:S(2)}, u32[]{:S(2)}) collective-permute-start(bf16[1,2,2,8,256]{4,3,2,1,0:T(8,128)(2,1)S(1)} %convert_element_type.3), channel_id=1, source_target_pairs={{0,32},{32,64},{64,96},{96,128},{128,160},{160,192},{192,224},{224... | collective-permute-start | bytes 49160 | tf_op jit(solution)/shard_map/ppermute | solution.py:332
  34.5 4.0 %collective-permute-start.7 = (bf16[1,2,2,8,256]{4,3,2,1,0:T(8,128)(2,1)S(1)}, bf16[1,2,2,8,256]{4,3,2,1,0:T(8,128)(2,1)S(1)}, u32[]{:S(2)}, u32[]{:S(2)}) collective-permute-start(bf16[1,2,2,8,256]{4,3,2,1,0:T(8,128)(2,1)S(1)} %convert_element_type.3), channel_id=1, source_target_pairs={{0,224},{32,0},{64,32},{96,64},{128,96},{160,128},{192,160},{224,1... | collective-permute-start | bytes 49160 | tf_op jit(solution)/shard_map/ppermute | solution.py:333
  38.5 1.3 %collective-permute-done.6.low_ref = bf16[1,2,2,8,256]{4,3,2,1,0:T(8,128)(2,1)S(1)} collective-permute-done((bf16[1,2,2,8,256]{4,3,2,1,0:T(8,128)(2,1)S(1)}, bf16[1,2,2,8,256]{4,3,2,1,0:T(8,128)(2,1)S(1)}, u32[]{:S(2)}, u32[]{:S(2)}) %collective-permute-start.6) | collective-permute-done | bytes 16416 | tf_op jit(solution)/shard_map/ppermute | solution.py:332
  39.8 0.0 collective-permute-done.7.high_ref
  39.9 1.6 %all-to-all-done.1.parts_ref = bf16[32,16,256]{2,1,0:T(8,128)(2,1)S(1)} async-done(((bf16[32,16,256]{2,1,0:T(8,128)(2,1)}), bf16[32,16,256]{2,1,0:T(8,128)(2,1)S(1)}, u32[]{:S(2)}, u32[]{:S(2)}) %all-to-all-start.1) | async-done | bytes 262176 | tf_op jit(solution)/shard_map/all_to_all | solution.py:396
  41.5 0.1 applied.1
  41.6 24.2 %all_to_all.21 = f32[256,1,8]{2,1,0:T(1,128)S(1)} all-to-all(f32[256,1,8]{2,1,0:T(1,128)S(1)} %bitcast.6), channel_id=1, replica_groups=mesh['frames'=8,'segments'=4,'coils'=8] {'frames','segments','coils'}, dimensions={0} | all-to-all | bytes 16384 | tf_op jit(solution)/shard_map/all_to_all | solution.py:406
  65.8 0.8 %update.1 = (f32[1,2,2,8,256]{4,3,2,1,0:T(8,128)}, f32[1,2,2,8,256]{4,3,2,1,0:T(8,128)}, f32[1,2,2,8,256]{4,3,2,1,0:T(8,128)}) custom-call(f32[256,8]{1,0:T(8,128)S(1)} %bitcast.5, f32[1,2,2,8,256]{4,3,2,1,0:T(8,128)S(1)} %copy-done.2, f32[1,2,2,8,256]{4,3,2,1,0:T(8,128)S(1)} %copy-done.1, f32[1,2,2,8,256]{4,3,2,1,0:T(8,128)S(1)} %copy-done, ...), custom_call_target="tpu_custom_call" | custom-call | tf_op jit(solution)/shard_map/update/pallas_call | solution.py:408
  (10 shorter events, 0.0 us)
Async XLA Ops:
  2.4 14.1 %collective-permute-start = (bf16[3,4,16,256]{3,2,1,0:T(8,128)(2,1)S(1)}, bf16[3,4,16,256]{3,2,1,0:T(8,128)(2,1)S(1)}, u32[]{:S(2)}, u32[]{:S(2)}) collective-permute-start(bf16[3,4,16,256]{3,2,1,0:T(8,128)(2,1)S(1)} %get-tuple-element.18), channel_id=1, source_target_pairs={{0,8},{8,16},{16,24},{24,0},{1,9},{9,17},{17,25},{25,1},{2,10},{10... | collective-permute-start | bytes 294920 | tf_op jit(solution)/shard_map/ppermute | solution.py:327
  4.5 12.3 %collective-permute-start.2 = (bf16[3,4,16,256]{3,2,1,0:T(8,128)(2,1)S(1)}, bf16[3,4,16,256]{3,2,1,0:T(8,128)(2,1)S(1)}, u32[]{:S(2)}, u32[]{:S(2)}) collective-permute-start(bf16[3,4,16,256]{3,2,1,0:T(8,128)(2,1)S(1)} %get-tuple-element.19), channel_id=1, source_target_pairs={{0,16},{8,24},{16,0},{24,8},{1,17},{9,25},{17,1},{25,9},{2,18},{10... | collective-permute-start | bytes 294920 | tf_op jit(solution)/shard_map/ppermute | solution.py:327
  7.1 10.0 %collective-permute-start.4 = (bf16[3,4,16,256]{3,2,1,0:T(8,128)(2,1)S(1)}, bf16[3,4,16,256]{3,2,1,0:T(8,128)(2,1)S(1)}, u32[]{:S(2)}, u32[]{:S(2)}) collective-permute-start(bf16[3,4,16,256]{3,2,1,0:T(8,128)(2,1)S(1)} %get-tuple-element.18), channel_id=1, source_target_pairs={{0,24},{8,0},{16,8},{24,16},{1,25},{9,1},{17,9},{25,17},{2,26},{10... | collective-permute-start | bytes 294920 | tf_op jit(solution)/shard_map/ppermute | solution.py:327
  8.2 15.0 %all-to-all-start = ((s16[32,16,256]{2,1,0:T(8,128)(2,1)}), s16[32,16,256]{2,1,0:T(8,128)(2,1)S(1)}, u32[]{:S(2)}, u32[]{:S(2)}) async-start(s16[32,16,256]{2,1,0:T(8,128)(2,1)} %get-tuple-element.14), calls=%async_computation | async-start | bytes 524288 | tf_op jit(solution)/shard_map/all_to_all | solution.py:330
  16.5 3.1 %collective-permute-start.1 = (bf16[3,4,16,256]{3,2,1,0:T(8,128)(2,1)S(1)}, bf16[3,4,16,256]{3,2,1,0:T(8,128)(2,1)S(1)}, u32[]{:S(2)}, u32[]{:S(2)}) collective-permute-start(bf16[3,4,16,256]{3,2,1,0:T(8,128)(2,1)S(1)} %collective-permute-done.h1), channel_id=1, source_target_pairs={{0,1},{1,0},{2,3},{3,2},{4,5},{5,4},{6,7},{7,6},{8,9},{9,8},{10,11... | collective-permute-start | bytes 294920 | tf_op jit(solution)/shard_map/ppermute | solution.py:368
  16.8 2.8 %collective-permute-start.3 = (bf16[3,4,16,256]{3,2,1,0:T(8,128)(2,1)S(1)}, bf16[3,4,16,256]{3,2,1,0:T(8,128)(2,1)S(1)}, u32[]{:S(2)}, u32[]{:S(2)}) collective-permute-start(bf16[3,4,16,256]{3,2,1,0:T(8,128)(2,1)S(1)} %collective-permute-done.2.h2), channel_id=1, source_target_pairs={{0,1},{1,0},{2,3},{3,2},{4,5},{5,4},{6,7},{7,6},{8,9},{9,8},{10,11... | collective-permute-start | bytes 294920 | tf_op jit(solution)/shard_map/ppermute | solution.py:368
  17.1 2.6 %collective-permute-start.5 = (bf16[3,4,16,256]{3,2,1,0:T(8,128)(2,1)S(1)}, bf16[3,4,16,256]{3,2,1,0:T(8,128)(2,1)S(1)}, u32[]{:S(2)}, u32[]{:S(2)}) collective-permute-start(bf16[3,4,16,256]{3,2,1,0:T(8,128)(2,1)S(1)} %collective-permute-done.4.h3), channel_id=1, source_target_pairs={{0,1},{1,0},{2,3},{3,2},{4,5},{5,4},{6,7},{7,6},{8,9},{9,8},{10,11... | collective-permute-start | bytes 294920 | tf_op jit(solution)/shard_map/ppermute | solution.py:368
  23.2 9.4 %copy-start = (f32[1,2,2,8,256]{4,3,2,1,0:T(8,128)S(1)}, f32[1,2,2,8,256]{4,3,2,1,0:T(8,128)}, u32[]{:S(2)}) copy-start(f32[1,2,2,8,256]{4,3,2,1,0:T(8,128)} %p_ref.5) | copy-start | bytes 98308
  23.2 18.3 %copy-start.1 = (f32[1,2,2,8,256]{4,3,2,1,0:T(8,128)S(1)}, f32[1,2,2,8,256]{4,3,2,1,0:T(8,128)}, u32[]{:S(2)}) copy-start(f32[1,2,2,8,256]{4,3,2,1,0:T(8,128)} %r_ref.3) | copy-start | bytes 98308
  23.2 42.6 %copy-start.2 = (f32[1,2,2,8,256]{4,3,2,1,0:T(8,128)S(1)}, f32[1,2,2,8,256]{4,3,2,1,0:T(8,128)}, u32[]{:S(2)}) copy-start(f32[1,2,2,8,256]{4,3,2,1,0:T(8,128)} %x_ref.1) | copy-start | bytes 98308
  28.7 12.8 %all-to-all-start.1 = ((bf16[32,16,256]{2,1,0:T(8,128)(2,1)}), bf16[32,16,256]{2,1,0:T(8,128)(2,1)S(1)}, u32[]{:S(2)}, u32[]{:S(2)}) async-start(bf16[32,16,256]{2,1,0:T(8,128)(2,1)} %normal.1), calls=%async_computation.1 | async-start | bytes 524288 | tf_op jit(solution)/shard_map/all_to_all | solution.py:396
  32.6 7.3 %collective-permute-start.6 = (bf16[1,2,2,8,256]{4,3,2,1,0:T(8,128)(2,1)S(1)}, bf16[1,2,2,8,256]{4,3,2,1,0:T(8,128)(2,1)S(1)}, u32[]{:S(2)}, u32[]{:S(2)}) collective-permute-start(bf16[1,2,2,8,256]{4,3,2,1,0:T(8,128)(2,1)S(1)} %convert_element_type.3), channel_id=1, source_target_pairs={{0,32},{32,64},{64,96},{96,128},{128,160},{160,192},{192,224},{224... | collective-permute-start | bytes 49160 | tf_op jit(solution)/shard_map/ppermute | solution.py:332
  34.5 5.4 %collective-permute-start.7 = (bf16[1,2,2,8,256]{4,3,2,1,0:T(8,128)(2,1)S(1)}, bf16[1,2,2,8,256]{4,3,2,1,0:T(8,128)(2,1)S(1)}, u32[]{:S(2)}, u32[]{:S(2)}) collective-permute-start(bf16[1,2,2,8,256]{4,3,2,1,0:T(8,128)(2,1)S(1)} %convert_element_type.3), channel_id=1, source_target_pairs={{0,224},{32,0},{64,32},{96,64},{128,96},{160,128},{192,160},{224,1... | collective-permute-start | bytes 49160 | tf_op jit(solution)/shard_map/ppermute | solution.py:333

commit v6 on v5

--- a/solution.py
+++ b/solution.py
@@ -69,19 +69,31 @@
     return out
 
 
-def prep_kernel(p_ref, w_ref, send_ref, same_ref, other_ref):
+def prep_kernel(p_in, w_in, send_out, same_ref, other_ref, p_ref, w_ref, code, sem, send_sem):
     plane = lax.rem(lax.axis_index("segments"), 2)
     core = lax.rem(lax.axis_index("coils"), 2)
+    load_p = pltpu.make_async_copy(p_in, p_ref, sem.at[0])
+    load_w = pltpu.make_async_copy(w_in.at[:, pl.ds(core * HALF, HALF)], w_ref, sem.at[1])
+    load_p.start()
+    load_w.start()
+    load_p.wait()
+    saves = []
+    for q in range(2):
+        both = jnp.concatenate([p_ref[0, q, 0], p_ref[0, q, 1]], axis=0)
+        value = jnp.floor(both * F32(CODE) + 0.5).astype(jnp.int32).astype(jnp.int16)
+        for xc in range(8):
+            code[q, xc] = value
+        for pair in range(2):
+            target = send_out.at[pl.ds((pair * 2 + q) * 8, 8)]
+            saves.append(pltpu.make_async_copy(code.at[q], target, send_sem.at[pair * 2 + q]))
+            saves[-1].start()
+    load_w.wait()
     for i in range(SEGS_DEV):
         for t in range(HALF):
-            same_ref[i, t] = w_ref[i, core * HALF + t, plane]
-            other_ref[i, t] = w_ref[i, core * HALF + t, 1 - plane]
-    for q in range(2):
-        both = jnp.concatenate([p_ref[0, q, 0], p_ref[0, q, 1]], axis=0)
-        code = jnp.floor(both * F32(CODE) + 0.5).astype(jnp.int32).astype(jnp.int16)
-        for pair in range(2):
-            for xc in range(8):
-                send_ref[(pair * 2 + q) * 8 + xc] = code
+            same_ref[i, t] = w_ref[i, t, plane]
+            other_ref[i, t] = w_ref[i, t, 1 - plane]
+    for save in saves:
+        save.wait()
 
 
 def turns_kernel(elapsed_ref, freq_ref, h1, h2, h3, turn_out, turn, turn_sem):
@@ -317,9 +329,16 @@
     half_shape = jax.ShapeDtypeStruct((SEGS_DEV, HALF, BR, NX), BF16)
     send, same, other = pl.pallas_call(
         prep_kernel,
-        in_specs=[VM, VM],
-        out_specs=[VM, VM, VM],
-        out_shape=[jax.ShapeDtypeStruct((GROUP, 2 * ROWS, NX), jnp.int16), half_shape, half_shape],
+        in_specs=[HB, HB],
+        out_specs=[HB, VM, VM],
+        out_shape=[pltpu.HBM((GROUP, 2 * ROWS, NX), jnp.int16), half_shape, half_shape],
+        scratch_shapes=[
+            pltpu.VMEM((1, 2, 2, ROWS, NX), F32),
+            pltpu.VMEM((SEGS_DEV, HALF, 2, BR, NX), BF16),
+            pltpu.VMEM((2, 8, 2 * ROWS, NX), jnp.int16),
+            pltpu.SemaphoreType.DMA((2,)),
+            pltpu.SemaphoreType.DMA((4,)),
+        ],
         compiler_params=pltpu.CompilerParams(vmem_limit_bytes=4 << 20),
         name="prep",
     )(hbm(p_in), hbm(seg_weights))

time: 66.9 us -> 66.8 us (level)
  no operation moved by 1% of the time
where the time goes in v6:
time: 66.8 us; the launch traced here: 66.4 us
  blocking collectives  24.2 us (36%)
  starting transfers between devices  22.6 us (34%)
  Pallas kernels  12.4 us (19%)
  waiting for transfers between devices  6.5 us (10%)
  between operations  0.74 us (1%)
    all_to_all x1, blocking collectives, local(): lax.all_to_all(sums, ('frames', 'segments', 'coils'), 0, 0, tiled=True)  24.2 us
    all_to_all x1, starting transfers between devices, local(): whole = lax.all_to_all(send, SPACE, 0, 0, tiled=True)  6.08 us
    ppermute x3, starting transfers between devices, local(): lax.ppermute(same if k == 2 else other, 'segments', [(i, (i + k) % 4) for...  5.89 us
    pallas_call x1, Pallas kernels, local(): pl.pallas_call(normal_kernel, in_specs=[HB] * 2 + [VM] * 11 + [HB] * 2, o...  5.47 us
    ppermute x1, starting transfers between devices, local(): high = lax.ppermute(halo, 'frames', [(i, (i + 7) % 8) for i in range(8)])  4.02 us
    all_to_all x1, starting transfers between devices, local(): parts = lax.all_to_all(parts, SPACE, 0, 0, tiled=True)  3.87 us
    all_to_all x1, waiting for transfers between devices, local(): whole = lax.all_to_all(send, SPACE, 0, 0, tiled=True)  3.51 us
    pallas_call x1, Pallas kernels, local(): pl.pallas_call(turns_kernel, in_specs=[VM, VM] + [pl.BlockSpec(memory_spa...  2.29 us
  transfers between devices with their start and end apart: 10, of which 3 were waited for; matrix products, arithmetic and copies ran while one was open for 0% of the time, Pallas kernels for 7%

profile of v6, /device:TPU:1, one launch (start us, length us, event | category | flops | bytes accessed | tf_op | source)
XLA Modules:
  0.0 66.4 jit_solution(147032264238457622)
XLA Ops:
  0.6 1.5 %prep.1 = (s16[32,16,256]{2,1,0:T(8,128)(2,1)}, bf16[3,4,16,256]{3,2,1,0:T(8,128)(2,1)S(1)}, bf16[3,4,16,256]{3,2,1,0:T(8,128)(2,1)S(1)}) custom-call(f32[1,2,2,8,256]{4,3,2,1,0:T(8,128)} %p_ref.3, bf16[3,8,2,16,256]{4,3,2,1,0:T(8,128)(2,1)} %w_in.3), custom_call_target="tpu_custom_call" | custom-call | tf_op jit(solution)/shard_map/prep/pallas_call | solution.py:330
  2.2 2.2 %collective-permute-start = (bf16[3,4,16,256]{3,2,1,0:T(8,128)(2,1)S(1)}, bf16[3,4,16,256]{3,2,1,0:T(8,128)(2,1)S(1)}, u32[]{:S(2)}, u32[]{:S(2)}) collective-permute-start(bf16[3,4,16,256]{3,2,1,0:T(8,128)(2,1)S(1)} %get-tuple-element.18), channel_id=1, source_target_pairs={{0,8},{8,16},{16,24},{24,0},{1,9},{9,17},{17,25},{25,1},{2,10},{10... | collective-permute-start | bytes 294920 | tf_op jit(solution)/shard_map/ppermute | solution.py:346
  4.4 2.6 %collective-permute-start.2 = (bf16[3,4,16,256]{3,2,1,0:T(8,128)(2,1)S(1)}, bf16[3,4,16,256]{3,2,1,0:T(8,128)(2,1)S(1)}, u32[]{:S(2)}, u32[]{:S(2)}) collective-permute-start(bf16[3,4,16,256]{3,2,1,0:T(8,128)(2,1)S(1)} %get-tuple-element.19), channel_id=1, source_target_pairs={{0,16},{8,24},{16,0},{24,8},{1,17},{9,25},{17,1},{25,9},{2,18},{10... | collective-permute-start | bytes 294920 | tf_op jit(solution)/shard_map/ppermute | solution.py:346
  7.0 1.1 %collective-permute-start.4 = (bf16[3,4,16,256]{3,2,1,0:T(8,128)(2,1)S(1)}, bf16[3,4,16,256]{3,2,1,0:T(8,128)(2,1)S(1)}, u32[]{:S(2)}, u32[]{:S(2)}) collective-permute-start(bf16[3,4,16,256]{3,2,1,0:T(8,128)(2,1)S(1)} %get-tuple-element.18), channel_id=1, source_target_pairs={{0,24},{8,0},{16,8},{24,16},{1,25},{9,1},{17,9},{25,17},{2,26},{10... | collective-permute-start | bytes 294920 | tf_op jit(solution)/shard_map/ppermute | solution.py:346
  8.1 6.1 %all-to-all-start = ((s16[32,16,256]{2,1,0:T(8,128)(2,1)}), s16[32,16,256]{2,1,0:T(8,128)(2,1)S(1)}, u32[]{:S(2)}, u32[]{:S(2)}) async-start(s16[32,16,256]{2,1,0:T(8,128)(2,1)} %get-tuple-element.14), calls=%async_computation | async-start | bytes 524288 | tf_op jit(solution)/shard_map/all_to_all | solution.py:349
  14.1 2.2 %tables.1 = (bf16[12,256,256]{2,1,0:T(8,128)(2,1)S(1)}, bf16[2,256,256]{2,1,0:T(8,128)(2,1)S(1)}, bf16[2,256,256]{2,1,0:T(8,128)(2,1)S(1)}, f32[128,256]{1,0:T(8...) custom-call(s32[8,12]{1,0:T(8,128)} %bitcast.7, s32[1,16]{1,0:T(1,128)} %kb_in.1, f32[12]{0:T(128)} %freq_in.1, ...), custom_call_target="tpu_custom_call" | custom-call | flops 1000000000 | bytes 2097152 | tf_op jit(solution)/shard_map/tables/pallas_call | solution.py:354
  16.4 0.0 collective-permute-done.h1
  16.4 0.3 collective-permute-start.1
  16.7 0.0 collective-permute-done.2.h2
  16.7 0.3 collective-permute-start.3
  17.0 0.0 collective-permute-done.4.h3
  17.0 0.2 collective-permute-start.5
  17.2 2.3 %turns.1.turn_in = f32[12,2,128,256]{3,2,1,0:T(8,128)} custom-call(f32[128,256]{1,0:T(8,128)S(1)} %get-tuple-element.21.elapsed_ref, f32[12,1,256]{2,1,0:T(1,128)S(1)} %get-tuple-element.22.freq_ref, bf16[3,4,16,256]{3,2,1,0:T(8,128)(2,1)S(1)} %collective-permute-done.h1, bf16[3,4,16,256]{3,2,1,0:T(8,128)(2,1)S(1)} %collective-permute-done.2.h2, ...), custom_call_target="tpu_custom_call" | custom-call | flops 40000000000 | bytes 3145728 | tf_op jit(solution)/shard_map/turns/pallas_call | solution.py:377
  19.5 0.0 collective-permute-done.1.o1
  19.5 3.5 %all-to-all-done.p_ref = s16[32,16,256]{2,1,0:T(8,128)(2,1)S(1)} async-done(((s16[32,16,256]{2,1,0:T(8,128)(2,1)}), s16[32,16,256]{2,1,0:T(8,128)(2,1)S(1)}, u32[]{:S(2)}, u32[]{:S(2)}) %all-to-all-start) | async-done | bytes 262176 | tf_op jit(solution)/shard_map/all_to_all | solution.py:349
  23.1 5.5 %normal.1 = bf16[32,16,256]{2,1,0:T(8,128)(2,1)} custom-call(s32[8,12]{1,0:T(8,128)} %bitcast.8, s32[12]{0:T(128)} %count_in.1, s16[32,16,256]{2,1,0:T(8,128)(2,1)S(1)} %all-to-all-done.p_ref, bf16[12,256,256]{2,1,0:T(8,128)(2,1)S(1)} %get-tuple-element.15.g, bf16[2,256,256]{2,1,0:T(8,128)(2,1)S(1)} %get-tuple-element.16.ft, ...), custom_call_target="tpu_custom_call" | custom-call | flops 2400000000 | bytes 8388608 | tf_op jit(solution)/shard_map/normal/pallas_call | solution.py:388
  28.5 3.9 %all-to-all-start.1 = ((bf16[32,16,256]{2,1,0:T(8,128)(2,1)}), bf16[32,16,256]{2,1,0:T(8,128)(2,1)S(1)}, u32[]{:S(2)}, u32[]{:S(2)}) async-start(bf16[32,16,256]{2,1,0:T(8,128)(2,1)} %normal.1), calls=%async_computation.1 | async-start | bytes 524288 | tf_op jit(solution)/shard_map/all_to_all | solution.py:415
  32.4 1.9 %collective-permute-start.6 = (bf16[1,2,2,8,256]{4,3,2,1,0:T(8,128)(2,1)S(1)}, bf16[1,2,2,8,256]{4,3,2,1,0:T(8,128)(2,1)S(1)}, u32[]{:S(2)}, u32[]{:S(2)}) collective-permute-start(bf16[1,2,2,8,256]{4,3,2,1,0:T(8,128)(2,1)S(1)} %convert_element_type.3), channel_id=1, source_target_pairs={{0,32},{32,64},{64,96},{96,128},{128,160},{160,192},{192,224},{224... | collective-permute-start | bytes 49160 | tf_op jit(solution)/shard_map/ppermute | solution.py:351
  34.3 4.0 %collective-permute-start.7 = (bf16[1,2,2,8,256]{4,3,2,1,0:T(8,128)(2,1)S(1)}, bf16[1,2,2,8,256]{4,3,2,1,0:T(8,128)(2,1)S(1)}, u32[]{:S(2)}, u32[]{:S(2)}) collective-permute-start(bf16[1,2,2,8,256]{4,3,2,1,0:T(8,128)(2,1)S(1)} %convert_element_type.3), channel_id=1, source_target_pairs={{0,224},{32,0},{64,32},{96,64},{128,96},{160,128},{192,160},{224,1... | collective-permute-start | bytes 49160 | tf_op jit(solution)/shard_map/ppermute | solution.py:352
  38.3 1.3 %collective-permute-done.6.low_ref = bf16[1,2,2,8,256]{4,3,2,1,0:T(8,128)(2,1)S(1)} collective-permute-done((bf16[1,2,2,8,256]{4,3,2,1,0:T(8,128)(2,1)S(1)}, bf16[1,2,2,8,256]{4,3,2,1,0:T(8,128)(2,1)S(1)}, u32[]{:S(2)}, u32[]{:S(2)}) %collective-permute-start.6) | collective-permute-done | bytes 16416 | tf_op jit(solution)/shard_map/ppermute | solution.py:351
  39.7 1.6 %all-to-all-done.1.parts_ref = bf16[32,16,256]{2,1,0:T(8,128)(2,1)S(1)} async-done(((bf16[32,16,256]{2,1,0:T(8,128)(2,1)}), bf16[32,16,256]{2,1,0:T(8,128)(2,1)S(1)}, u32[]{:S(2)}, u32[]{:S(2)}) %all-to-all-start.1) | async-done | bytes 262176 | tf_op jit(solution)/shard_map/all_to_all | solution.py:415
  41.3 0.1 applied.1
  41.5 24.2 %all_to_all.21 = f32[256,1,8]{2,1,0:T(1,128)S(1)} all-to-all(f32[256,1,8]{2,1,0:T(1,128)S(1)} %bitcast.6), channel_id=1, replica_groups=mesh['frames'=8,'segments'=4,'coils'=8] {'frames','segments','coils'}, dimensions={0} | all-to-all | bytes 16384 | tf_op jit(solution)/shard_map/all_to_all | solution.py:425
  65.6 0.8 %update.1 = (f32[1,2,2,8,256]{4,3,2,1,0:T(8,128)}, f32[1,2,2,8,256]{4,3,2,1,0:T(8,128)}, f32[1,2,2,8,256]{4,3,2,1,0:T(8,128)}) custom-call(f32[256,8]{1,0:T(8,128)S(1)} %bitcast.5, f32[1,2,2,8,256]{4,3,2,1,0:T(8,128)S(1)} %copy-done.2, f32[1,2,2,8,256]{4,3,2,1,0:T(8,128)S(1)} %copy-done.1, f32[1,2,2,8,256]{4,3,2,1,0:T(8,128)S(1)} %copy-done, ...), custom_call_target="tpu_custom_call" | custom-call | tf_op jit(solution)/shard_map/update/pallas_call | solution.py:427
  (10 shorter events, 0.0 us)
Async XLA Ops:
  2.2 14.2 %collective-permute-start = (bf16[3,4,16,256]{3,2,1,0:T(8,128)(2,1)S(1)}, bf16[3,4,16,256]{3,2,1,0:T(8,128)(2,1)S(1)}, u32[]{:S(2)}, u32[]{:S(2)}) collective-permute-start(bf16[3,4,16,256]{3,2,1,0:T(8,128)(2,1)S(1)} %get-tuple-element.18), channel_id=1, source_target_pairs={{0,8},{8,16},{16,24},{24,0},{1,9},{9,17},{17,25},{25,1},{2,10},{10... | collective-permute-start | bytes 294920 | tf_op jit(solution)/shard_map/ppermute | solution.py:346
  4.4 12.3 %collective-permute-start.2 = (bf16[3,4,16,256]{3,2,1,0:T(8,128)(2,1)S(1)}, bf16[3,4,16,256]{3,2,1,0:T(8,128)(2,1)S(1)}, u32[]{:S(2)}, u32[]{:S(2)}) collective-permute-start(bf16[3,4,16,256]{3,2,1,0:T(8,128)(2,1)S(1)} %get-tuple-element.19), channel_id=1, source_target_pairs={{0,16},{8,24},{16,0},{24,8},{1,17},{9,25},{17,1},{25,9},{2,18},{10... | collective-permute-start | bytes 294920 | tf_op jit(solution)/shard_map/ppermute | solution.py:346
  7.0 10.0 %collective-permute-start.4 = (bf16[3,4,16,256]{3,2,1,0:T(8,128)(2,1)S(1)}, bf16[3,4,16,256]{3,2,1,0:T(8,128)(2,1)S(1)}, u32[]{:S(2)}, u32[]{:S(2)}) collective-permute-start(bf16[3,4,16,256]{3,2,1,0:T(8,128)(2,1)S(1)} %get-tuple-element.18), channel_id=1, source_target_pairs={{0,24},{8,0},{16,8},{24,16},{1,25},{9,1},{17,9},{25,17},{2,26},{10... | collective-permute-start | bytes 294920 | tf_op jit(solution)/shard_map/ppermute | solution.py:346
  8.1 15.0 %all-to-all-start = ((s16[32,16,256]{2,1,0:T(8,128)(2,1)}), s16[32,16,256]{2,1,0:T(8,128)(2,1)S(1)}, u32[]{:S(2)}, u32[]{:S(2)}) async-start(s16[32,16,256]{2,1,0:T(8,128)(2,1)} %get-tuple-element.14), calls=%async_computation | async-start | bytes 524288 | tf_op jit(solution)/shard_map/all_to_all | solution.py:349
  16.4 3.1 %collective-permute-start.1 = (bf16[3,4,16,256]{3,2,1,0:T(8,128)(2,1)S(1)}, bf16[3,4,16,256]{3,2,1,0:T(8,128)(2,1)S(1)}, u32[]{:S(2)}, u32[]{:S(2)}) collective-permute-start(bf16[3,4,16,256]{3,2,1,0:T(8,128)(2,1)S(1)} %collective-permute-done.h1), channel_id=1, source_target_pairs={{0,1},{1,0},{2,3},{3,2},{4,5},{5,4},{6,7},{7,6},{8,9},{9,8},{10,11... | collective-permute-start | bytes 294920 | tf_op jit(solution)/shard_map/ppermute | solution.py:387
  16.7 2.8 %collective-permute-start.3 = (bf16[3,4,16,256]{3,2,1,0:T(8,128)(2,1)S(1)}, bf16[3,4,16,256]{3,2,1,0:T(8,128)(2,1)S(1)}, u32[]{:S(2)}, u32[]{:S(2)}) collective-permute-start(bf16[3,4,16,256]{3,2,1,0:T(8,128)(2,1)S(1)} %collective-permute-done.2.h2), channel_id=1, source_target_pairs={{0,1},{1,0},{2,3},{3,2},{4,5},{5,4},{6,7},{7,6},{8,9},{9,8},{10,11... | collective-permute-start | bytes 294920 | tf_op jit(solution)/shard_map/ppermute | solution.py:387
  17.0 2.6 %collective-permute-start.5 = (bf16[3,4,16,256]{3,2,1,0:T(8,128)(2,1)S(1)}, bf16[3,4,16,256]{3,2,1,0:T(8,128)(2,1)S(1)}, u32[]{:S(2)}, u32[]{:S(2)}) collective-permute-start(bf16[3,4,16,256]{3,2,1,0:T(8,128)(2,1)S(1)} %collective-permute-done.4.h3), channel_id=1, source_target_pairs={{0,1},{1,0},{2,3},{3,2},{4,5},{5,4},{6,7},{7,6},{8,9},{9,8},{10,11... | collective-permute-start | bytes 294920 | tf_op jit(solution)/shard_map/ppermute | solution.py:387
  23.0 9.4 %copy-start = (f32[1,2,2,8,256]{4,3,2,1,0:T(8,128)S(1)}, f32[1,2,2,8,256]{4,3,2,1,0:T(8,128)}, u32[]{:S(2)}) copy-start(f32[1,2,2,8,256]{4,3,2,1,0:T(8,128)} %p_ref.3) | copy-start | bytes 98308
  23.1 18.3 %copy-start.1 = (f32[1,2,2,8,256]{4,3,2,1,0:T(8,128)S(1)}, f32[1,2,2,8,256]{4,3,2,1,0:T(8,128)}, u32[]{:S(2)}) copy-start(f32[1,2,2,8,256]{4,3,2,1,0:T(8,128)} %r_ref.3) | copy-start | bytes 98308
  23.1 42.6 %copy-start.2 = (f32[1,2,2,8,256]{4,3,2,1,0:T(8,128)S(1)}, f32[1,2,2,8,256]{4,3,2,1,0:T(8,128)}, u32[]{:S(2)}) copy-start(f32[1,2,2,8,256]{4,3,2,1,0:T(8,128)} %x_ref.1) | copy-start | bytes 98308
  28.5 12.8 %all-to-all-start.1 = ((bf16[32,16,256]{2,1,0:T(8,128)(2,1)}), bf16[32,16,256]{2,1,0:T(8,128)(2,1)S(1)}, u32[]{:S(2)}, u32[]{:S(2)}) async-start(bf16[32,16,256]{2,1,0:T(8,128)(2,1)} %normal.1), calls=%async_computation.1 | async-start | bytes 524288 | tf_op jit(solution)/shard_map/all_to_all | solution.py:415
  32.4 7.2 %collective-permute-start.6 = (bf16[1,2,2,8,256]{4,3,2,1,0:T(8,128)(2,1)S(1)}, bf16[1,2,2,8,256]{4,3,2,1,0:T(8,128)(2,1)S(1)}, u32[]{:S(2)}, u32[]{:S(2)}) collective-permute-start(bf16[1,2,2,8,256]{4,3,2,1,0:T(8,128)(2,1)S(1)} %convert_element_type.3), channel_id=1, source_target_pairs={{0,32},{32,64},{64,96},{96,128},{128,160},{160,192},{192,224},{224... | collective-permute-start | bytes 49160 | tf_op jit(solution)/shard_map/ppermute | solution.py:351
  34.3 5.4 %collective-permute-start.7 = (bf16[1,2,2,8,256]{4,3,2,1,0:T(8,128)(2,1)S(1)}, bf16[1,2,2,8,256]{4,3,2,1,0:T(8,128)(2,1)S(1)}, u32[]{:S(2)}, u32[]{:S(2)}) collective-permute-start(bf16[1,2,2,8,256]{4,3,2,1,0:T(8,128)(2,1)S(1)} %convert_element_type.3), channel_id=1, source_target_pairs={{0,224},{32,0},{64,32},{96,64},{128,96},{160,128},{192,160},{224,1... | collective-permute-start | bytes 49160 | tf_op jit(solution)/shard_map/ppermute | solution.py:352

commit v7 on v6

--- a/solution.py
+++ b/solution.py
@@ -160,7 +160,7 @@
 
 
 def normal_kernel(
-    bands_in, count_in, p_ref, g, ft, gx_ref, h1, o1, h2, o2, h3, o3, mine, w_in, turn_in, out,
+    bands_in, count_in, low_any, p_ref, g, ft, gx_ref, h1, o1, h2, o2, h3, o3, mine, w_in, turn_in, out,
     coil, blk, first, ks, acc, near, gx, turn, out_ref, bands_ref, count_ref, sem, out_sem,
 ):
     y = lax.axis_index("segments")
@@ -387,7 +387,7 @@
     others = [lax.ppermute(half, "coils", [(i, i ^ 1) for i in range(8)]) for half in halves]
     parts = pl.pallas_call(
         normal_kernel,
-        in_specs=[HB] * 2 + [VM] * 11 + [HB] * 2,
+        in_specs=[HB] * 2 + [pl.BlockSpec(memory_space=pl.ANY)] + [VM] * 11 + [HB] * 2,
         out_specs=HB,
         out_shape=pltpu.HBM((GROUP, 2 * ROWS, NX), BF16),
         scratch_shapes=[
@@ -409,7 +409,7 @@
         cost_estimate=pl.CostEstimate(flops=2_400_000_000, bytes_accessed=8 << 20, transcendentals=0),
         name="normal",
     )(
-        bands, hbm(seg_count), whole, g, ft, gx,
+        bands, hbm(seg_count), low, whole, g, ft, gx,
         halves[0], others[0], halves[1], others[1], halves[2], others[2], mine, hbm(seg_weights), hbm(turn),
     )
     parts = lax.all_to_all(parts, SPACE, 0, 0, tiled=True)

time: 66.8 us -> 69.2 us (1.036)
  waiting for transfers between devices: 6.5 us -> 8.65 us
  blocking collectives: 24.2 us -> 22.7 us
  starting transfers between devices: 22.6 us -> 23.5 us
  other arithmetic: 0.01 us -> 0.76 us
    all_to_all x1, waiting for transfers between devices: 1.64 us -> 4.3 us  [local(): parts = lax.all_to_all(parts, SPACE, 0, 0, tiled=True)]
    all_to_all x1, starting transfers between devices: 6.08 us -> 7.95 us  [local(): whole = lax.all_to_all(send, SPACE, 0, 0, tiled=True)]
    all_to_all x1, blocking collectives: 24.2 us -> 22.7 us  [local(): lax.all_to_all(sums, ('frames', 'segments', 'coils'), 0, 0, tiled=True)]
    ppermute x1, waiting for transfers between devices: 1.33 us -> 0.01 us  [local(): low = lax.ppermute(halo, 'frames', [(i, (i + 1) % 8) for i in range(8)])]
    ppermute x1, waiting for transfers between devices: 0.01 us -> 0.87 us  [local(): high = lax.ppermute(halo, 'frames', [(i, (i + 7) % 8) for i in range(8)])]
    convert_element_type x1, other arithmetic: 0.01 us -> 0.76 us  [local(): halo = p_in.astype(BF16)]
  transfers between devices with their start and end apart: 10 -> 10, of which waited for: 3 -> 3; matrix products, arithmetic and copies ran while one was open for 0% -> 1% of each run, Pallas kernels for 7% -> 7%
where the time goes in v7:
time: 69.2 us; the launch traced here: 68.8 us
  starting transfers between devices  23.5 us (34%)
  blocking collectives  22.7 us (33%)
  Pallas kernels  12.4 us (18%)
  waiting for transfers between devices  8.65 us (12%)
  other arithmetic  0.76 us (1%)
  between operations  0.73 us (1%)
    all_to_all x1, blocking collectives, local(): lax.all_to_all(sums, ('frames', 'segments', 'coils'), 0, 0, tiled=True)  22.7 us
    all_to_all x1, starting transfers between devices, local(): whole = lax.all_to_all(send, SPACE, 0, 0, tiled=True)  7.95 us
    pallas_call x1, Pallas kernels, local(): pl.pallas_call(normal_kernel, in_specs=[HB] * 2 + [pl.BlockSpec(memory_sp...  5.46 us
    ppermute x3, starting transfers between devices, local(): lax.ppermute(same if k == 2 else other, 'segments', [(i, (i + k) % 4) for...  5.3 us
    all_to_all x1, waiting for transfers between devices, local(): parts = lax.all_to_all(parts, SPACE, 0, 0, tiled=True)  4.3 us
    all_to_all x1, starting transfers between devices, local(): parts = lax.all_to_all(parts, SPACE, 0, 0, tiled=True)  4 us
    ppermute x1, starting transfers between devices, local(): high = lax.ppermute(halo, 'frames', [(i, (i + 7) % 8) for i in range(8)])  3.73 us
    all_to_all x1, waiting for transfers between devices, local(): whole = lax.all_to_all(send, SPACE, 0, 0, tiled=True)  3.47 us
  transfers between devices with their start and end apart: 10, of which 3 were waited for; matrix products, arithmetic and copies ran while one was open for 1% of the time, Pallas kernels for 7%

profile of v7, /device:TPU:1, one launch (start us, length us, event | category | flops | bytes accessed | tf_op | source)
XLA Modules:
  0.0 68.8 jit_solution(2117954843274827082)
XLA Ops:
  0.6 1.5 %prep.1 = (s16[32,16,256]{2,1,0:T(8,128)(2,1)}, bf16[3,4,16,256]{3,2,1,0:T(8,128)(2,1)S(1)}, bf16[3,4,16,256]{3,2,1,0:T(8,128)(2,1)S(1)}) custom-call(f32[1,2,2,8,256]{4,3,2,1,0:T(8,128)} %p_ref.3, bf16[3,8,2,16,256]{4,3,2,1,0:T(8,128)(2,1)} %w_in.3), custom_call_target="tpu_custom_call" | custom-call | tf_op jit(solution)/shard_map/prep/pallas_call | solution.py:330
  2.2 3.8 %collective-permute-start.3 = (bf16[3,4,16,256]{3,2,1,0:T(8,128)(2,1)S(1)}, bf16[3,4,16,256]{3,2,1,0:T(8,128)(2,1)S(1)}, u32[]{:S(2)}, u32[]{:S(2)}) collective-permute-start(bf16[3,4,16,256]{3,2,1,0:T(8,128)(2,1)S(1)} %get-tuple-element.19), channel_id=1, source_target_pairs={{0,16},{8,24},{16,0},{24,8},{1,17},{9,25},{17,1},{25,9},{2,18},{10... | collective-permute-start | bytes 294920 | tf_op jit(solution)/shard_map/ppermute | solution.py:346
  6.0 0.8 %collective-permute-start.5 = (bf16[3,4,16,256]{3,2,1,0:T(8,128)(2,1)S(1)}, bf16[3,4,16,256]{3,2,1,0:T(8,128)(2,1)S(1)}, u32[]{:S(2)}, u32[]{:S(2)}) collective-permute-start(bf16[3,4,16,256]{3,2,1,0:T(8,128)(2,1)S(1)} %get-tuple-element.18), channel_id=1, source_target_pairs={{0,24},{8,0},{16,8},{24,16},{1,25},{9,1},{17,9},{25,17},{2,26},{10... | collective-permute-start | bytes 294920 | tf_op jit(solution)/shard_map/ppermute | solution.py:346
  6.8 0.7 %collective-permute-start.1 = (bf16[3,4,16,256]{3,2,1,0:T(8,128)(2,1)S(1)}, bf16[3,4,16,256]{3,2,1,0:T(8,128)(2,1)S(1)}, u32[]{:S(2)}, u32[]{:S(2)}) collective-permute-start(bf16[3,4,16,256]{3,2,1,0:T(8,128)(2,1)S(1)} %get-tuple-element.18), channel_id=1, source_target_pairs={{0,8},{8,16},{16,24},{24,0},{1,9},{9,17},{17,25},{25,1},{2,10},{10... | collective-permute-start | bytes 294920 | tf_op jit(solution)/shard_map/ppermute | solution.py:346
  7.5 0.8 %convert_element_type.3 = bf16[1,2,2,8,256]{4,3,2,1,0:T(8,128)(2,1)S(1)} convert(f32[1,2,2,8,256]{4,3,2,1,0:T(8,128)} %p_ref.3) | non-fusion elementwise | flops 8192 | bytes 49152 | tf_op jit(solution)/shard_map/convert_element_type | solution.py:350
  8.2 1.6 %collective-permute-start = (bf16[1,2,2,8,256]{4,3,2,1,0:T(8,128)(2,1)S(1)}, bf16[1,2,2,8,256]{4,3,2,1,0:T(8,128)(2,1)S(1)}, u32[]{:S(2)}, u32[]{:S(2)}) collective-permute-start(bf16[1,2,2,8,256]{4,3,2,1,0:T(8,128)(2,1)S(1)} %convert_element_type.3), channel_id=1, source_target_pairs={{0,32},{32,64},{64,96},{96,128},{128,160},{160,192},{192,224},{224... | collective-permute-start | bytes 49160 | tf_op jit(solution)/shard_map/ppermute | solution.py:351
  9.9 7.9 %all-to-all-start = ((s16[32,16,256]{2,1,0:T(8,128)(2,1)}), s16[32,16,256]{2,1,0:T(8,128)(2,1)S(1)}, u32[]{:S(2)}, u32[]{:S(2)}) async-start(s16[32,16,256]{2,1,0:T(8,128)(2,1)} %get-tuple-element.14), calls=%async_computation | async-start | bytes 524288 | tf_op jit(solution)/shard_map/all_to_all | solution.py:349
  17.8 2.2 %tables.1 = (bf16[12,256,256]{2,1,0:T(8,128)(2,1)S(1)}, bf16[2,256,256]{2,1,0:T(8,128)(2,1)S(1)}, bf16[2,256,256]{2,1,0:T(8,128)(2,1)S(1)}, f32[128,256]{1,0:T(8...) custom-call(s32[8,12]{1,0:T(8,128)} %bitcast.7, s32[1,16]{1,0:T(1,128)} %kb_in.1, f32[12]{0:T(128)} %freq_in.1, ...), custom_call_target="tpu_custom_call" | custom-call | flops 1000000000 | bytes 2097152 | tf_op jit(solution)/shard_map/tables/pallas_call | solution.py:354
  20.0 0.3 collective-permute-start.4
  20.4 0.0 collective-permute-done.5.h3
  20.4 0.3 collective-permute-start.6
  20.6 0.0 collective-permute-done.1.h1
  20.6 0.3 collective-permute-start.2
  20.9 2.3 %turns.1.turn_in = f32[12,2,128,256]{3,2,1,0:T(8,128)} custom-call(f32[128,256]{1,0:T(8,128)S(1)} %get-tuple-element.21.elapsed_ref, f32[12,1,256]{2,1,0:T(1,128)S(1)} %get-tuple-element.22.freq_ref, bf16[3,4,16,256]{3,2,1,0:T(8,128)(2,1)S(1)} %collective-permute-done.1.h1, bf16[3,4,16,256]{3,2,1,0:T(8,128)(2,1)S(1)} %collective-permute-done.3.h2, ...), custom_call_target="tpu_custom_call" | custom-call | flops 40000000000 | bytes 3145728 | tf_op jit(solution)/shard_map/turns/pallas_call | solution.py:377
  23.2 0.0 collective-permute-done.low_any.low_ref
  23.3 3.5 %all-to-all-done.p_ref = s16[32,16,256]{2,1,0:T(8,128)(2,1)S(1)} async-done(((s16[32,16,256]{2,1,0:T(8,128)(2,1)}), s16[32,16,256]{2,1,0:T(8,128)(2,1)S(1)}, u32[]{:S(2)}, u32[]{:S(2)}) %all-to-all-start) | async-done | bytes 262176 | tf_op jit(solution)/shard_map/all_to_all | solution.py:349
  26.7 5.5 %normal.1 = bf16[32,16,256]{2,1,0:T(8,128)(2,1)} custom-call(s32[8,12]{1,0:T(8,128)} %bitcast.8, s32[12]{0:T(128)} %count_in.1, bf16[1,2,2,8,256]{4,3,2,1,0:T(8,128)(2,1)S(1)} %collective-permute-done.low_any.low_ref, s16[32,16,256]{2,1,0:T(8,128)(2,1)S(1)} %all-to-all-done.p_ref, bf16[12,256,256]{2,1,0:T(8,128)(2,1)S(1)} %get-tuple-element.15.g, ...), custom_call_target="tpu_custom_call" | custom-call | flops 2400000000 | bytes 8388608 | tf_op jit(solution)/shard_map/normal/pallas_call | solution.py:388
  32.2 4.0 %all-to-all-start.1 = ((bf16[32,16,256]{2,1,0:T(8,128)(2,1)}), bf16[32,16,256]{2,1,0:T(8,128)(2,1)S(1)}, u32[]{:S(2)}, u32[]{:S(2)}) async-start(bf16[32,16,256]{2,1,0:T(8,128)(2,1)} %normal.1), calls=%async_computation.1 | async-start | bytes 524288 | tf_op jit(solution)/shard_map/all_to_all | solution.py:415
  36.2 3.7 %collective-permute-start.7 = (bf16[1,2,2,8,256]{4,3,2,1,0:T(8,128)(2,1)S(1)}, bf16[1,2,2,8,256]{4,3,2,1,0:T(8,128)(2,1)S(1)}, u32[]{:S(2)}, u32[]{:S(2)}) collective-permute-start(bf16[1,2,2,8,256]{4,3,2,1,0:T(8,128)(2,1)S(1)} %convert_element_type.3), channel_id=1, source_target_pairs={{0,224},{32,0},{64,32},{96,64},{128,96},{160,128},{192,160},{224,1... | collective-permute-start | bytes 49160 | tf_op jit(solution)/shard_map/ppermute | solution.py:352
  39.9 0.9 %collective-permute-done.7.high_ref = bf16[1,2,2,8,256]{4,3,2,1,0:T(8,128)(2,1)S(1)} collective-permute-done((bf16[1,2,2,8,256]{4,3,2,1,0:T(8,128)(2,1)S(1)}, bf16[1,2,2,8,256]{4,3,2,1,0:T(8,128)(2,1)S(1)}, u32[]{:S(2)}, u32[]{:S(2)}) %collective-permute-start.7) | collective-permute-done | bytes 16416 | tf_op jit(solution)/shard_map/ppermute | solution.py:352
  40.8 4.3 %all-to-all-done.1.parts_ref = bf16[32,16,256]{2,1,0:T(8,128)(2,1)S(1)} async-done(((bf16[32,16,256]{2,1,0:T(8,128)(2,1)}), bf16[32,16,256]{2,1,0:T(8,128)(2,1)S(1)}, u32[]{:S(2)}, u32[]{:S(2)}) %all-to-all-start.1) | async-done | bytes 262176 | tf_op jit(solution)/shard_map/all_to_all | solution.py:415
  45.1 0.1 applied.1
  45.3 22.7 %all_to_all.21 = f32[256,1,8]{2,1,0:T(1,128)S(1)} all-to-all(f32[256,1,8]{2,1,0:T(1,128)S(1)} %bitcast.6), channel_id=1, replica_groups=mesh['frames'=8,'segments'=4,'coils'=8] {'frames','segments','coils'}, dimensions={0} | all-to-all | bytes 16384 | tf_op jit(solution)/shard_map/all_to_all | solution.py:425
  68.0 0.8 %update.1 = (f32[1,2,2,8,256]{4,3,2,1,0:T(8,128)}, f32[1,2,2,8,256]{4,3,2,1,0:T(8,128)}, f32[1,2,2,8,256]{4,3,2,1,0:T(8,128)}) custom-call(f32[256,8]{1,0:T(8,128)S(1)} %bitcast.5, f32[1,2,2,8,256]{4,3,2,1,0:T(8,128)S(1)} %copy-done.2, f32[1,2,2,8,256]{4,3,2,1,0:T(8,128)S(1)} %copy-done.1, f32[1,2,2,8,256]{4,3,2,1,0:T(8,128)S(1)} %copy-done, ...), custom_call_target="tpu_custom_call" | custom-call | tf_op jit(solution)/shard_map/update/pallas_call | solution.py:427
  (10 shorter events, 0.0 us)
Async XLA Ops:
  2.2 17.9 %collective-permute-start.3 = (bf16[3,4,16,256]{3,2,1,0:T(8,128)(2,1)S(1)}, bf16[3,4,16,256]{3,2,1,0:T(8,128)(2,1)S(1)}, u32[]{:S(2)}, u32[]{:S(2)}) collective-permute-start(bf16[3,4,16,256]{3,2,1,0:T(8,128)(2,1)S(1)} %get-tuple-element.19), channel_id=1, source_target_pairs={{0,16},{8,24},{16,0},{24,8},{1,17},{9,25},{17,1},{25,9},{2,18},{10... | collective-permute-start | bytes 294920 | tf_op jit(solution)/shard_map/ppermute | solution.py:346
  6.0 14.4 %collective-permute-start.5 = (bf16[3,4,16,256]{3,2,1,0:T(8,128)(2,1)S(1)}, bf16[3,4,16,256]{3,2,1,0:T(8,128)(2,1)S(1)}, u32[]{:S(2)}, u32[]{:S(2)}) collective-permute-start(bf16[3,4,16,256]{3,2,1,0:T(8,128)(2,1)S(1)} %get-tuple-element.18), channel_id=1, source_target_pairs={{0,24},{8,0},{16,8},{24,16},{1,25},{9,1},{17,9},{25,17},{2,26},{10... | collective-permute-start | bytes 294920 | tf_op jit(solution)/shard_map/ppermute | solution.py:346
  6.8 13.9 %collective-permute-start.1 = (bf16[3,4,16,256]{3,2,1,0:T(8,128)(2,1)S(1)}, bf16[3,4,16,256]{3,2,1,0:T(8,128)(2,1)S(1)}, u32[]{:S(2)}, u32[]{:S(2)}) collective-permute-start(bf16[3,4,16,256]{3,2,1,0:T(8,128)(2,1)S(1)} %get-tuple-element.18), channel_id=1, source_target_pairs={{0,8},{8,16},{16,24},{24,0},{1,9},{9,17},{17,25},{25,1},{2,10},{10... | collective-permute-start | bytes 294920 | tf_op jit(solution)/shard_map/ppermute | solution.py:346
  8.2 15.0 %collective-permute-start = (bf16[1,2,2,8,256]{4,3,2,1,0:T(8,128)(2,1)S(1)}, bf16[1,2,2,8,256]{4,3,2,1,0:T(8,128)(2,1)S(1)}, u32[]{:S(2)}, u32[]{:S(2)}) collective-permute-start(bf16[1,2,2,8,256]{4,3,2,1,0:T(8,128)(2,1)S(1)} %convert_element_type.3), channel_id=1, source_target_pairs={{0,32},{32,64},{64,96},{96,128},{128,160},{160,192},{192,224},{224... | collective-permute-start | bytes 49160 | tf_op jit(solution)/shard_map/ppermute | solution.py:351
  9.9 16.9 %all-to-all-start = ((s16[32,16,256]{2,1,0:T(8,128)(2,1)}), s16[32,16,256]{2,1,0:T(8,128)(2,1)S(1)}, u32[]{:S(2)}, u32[]{:S(2)}) async-start(s16[32,16,256]{2,1,0:T(8,128)(2,1)} %get-tuple-element.14), calls=%async_computation | async-start | bytes 524288 | tf_op jit(solution)/shard_map/all_to_all | solution.py:349
  20.0 3.2 %collective-permute-start.4 = (bf16[3,4,16,256]{3,2,1,0:T(8,128)(2,1)S(1)}, bf16[3,4,16,256]{3,2,1,0:T(8,128)(2,1)S(1)}, u32[]{:S(2)}, u32[]{:S(2)}) collective-permute-start(bf16[3,4,16,256]{3,2,1,0:T(8,128)(2,1)S(1)} %collective-permute-done.3.h2), channel_id=1, source_target_pairs={{0,1},{1,0},{2,3},{3,2},{4,5},{5,4},{6,7},{7,6},{8,9},{9,8},{10,11... | collective-permute-start | bytes 294920 | tf_op jit(solution)/shard_map/ppermute | solution.py:387
  20.4 2.9 %collective-permute-start.6 = (bf16[3,4,16,256]{3,2,1,0:T(8,128)(2,1)S(1)}, bf16[3,4,16,256]{3,2,1,0:T(8,128)(2,1)S(1)}, u32[]{:S(2)}, u32[]{:S(2)}) collective-permute-start(bf16[3,4,16,256]{3,2,1,0:T(8,128)(2,1)S(1)} %collective-permute-done.5.h3), channel_id=1, source_target_pairs={{0,1},{1,0},{2,3},{3,2},{4,5},{5,4},{6,7},{7,6},{8,9},{9,8},{10,11... | collective-permute-start | bytes 294920 | tf_op jit(solution)/shard_map/ppermute | solution.py:387
  20.6 2.6 %collective-permute-start.2 = (bf16[3,4,16,256]{3,2,1,0:T(8,128)(2,1)S(1)}, bf16[3,4,16,256]{3,2,1,0:T(8,128)(2,1)S(1)}, u32[]{:S(2)}, u32[]{:S(2)}) collective-permute-start(bf16[3,4,16,256]{3,2,1,0:T(8,128)(2,1)S(1)} %collective-permute-done.1.h1), channel_id=1, source_target_pairs={{0,1},{1,0},{2,3},{3,2},{4,5},{5,4},{6,7},{7,6},{8,9},{9,8},{10,11... | collective-permute-start | bytes 294920 | tf_op jit(solution)/shard_map/ppermute | solution.py:387
  26.7 18.4 %copy-start = (f32[1,2,2,8,256]{4,3,2,1,0:T(8,128)S(1)}, f32[1,2,2,8,256]{4,3,2,1,0:T(8,128)}, u32[]{:S(2)}) copy-start(f32[1,2,2,8,256]{4,3,2,1,0:T(8,128)} %p_ref.3) | copy-start | bytes 98308
  26.7 18.4 %copy-start.1 = (f32[1,2,2,8,256]{4,3,2,1,0:T(8,128)S(1)}, f32[1,2,2,8,256]{4,3,2,1,0:T(8,128)}, u32[]{:S(2)}) copy-start(f32[1,2,2,8,256]{4,3,2,1,0:T(8,128)} %r_ref.3) | copy-start | bytes 98308
  26.7 41.3 %copy-start.2 = (f32[1,2,2,8,256]{4,3,2,1,0:T(8,128)S(1)}, f32[1,2,2,8,256]{4,3,2,1,0:T(8,128)}, u32[]{:S(2)}) copy-start(f32[1,2,2,8,256]{4,3,2,1,0:T(8,128)} %x_ref.1) | copy-start | bytes 98308
  32.2 12.9 %all-to-all-start.1 = ((bf16[32,16,256]{2,1,0:T(8,128)(2,1)}), bf16[32,16,256]{2,1,0:T(8,128)(2,1)S(1)}, u32[]{:S(2)}, u32[]{:S(2)}) async-start(bf16[32,16,256]{2,1,0:T(8,128)(2,1)} %normal.1), calls=%async_computation.1 | async-start | bytes 524288 | tf_op jit(solution)/shard_map/all_to_all | solution.py:415
  36.2 4.6 %collective-permute-start.7 = (bf16[1,2,2,8,256]{4,3,2,1,0:T(8,128)(2,1)S(1)}, bf16[1,2,2,8,256]{4,3,2,1,0:T(8,128)(2,1)S(1)}, u32[]{:S(2)}, u32[]{:S(2)}) collective-permute-start(bf16[1,2,2,8,256]{4,3,2,1,0:T(8,128)(2,1)S(1)} %convert_element_type.3), channel_id=1, source_target_pairs={{0,224},{32,0},{64,32},{96,64},{128,96},{160,128},{192,160},{224,1... | collective-permute-start | bytes 49160 | tf_op jit(solution)/shard_map/ppermute | solution.py:352
